TPU v7x, 32 devices: a whole 2x2x4 slice. The times are simulated.
32 devices in a mesh: gx: 8 (over z, y), gy: 4 (over x, core).
Axes of the slice: x: 2, y: 2, z: 4, core: 2. Of those that a mesh axis runs over, the one named last changes fastest.
Arguments:
- layer_input: bfloat16 [8192, 768], P('gx'), may hold values from -6 to 6
- w_query: bfloat16 [768, 768], P('gx', 'gy'), may hold values from -0.21875 to 0.21875
- w_key: bfloat16 [768, 768], P('gx', 'gy'), may hold values from -0.21875 to 0.21875
- w_value: bfloat16 [768, 768], P('gx', 'gy'), may hold values from -0.21875 to 0.21875
- w_output: bfloat16 [768, 768], P('gx', 'gy'), may hold values from -1.25 to 1.25
- attn_gain: bfloat16 [768], P('gx'), may hold values from 0.5 to 1.5
- moe_gain: bfloat16 [768], P('gx'), may hold values from 0.5 to 1.5
- router: bfloat16 [768, 4], P('gx'), may hold values from -0.15625 to 0.15625
- rel_table: float32 [12, 32], P('gy'), may hold values from -4 to 4
- w_in: bfloat16 [8, 768, 1536], P('gx', None, 'gy'), may hold values from -0.21875 to 0.21875
- w_out: bfloat16 [8, 1536, 768], P('gx', 'gy'), may hold values from -0.4375 to 0.4375
- expert_ids: int32 [8192, 1], P('gx'), may hold values from 0 to 3
- buckets: int32 [1024], replicated, may hold values from 0 to 31
- block_mask: int32 [4, 4], replicated, may hold values from 0 to 1, as said below
- grad_out: bfloat16 [8192, 768], P('gx'), may hold values from -6 to 6
Outputs:
- layer_output: float32 [8192, 768], P('gx')
- grad_input: float32 [8192, 768], P('gx')
- grad_query: float32 [768, 768], P('gx', 'gy')
- grad_key: float32 [768, 768], P('gx', 'gy')
- grad_value: float32 [768, 768], P('gx', 'gy')
- grad_out_proj: float32 [768, 768], P('gx', 'gy')
- grad_attn_gain: float32 [768], P('gx')
- grad_moe_gain: float32 [768], P('gx')
- grad_router: float32 [768, 4], P('gx')
- grad_table: float32 [12, 32], P('gy')
- grad_w_in: float32 [8, 768, 1536], P('gx', None, 'gy')
- grad_w_out: float32 [8, 1536, 768], P('gx', 'gy')
Inputs may be any that keep to these rules, and one draw needn't show every extreme that they name: block_mask is 1 on its diagonal and 0 above it. `expert_ids`: every expert is named by some token.
All inputs are finite; a program needn't handle non-finite values.
Results may differ from a plain program's by a relative error of at most 0.02.
Values may be sent and summed in bfloat16 or wider, within the bound.
No kernel may reach another device: no remote copies, remote signals or barrier semaphores. Data moves between devices by JAX's collectives and lax.ppermute only.
A program may use at most 256 MiB of HBM per device.

v0:
```python
from functools import partial

import jax
import jax.numpy as jnp
from jax import lax
from jax.experimental import pallas as pl
from jax.experimental.pallas import tpu as pltpu
from jax.sharding import PartitionSpec as P

BLOCK = 256
EPS = 1e-06
LANES = 128
BF = jnp.bfloat16
F32 = jnp.float32
HIGH = lax.Precision.HIGHEST
VMEM_BYTES = 56 * 1024 * 1024
PEAK = 1.15e9
RING = (0, 2, 4, 6, 7, 5, 3, 1)
RING_STEPS = (0, -1, 1, -2, 2, -3, 3, -4)


def mm(left, right, precision=None):
    return lax.dot_general(
        left, right, (((1,), (0,)), ((), ())), precision=precision, preferred_element_type=F32
    )


def mm_nt(left, right, precision=None):
    return lax.dot_general(
        left, right, (((1,), (1,)), ((), ())), precision=precision, preferred_element_type=F32
    )


def mm_tn(left, right, precision=None):
    return lax.dot_general(
        left, right, (((0,), (0,)), ((), ())), precision=precision, preferred_element_type=F32
    )


VM = pl.BlockSpec(memory_space=pltpu.VMEM)
SM = pl.BlockSpec(memory_space=pltpu.SMEM)
ANY = pl.BlockSpec(memory_space=pl.ANY)


def call(kernel, name, outs, in_specs, args, scratch=(), cost=1):
    return pl.pallas_call(
        kernel,
        name=name,
        out_shape=list(outs),
        in_specs=in_specs,
        out_specs=[VM] * len(outs),
        scratch_shapes=list(scratch),
        compiler_params=pltpu.CompilerParams(vmem_limit_bytes=VMEM_BYTES),
        cost_estimate=pl.CostEstimate(
            flops=int(cost * PEAK), bytes_accessed=1, transcendentals=0
        ),
    )(*args)


def struct(shape, dtype):
    return jax.ShapeDtypeStruct(shape, dtype)


def one_hot_rows(pos_row, start, count):
    slots = lax.broadcasted_iota(jnp.int32, (count, pos_row.shape[1]), 0) + start
    return jnp.where(slots == pos_row, 1.0, 0.0).astype(BF)


def one_hot_cols(pos_col, start, count):
    slots = lax.broadcasted_iota(jnp.int32, (pos_col.shape[0], count), 1) + start
    return jnp.where(slots == pos_col, 1.0, 0.0).astype(BF)


def pack_kernel(q_ref, k_ref, v_ref, o_ref, attn_ref, moe_ref, router_ref, qkv_ref, extras_ref):
    qkv_ref[...] = jnp.concatenate([q_ref[...], k_ref[...], v_ref[...]], axis=1)
    rows, experts = router_ref.shape
    blank = jnp.zeros((1, LANES - rows), F32)
    row = lax.broadcasted_iota(jnp.int32, (LANES, LANES), 0)
    first = jnp.concatenate([attn_ref[...].astype(F32), blank], axis=1)
    second = jnp.concatenate([moe_ref[...].astype(F32), blank], axis=1)
    gains = jnp.where(row == 0, first, jnp.where(row == 1, second, 0.0))
    gains = jnp.transpose(gains)[:rows]
    route = jnp.concatenate(
        [
            jnp.zeros((rows, 2), F32),
            router_ref[...].astype(F32),
            jnp.zeros((rows, LANES - 2 - experts), F32),
        ],
        axis=1,
    )
    extras_ref[...] = jnp.concatenate([(gains + route).astype(BF), o_ref[...]], axis=1)


def lane_prefix(values):
    row = lax.broadcasted_iota(jnp.int32, (LANES, LANES), 0)
    column = lax.broadcasted_iota(jnp.int32, (LANES, LANES), 1)
    sooner = jnp.where(row < column, 1.0, 0.0).astype(BF)
    carry = jnp.zeros((values.shape[0], 1), F32)
    out = []
    for start in range(0, values.shape[1], LANES):
        part = values[:, start : start + LANES]
        out.append(mm(part.astype(BF), sooner) + carry)
        carry = carry + jnp.sum(part, axis=1, keepdims=True)
    return jnp.concatenate(out, axis=1), carry


def place_kernel(experts, capacity, group, gx_ref, ids_ref, row_ref, col_ref, info_ref):
    seq = ids_ref.shape[1]
    ids = ids_ref[...]
    deep = -(-experts // 8) * 8
    label = lax.broadcasted_iota(jnp.int32, (deep, seq), 0)
    hot = jnp.where(label == ids, 1.0, 0.0)
    before, total = lane_prefix(hot)
    rank = jnp.sum(before * hot, axis=0, keepdims=True)
    kept = rank < capacity
    filled = jnp.minimum(total, 1.0 * capacity)
    empty = jnp.where(label[:, 0:1] < experts, capacity - filled, 0.0)
    row = lax.broadcasted_iota(jnp.int32, (deep, deep), 0)
    column = lax.broadcasted_iota(jnp.int32, (deep, deep), 1)
    sooner = jnp.where(column < row, 1.0, 0.0)
    begins = mm(sooner, jnp.broadcast_to(empty, (deep, LANES)), HIGH)[:, 0:1]
    lost = jnp.broadcast_to(jnp.where(kept, 0.0, 1.0), (8, seq))
    order = lane_prefix(lost)[0][0:1]
    inside = (order >= begins) & (order < begins + empty)
    spare_expert = jnp.sum(jnp.where(inside, label.astype(F32), 0.0), axis=0, keepdims=True)
    spare_rank = jnp.sum(jnp.where(inside, order - begins + filled, 0.0), axis=0, keepdims=True)
    expert = jnp.where(kept, ids.astype(F32), spare_expert).astype(jnp.int32)
    rank = jnp.where(kept, rank, spare_rank)
    block = jnp.floor((rank + 0.5) * (1.0 / group))
    near = jnp.bitwise_xor(expert, gx_ref[0] // 2).astype(F32)
    position = block * (experts * group) + near * group + rank - block * group
    row_ref[...] = position.astype(jnp.int32)
    tall = jnp.transpose(jnp.broadcast_to(position, (LANES, seq)))
    col_ref[...] = tall[:, 0:1].astype(jnp.int32)
    line = lax.broadcasted_iota(jnp.int32, (LANES, seq), 0)
    info = jnp.where(line == 0, jnp.where(kept, 1.0, 0.0), jnp.where(line - 2 == ids, 1.0, 0.0))
    info_ref[...] = info.astype(BF)


def presort_kernel(gy_ref, pos_ref, x_ref, g_ref, info_ref, xs_ref, gs_ref, infos_ref):
    own = xs_ref.shape[0]
    pick = one_hot_rows(pos_ref[...], gy_ref[0] * own, own)
    xs_ref[...] = mm(pick, x_ref[...]).astype(BF)
    gs_ref[...] = mm(pick, g_ref[...]).astype(BF)
    infos_ref[...] = mm_nt(pick, info_ref[...])


def ring_source(gx, step):
    spot = jnp.where(gx % 2 == 0, gx // 2, 7 - gx // 2)
    spot = jnp.bitwise_and(spot + step, 7)
    return jnp.where(spot < 4, 2 * spot, 2 * (7 - spot) + 1)


def assemble(pieces, gx_ref, target, sems):
    copies = []
    rows = pieces[0].shape[0]
    for n, piece in enumerate(pieces):
        place = target
        if len(pieces) > 1:
            at = pl.multiple_of(ring_source(gx_ref[0], RING_STEPS[n]) * rows, 32)
            place = target.at[pl.ds(at, rows), :]
        copy = pltpu.make_async_copy(piece, place, sems.at[n])
        copy.start()
        copies.append(copy)
    return copies


def unpack_kernel(count, *refs):
    gx_ref, pieces = refs[0], refs[1 : 1 + count]
    extras_ref, out_ref, buf, sems = refs[1 + count :]
    for copy in assemble(pieces, gx_ref, buf, sems):
        copy.wait()
    extras_ref[...] = buf[:, :LANES]
    out_ref[...] = buf[:, LANES:]


def attend_kernel(count, *refs):
    gy_ref, gx_ref, mask_ref, x_ref, extras_ref, table_ref, brev_ref, pos_ref = refs[:8]
    pieces = refs[8 : 8 + count]
    h1_ref, qkv_ref, prob_ref, mixed_ref, s0_ref, s1_ref, s2_ref, s3_ref = refs[
        8 + count : 16 + count
    ]
    w_ref, toep_ref, sems = refs[16 + count :]
    copies = assemble(pieces, gx_ref, w_ref, sems)
    seq = x_ref.shape[0]
    width = mixed_ref.shape[1]
    blocks = seq // BLOCK
    head = 64
    heads = width // head
    gain = jnp.transpose(extras_ref[...].astype(F32))[0:1]
    for copy in copies:
        copy.wait()
    for i in range(blocks):
        rows = pl.ds(i * BLOCK, BLOCK)
        x = x_ref[rows, :].astype(F32)
        scale = lax.rsqrt(jnp.mean(x * x, axis=-1, keepdims=True) + EPS)
        h1 = (x * scale * gain).astype(BF)
        h1_ref[rows, :] = h1
        out = mm(h1, w_ref[...])
        qkv_ref[rows, :] = jnp.concatenate(
            [out[:, :width].astype(BF) * jnp.asarray(0.125, BF), out[:, width:].astype(BF)], axis=1
        )
    bucket_count = table_ref.shape[1]
    biases = []
    for k in range(blocks):
        labels = lax.broadcasted_iota(jnp.int32, (bucket_count, 2 * BLOCK), 0)
        hot = jnp.where(labels == brev_ref[k : k + 1, :], 1.0, 0.0)
        biases.append(mm(table_ref[...], hot, HIGH))
    for h in range(heads):
        for k in range(blocks):
            line = jnp.broadcast_to(biases[k][h : h + 1, :], (BLOCK, 2 * BLOCK))
            skew = pltpu.roll(line, BLOCK + 1, 1, stride=1, stride_axis=0)[:, :BLOCK]
            if k == 0:
                r = lax.broadcasted_iota(jnp.int32, (BLOCK, BLOCK), 0)
                c = lax.broadcasted_iota(jnp.int32, (BLOCK, BLOCK), 1)
                skew = jnp.where(r >= c, skew, -1e30)
            toep_ref[k] = skew
        at = h * head
        for i in range(blocks):
            q = qkv_ref[pl.ds(i * BLOCK, BLOCK), :][:, at : at + head]
            scores = []
            peak = None
            for j in range(i + 1):
                key = qkv_ref[pl.ds(j * BLOCK, BLOCK), :][:, width + at : width + at + head]
                s = mm_nt(q, key) + toep_ref[i - j]
                if j < i:
                    s = s + jnp.where(mask_ref[i, j] == 1, 0.0, -1e30)
                scores.append(s)
                peak = s if peak is None else jnp.maximum(peak, s)
            peak = jnp.max(peak, axis=-1, keepdims=True)
            total = None
            terms = []
            for s in scores:
                e = jnp.exp(s - peak)
                terms.append(e)
                total = e if total is None else total + e
            inverse = 1.0 / jnp.sum(total, axis=-1, keepdims=True)
            acc = None
            for j in range(i + 1):
                prob = (terms[j] * inverse).astype(BF)
                prob_ref[h * (blocks * (blocks + 1) // 2) + i * (i + 1) // 2 + j] = prob
                value = qkv_ref[pl.ds(j * BLOCK, BLOCK), :][
                    :, 2 * width + at : 2 * width + at + head
                ]
                part = mm(prob, value)
                acc = part if acc is None else acc + part
            mixed_ref[pl.ds(i * BLOCK, BLOCK), at : at + head] = acc.astype(BF)
    own = s0_ref.shape[0]
    mixed = mixed_ref[...]
    for j, ref in enumerate((s0_ref, s1_ref, s2_ref, s3_ref)):
        start = jnp.bitwise_xor(gy_ref[0], j) * own
        ref[...] = mm(one_hot_rows(pos_ref[...], start, own), mixed).astype(BF)


def route_kernel(experts, pieces, *refs):
    mixed_refs, out_refs = refs[:4], refs[4:8]
    xs_ref, gs_ref, infos_ref, extras_ref = refs[8:12]
    h2_refs, sg_refs = refs[12 : 12 + pieces], refs[12 + pieces : 12 + 2 * pieces]
    res_ref, prob_ref, gate_ref = refs[12 + 2 * pieces :]
    attn = None
    for j in range(4):
        part = mm_nt(mixed_refs[j][...], out_refs[j][...])
        attn = part if attn is None else attn + part
    extras = extras_ref[...]
    gain = jnp.transpose(extras.astype(F32))[1:2]
    residual = xs_ref[...].astype(F32) + attn
    res_ref[...] = residual
    scale = lax.rsqrt(jnp.mean(residual * residual, axis=-1, keepdims=True) + EPS)
    h2 = (residual * scale * gain).astype(BF)
    logits = mm(h2, extras)
    lane = lax.broadcasted_iota(jnp.int32, logits.shape, 1)
    real = (lane >= 2) & (lane < 2 + experts)
    logits = jnp.where(real, logits, -1e30)
    e = jnp.exp(logits - jnp.max(logits, axis=-1, keepdims=True))
    prob = e / jnp.sum(e, axis=-1, keepdims=True)
    prob_ref[...] = prob
    info = infos_ref[...]
    keep = info[:, 0:1]
    gate = jnp.sum(jnp.where(real, prob * info, 0.0), axis=-1, keepdims=True)
    gate_ref[...] = jnp.broadcast_to(gate, gate_ref.shape)
    h2 = jnp.where(keep > 0.0, h2.astype(F32), 0.0).astype(BF)
    sg = jnp.where(keep > 0.0, gate * gs_ref[...].astype(F32), 0.0).astype(BF)
    split(h2, h2_refs)
    split(sg, sg_refs)


def split(value, refs):
    rows = refs[0].shape[0]
    for n, ref in enumerate(refs):
        ref[...] = value[n * rows : (n + 1) * rows, :]


def joined(refs):
    if len(refs) == 1:
        return refs[0][...]
    return jnp.concatenate([ref[...] for ref in refs], axis=0)


def fetch(packs, buf, sems, first):
    copies = []
    at = 0
    for n, pack in enumerate(packs):
        rows = pack.shape[0]
        copy = pltpu.make_async_copy(pack, buf.at[pl.ds(at, rows), :], sems.at[first + n])
        copy.start()
        copies.append(copy)
        at += rows
    return copies


def out_half(buf, j, n, hidden):
    model = buf.shape[1] // 2
    return buf[j, model + n * hidden : model + (n + 1) * hidden, :]


def expert_kernel(pieces, groups, last, *refs):
    row_refs = refs[:pieces]
    refs = refs[pieces:]
    if last:
        before_ref, refs = refs[0], refs[1:]
    total = sum(groups)
    packs, refs = refs[:total], refs[total:]
    outs = refs[: pieces if last else 1]
    act_ref, slope_ref, buf, sems = refs[len(outs) :]
    hidden = act_ref.shape[2]
    copies = []
    first = 0
    for j, size in enumerate(groups):
        copies.append(fetch(packs[first : first + size], buf.at[j], sems, first))
        first += size
    rows = joined(row_refs)
    left = before_ref[:, : rows.shape[1] // 2] if last else None
    right = before_ref[:, rows.shape[1] // 2 :] if last else None
    for j in range(len(groups)):
        for copy in copies[j]:
            copy.wait()
        pre = mm(rows, buf[j, : rows.shape[1], :])
        cdf = 0.5 * (1.0 + lax.erf(pre * 0.7071067811865476))
        slope = cdf + pre * (0.3989422804014327 * jnp.exp(-0.5 * pre * pre))
        act = (pre * cdf).astype(BF)
        act_ref[j] = act
        slope_ref[j] = slope.astype(BF)
        a = mm(act, out_half(buf, j, 0, hidden))
        b = mm(act, out_half(buf, j, 1, hidden))
        left = a if left is None else left + a
        right = b if right is None else right + b
    whole = jnp.concatenate([left, right], axis=1)
    if last:
        split(whole.astype(BF), outs)
    else:
        outs[0][...] = whole


def expert_back_kernel(pieces, groups, *refs):
    sg_refs = refs[:pieces]
    slopes = refs[pieces : pieces + 2]
    total = sum(groups)
    refs = refs[pieces + 2 :]
    packs, gr_refs = refs[:total], refs[total : total + pieces]
    gp_ref, buf, sems = refs[total + pieces :]
    hidden = gp_ref.shape[2]
    copies = []
    first = 0
    for j, size in enumerate(groups):
        copies.append(fetch(packs[first : first + size], buf.at[j], sems, first))
        first += size
    sg = joined(sg_refs)
    model = sg.shape[1]
    acc = None
    for j in range(len(groups)):
        for copy in copies[j]:
            copy.wait()
        grad = mm_nt(sg[:, : model // 2], out_half(buf, j, 0, hidden))
        grad = grad + mm_nt(sg[:, model // 2 :], out_half(buf, j, 1, hidden))
        grad = (grad * slopes[j // 4][j % 4].astype(F32)).astype(BF)
        gp_ref[j] = grad
        part = mm_nt(grad, buf[j, :model, :])
        acc = part if acc is None else acc + part
    split(acc.astype(BF), gr_refs)


def outer_sent_kernel(pieces, picks, flip, *refs):
    wide = joined(refs[:pieces])
    sources, out_ref = refs[pieces:-1], refs[-1]
    for n, (a, b) in enumerate(picks):
        thin = sources[a][b]
        out_ref[n] = (mm_tn(thin, wide) if flip else mm_tn(wide, thin)).astype(BF)


def outer_held_kernel(pieces, picks, flip, *refs):
    wide = joined(refs[:pieces])
    sources, arrived_ref = refs[pieces:-5], refs[-5]
    out_refs = refs[-4:]
    for n, (a, b) in enumerate(picks):
        thin = sources[a][b]
        value = mm_tn(thin, wide) if flip else mm_tn(wide, thin)
        value = value + arrived_ref[n].astype(F32)
        out_refs[n][...] = value.astype(out_refs[n].dtype)


def joined_kernel(counts, kernels, *refs):
    sources = refs[: sum(c[0] for c in counts)]
    results = refs[len(sources) :]
    for (taken, given), kernel in zip(counts, kernels):
        kernel(*sources[:taken], *results[:given])
        sources, results = sources[taken:], results[given:]


def deliver_kernel(experts, pieces, *refs):
    er_refs = refs[:pieces]
    res_ref, xs_ref, gs_ref, infos_ref, prob_ref, gate_ref, extras_ref = refs[
        pieces : pieces + 7
    ]
    h2_refs = refs[pieces + 7 : 2 * pieces + 7]
    d1_ref, gh_ref, router_ref = refs[2 * pieces + 7 :]
    prob = prob_ref[...]
    gate = gate_ref[...][:, 0:1]
    lane = lax.broadcasted_iota(jnp.int32, prob.shape, 1)
    real = (lane >= 2) & (lane < 2 + experts)
    hot = jnp.where(real, infos_ref[...], 0.0)
    result = joined(er_refs).astype(F32)
    d1_ref[...] = (res_ref[...] - xs_ref[...].astype(F32) + gate * result).astype(BF)
    grad_gate = jnp.sum(gs_ref[...].astype(F32) * result, axis=-1, keepdims=True)
    grad_logits = (prob * (hot - gate) * grad_gate).astype(BF)
    gh_ref[...] = mm_nt(grad_logits, extras_ref[...])
    router_ref[...] = mm_tn(grad_logits, joined(h2_refs))[: router_ref.shape[0]]


def combine_kernel(pieces, *refs):
    gr_refs = refs[:pieces]
    gh_ref, res_ref, gs_ref, router_ref, extras_ref = refs[pieces : pieces + 5]
    out_refs, mixed_refs = refs[pieces + 5 : pieces + 9], refs[pieces + 9 : pieces + 13]
    gm_refs = refs[pieces + 13 : pieces + 17]
    d2_ref, small_ref, keep_ref, send_ref = refs[pieces + 17 :]
    gain = jnp.transpose(extras_ref[...].astype(F32))[1:2]
    residual = res_ref[...]
    g = gs_ref[...].astype(F32)
    grad_h2 = gh_ref[...] + joined(gr_refs).astype(F32)
    scale = lax.rsqrt(jnp.mean(residual * residual, axis=-1, keepdims=True) + EPS)
    unit = residual * scale
    scaled = grad_h2 * gain
    centre = jnp.mean(scaled * unit, axis=-1, keepdims=True)
    d2 = (scale * (scaled - unit * centre)).astype(BF)
    d2_ref[...] = d2
    grad_attn = (g + d2.astype(F32)).astype(BF)
    for j in range(4):
        gm_refs[j][...] = mm(grad_attn, out_refs[j][...]).astype(BF)
    for target, j in ((keep_ref, 0), (send_ref, 1)):
        mixed = jnp.concatenate([mixed_refs[j][...], mixed_refs[j + 2][...]], axis=1)
        target[...] = mm_tn(grad_attn, mixed).astype(BF)
    grad_gain = jnp.sum(grad_h2 * unit, axis=0, keepdims=True)
    small = router_ref[...]
    row = lax.broadcasted_iota(jnp.int32, small.shape, 0)
    small_ref[...] = jnp.where(row == 1, grad_gain, small)


def unskew_sum(block):
    zeros = jnp.zeros((8, BLOCK), F32)
    acc = None
    for i in range(BLOCK // 8):
        piece = jnp.concatenate([block[8 * i : 8 * i + 8, :], zeros], axis=1)
        shift = BLOCK - 8 - 8 * i
        if shift:
            piece = pltpu.roll(piece, shift, 1)
        acc = piece if acc is None else acc + piece
    left = 7 - lax.broadcasted_iota(jnp.int32, acc.shape, 0)
    for bit in range(3):
        moved = pltpu.roll(acc, 1 << bit, 1)
        acc = jnp.where((left >> bit) & 1 == 1, moved, acc)
    return jnp.sum(acc, axis=0, keepdims=True)


def attend_back_kernel(count, *refs):
    gy_ref, gx_ref, g0_ref, g1_ref, g2_ref, g3_ref = refs[:6]
    pos_ref, prob_ref, qkv_ref, h1_ref, x_ref, w_ref, extras_ref, brev_ref = refs[6:14]
    d2_ref, small_ref = refs[14:16]
    dw_refs = refs[16 : 16 + count]
    keep_ref, send_ref, table_ref, gm_ref, grads_ref, dw_buf = refs[16 + count :]
    seq, width = gm_ref.shape
    blocks = seq // BLOCK
    head = 64
    heads = width // head
    own = g0_ref.shape[0]
    gy = gy_ref[0]
    for i in range(blocks):
        rows = pl.ds(i * BLOCK, BLOCK)
        pos = pos_ref[rows, :]
        acc = None
        for j, ref in enumerate((g0_ref, g1_ref, g2_ref, g3_ref)):
            part = mm(one_hot_cols(pos, jnp.bitwise_xor(gy, j) * own, own), ref[...])
            acc = part if acc is None else acc + part
        gm_ref[rows, :] = acc.astype(BF)
    sums = [[None] * heads for _ in range(blocks)]
    for h in range(heads):
        at = h * head
        diagonals = [None] * blocks
        grad_keys = [None] * blocks
        grad_values = [None] * blocks
        for i in range(blocks):
            rows = pl.ds(i * BLOCK, BLOCK)
            q = qkv_ref[rows, :][:, at : at + head]
            gm = gm_ref[rows, :][:, at : at + head]
            centre = None
            kept = []
            for j in range(i + 1):
                value = qkv_ref[pl.ds(j * BLOCK, BLOCK), :][
                    :, 2 * width + at : 2 * width + at + head
                ]
                low = prob_ref[h * (blocks * (blocks + 1) // 2) + i * (i + 1) // 2 + j]
                prob = low.astype(F32)
                grad_prob = mm_nt(gm, value)
                both = prob * grad_prob
                centre = both if centre is None else centre + both
                kept.append((prob, grad_prob))
                part = mm_tn(low, gm)
                grad_values[j] = part if grad_values[j] is None else grad_values[j] + part
            centre = jnp.sum(centre, axis=-1, keepdims=True)
            acc = None
            for j in range(i + 1):
                prob, grad_prob = kept[j]
                score = prob * (grad_prob - centre)
                diagonals[i - j] = score if diagonals[i - j] is None else diagonals[i - j] + score
                score = score.astype(BF)
                key = qkv_ref[pl.ds(j * BLOCK, BLOCK), :][:, width + at : width + at + head]
                part = mm(score, key)
                acc = part if acc is None else acc + part
                part = mm_tn(score, q)
                grad_keys[j] = part if grad_keys[j] is None else grad_keys[j] + part
            grads_ref[rows, at : at + head] = (acc * 0.125).astype(BF)
        for j in range(blocks):
            rows = pl.ds(j * BLOCK, BLOCK)
            grads_ref[rows, width + at : width + at + head] = grad_keys[j].astype(BF)
            grads_ref[rows, 2 * width + at : 2 * width + at + head] = grad_values[j].astype(BF)
        for k in range(blocks):
            sums[k][h] = unskew_sum(diagonals[k])
    bucket_count = table_ref.shape[0]
    columns = None
    for k in range(blocks):
        labels = lax.broadcasted_iota(jnp.int32, (bucket_count, 2 * BLOCK), 0)
        hot = jnp.where(labels == brev_ref[k : k + 1, :], 1.0, 0.0)
        lines = jnp.concatenate(sums[k] + [jnp.zeros((8 - heads, 2 * BLOCK), F32)], axis=0)
        part = mm_nt(hot, lines, HIGH)
        columns = part if columns is None else columns + part
    table_ref[...] = columns
    gain_total = None
    weights = w_ref[...]
    gain = jnp.transpose(extras_ref[...].astype(F32))[0:1]
    for j in range(4):
        rows = pl.ds(pl.multiple_of(jnp.bitwise_xor(gy, j) * BLOCK, BLOCK), BLOCK)
        part = mm_nt(grads_ref[rows, :], weights)
        x = x_ref[rows, :].astype(F32)
        scale = lax.rsqrt(jnp.mean(x * x, axis=-1, keepdims=True) + EPS)
        unit = x * scale
        line = jnp.sum(part * unit, axis=0, keepdims=True)
        gain_total = line if gain_total is None else gain_total + line
        scaled = part * gain
        centre = jnp.mean(scaled * unit, axis=-1, keepdims=True)
        part = scale * (scaled - unit * centre)
        part = part + mm(one_hot_cols(pos_ref[rows, :], gy * own, own), d2_ref[...])
        target = send_ref if j % 2 else keep_ref
        target[j // 2] = part.astype(BF)
    small = small_ref[...]
    row = lax.broadcasted_iota(jnp.int32, small.shape, 0)
    small = jnp.where(row == 0, gain_total, small)
    spare = dw_buf.shape[1] - 3 * width
    small = jnp.concatenate(
        [small, jnp.zeros((LANES - small.shape[0], small.shape[1]), F32)], axis=0
    )
    small = jnp.transpose(small)[:, :spare]
    grads = mm_tn(h1_ref[...], grads_ref[...])
    dw_buf[...] = jnp.concatenate([grads, small], axis=1).astype(BF)
    if len(dw_refs) == 1:
        dw_refs[0][...] = dw_buf[...]
        return
    rows = dw_refs[0].shape[1]
    column = jnp.concatenate([columns[:, h : h + 1] for h in range(heads)], axis=0)
    column = jnp.broadcast_to(column, (rows, spare)).astype(BF)
    last = lax.broadcasted_iota(jnp.int32, (rows, spare), 1) == spare - 1
    for n in range(8):
        at = pl.multiple_of(jnp.bitwise_xor(gx_ref[0], n) * rows, 32)
        piece = dw_buf[pl.ds(at, rows), :]
        tail = jnp.where(last, column, piece[:, 3 * width :])
        dw_refs[n % 2][n // 2] = jnp.concatenate([piece[:, : 3 * width], tail], axis=1)


def unsort_kernel(gy_ref, pos_ref, x_ref, d0_ref, d1_ref, d2_ref, d3_ref, out_ref):
    own = d0_ref.shape[0]
    gy = gy_ref[0]
    for i in range(x_ref.shape[0] // BLOCK):
        rows = pl.ds(i * BLOCK, BLOCK)
        pos = pos_ref[rows, :]
        acc = x_ref[rows, :].astype(F32)
        for j, ref in enumerate((d0_ref, d1_ref, d2_ref, d3_ref)):
            acc = acc + mm(one_hot_cols(pos, jnp.bitwise_xor(gy, j) * own, own), ref[...])
        out_ref[rows, :] = acc


def finish_kernel(gy_ref, own_ref, other_ref, g_ref, out_ref):
    gy = gy_ref[0]
    for j in range(4):
        rows = pl.ds(pl.multiple_of(jnp.bitwise_xor(gy, j) * BLOCK, BLOCK), BLOCK)
        source = other_ref if j % 2 else own_ref
        out_ref[rows, :] = g_ref[rows, :].astype(F32) + source[j // 2].astype(F32)


def swap(x, axis, bit):
    size = lax.axis_size(axis)
    return lax.ppermute(x, axis, [(i, i ^ bit) for i in range(size)])


def gather_rows(chains, *fills):
    size = lax.axis_size("gx")
    if size != len(RING):
        return [
            lax.all_to_all(
                jnp.broadcast_to(x[None], (size,) + x.shape).reshape(-1, x.shape[1]),
                "gx",
                split_axis=0,
                concat_axis=0,
                tiled=True,
            )
            for x in chains
        ]
    ahead = [(RING[n], RING[(n + 1) % size]) for n in range(size)]
    back = [(b, a) for a, b in ahead]
    out = [[x] for x in chains]
    up, down = list(chains), list(chains)
    for step in range(3):
        for n in range(len(chains)):
            up[n] = lax.ppermute(up[n], "gx", ahead)
            down[n] = lax.ppermute(down[n], "gx", back)
            out[n] += [up[n], down[n]]
        if step < len(fills):
            up[0] = after(up[0], *fills[step])
    return sum([out[n] + [lax.ppermute(up[n], "gx", ahead)] for n in range(len(chains))], [])


def spread(parts, experts):
    if len(parts) == experts:
        return [parts[0]] + [swap(parts[k], "gx", 2 * k) for k in range(1, experts)]
    rows = parts[0].shape[0] // experts
    cut = [parts[0][k * rows : (k + 1) * rows] for k in range(experts)]
    return [jnp.concatenate(spread(cut, experts), axis=0)]


def sum_rows(parts):
    if len(parts) == 1:
        size = lax.axis_size("gx")
        arrived = lax.all_to_all(parts[0], "gx", split_axis=0, concat_axis=0, tiled=True)
        arrived = arrived.reshape(size, parts[0].shape[0] // size, parts[0].shape[1])
        return arrived.astype(F32).sum(axis=0)
    pair = add(parts[0], swap(parts[1], "gx", 1))
    total = pair[0]
    for n in range(1, pair.shape[0]):
        total = total + swap(pair[n].astype(BF), "gx", 2 * n).astype(F32)
    return total


def sum_all(x, axis):
    bit = 1
    while bit < lax.axis_size(axis):
        x = x + swap(x, axis, bit)
        bit *= 2
    return x


def after(x, *others):
    return lax.optimization_barrier((x, *others))[0]


def add(a, b):
    return a.astype(F32) + b.astype(F32)


def on_device(
    layer_input,
    w_query,
    w_key,
    w_value,
    w_output,
    attn_gain,
    moe_gain,
    router,
    rel_table,
    w_in,
    w_out,
    expert_ids,
    buckets,
    block_mask,
    grad_out,
):
    n_gx = lax.axis_size("gx")
    n_gy = lax.axis_size("gy")
    seq, model = layer_input.shape
    heads, bucket_count = rel_table.shape
    width = w_query.shape[1]
    shard = w_query.shape[0]
    experts = router.shape[1]
    hidden = w_in.shape[2]
    capacity = 5 * seq // (4 * experts)
    piece = capacity // (2 * n_gy)
    own = experts * 2 * piece
    blocks = seq // BLOCK
    pairs = blocks * (blocks + 1) // 2
    gy = lax.axis_index("gy").astype(jnp.int32).reshape(1)

    gx = lax.axis_index("gx").astype(jnp.int32).reshape(1)
    group = own // experts
    pieces = experts if group % 16 == 0 else 1

    qkv_w, extras = call(
        pack_kernel,
        "pack",
        [struct((shard, 3 * width), BF), struct((shard, LANES + width), BF)],
        [VM] * 7,
        (
            w_query,
            w_key,
            w_value,
            w_output,
            attn_gain.reshape(1, shard),
            moe_gain.reshape(1, shard),
            router,
        ),
        cost=1,
    )
    half_model = model // 2
    pack = jnp.concatenate([w_in[0], w_out[0][:, :half_model], w_out[0][:, half_model:]], axis=0)
    pack_x = swap(pack, "gy", 2)

    pos_row, pos_col, info = call(
        partial(place_kernel, experts, capacity, group),
        "place",
        [
            struct((1, seq), jnp.int32),
            struct((seq, 1), jnp.int32),
            struct((LANES, seq), BF),
        ],
        [SM, VM],
        (gx, after(expert_ids, qkv_w).reshape(1, seq)),
        cost=2,
    )
    backwards = jnp.concatenate([buckets[::-1], jnp.full((BLOCK,), -1, jnp.int32)])
    brev = jnp.stack(
        [
            backwards[seq - BLOCK * (k + 1) : seq - BLOCK * (k + 1) + 2 * BLOCK]
            for k in range(blocks)
        ]
    )
    table_pad = jnp.concatenate([rel_table, jnp.zeros((8 - heads, bucket_count), F32)], axis=0)
    weights = gather_rows((qkv_w, extras), (pos_row,), (brev, table_pad))
    parts = len(weights) // 2
    pack_y = swap(after(pack, weights[-1]), "gx", 1)
    extras, out_own = call(
        partial(unpack_kernel, parts),
        "unpack",
        [struct((model, LANES), BF), struct((model, width), BF)],
        [SM] + [ANY] * parts,
        (gx, *weights[parts:]),
        scratch=[
            pltpu.VMEM((model, LANES + width), BF),
            pltpu.SemaphoreType.DMA((parts,)),
        ],
        cost=2,
    )
    extras, pack_x = lax.optimization_barrier((extras, pack_x))
    out_core = swap(out_own, "gy", 1)
    out_x = swap(out_own, "gy", 2)
    pack_c = swap(pack, "gy", 1)
    pack_xc = swap(pack_x, "gy", 1)

    h1, qkv, prob, mixed, *sorted_parts, w_full = call(
        partial(attend_kernel, parts),
        "attend",
        [
            struct((seq, model), BF),
            struct((seq, 3 * width), BF),
            struct((heads * pairs, BLOCK, BLOCK), BF),
            struct((seq, width), BF),
        ]
        + [struct((own, width), BF)] * 4
        + [struct((model, 3 * width), BF)],
        [SM, SM, SM] + [VM] * 5 + [ANY] * parts,
        (
            gy,
            gx,
            block_mask,
            layer_input,
            extras,
            table_pad,
            brev,
            pos_row,
            *weights[:parts],
        ),
        scratch=[
            pltpu.VMEM((blocks, BLOCK, BLOCK), F32),
            pltpu.SemaphoreType.DMA((parts,)),
        ],
        cost=60,
    )
    mixed_pieces = [sorted_parts[0]] + [swap(sorted_parts[j], "gy", j) for j in (1, 2, 3)]
    xs, gs, infos = call(
        presort_kernel,
        "presort",
        [struct((own, model), BF), struct((own, model), BF), struct((own, LANES), F32)],
        [SM, VM, VM, VM, VM],
        (gy, after(pos_row, sorted_parts[0]), layer_input, grad_out, info),
        cost=5,
    )
    pack_d = swap(after(pack_x, sorted_parts[0]), "gx", 1)
    out_far = swap(after(out_x, sorted_parts[0]), "gy", 1)
    out_pieces = [out_own, out_core, out_x, out_far]
    mixed_pieces[0], pack_c, pack_xc = lax.optimization_barrier((mixed_pieces[0], pack_c, pack_xc))
    slot_shapes = [struct((own // pieces, model), BF)] * pieces
    routed = call(
        partial(route_kernel, experts, pieces),
        "route",
        slot_shapes
        + slot_shapes
        + [
            struct((own, model), F32),
            struct((own, LANES), F32),
            struct((own, LANES), F32),
        ],
        [VM] * 12,
        (*mixed_pieces, *out_pieces, xs, gs, infos, extras),
        cost=5,
    )
    h2, sg = routed[:pieces], routed[pieces : 2 * pieces]
    residual, router_prob, gate = routed[2 * pieces :]
    pack_yc = swap(after(pack_y, h2[0]), "gy", 1)
    rows_in = spread(h2, experts)
    near = [pack, pack_c, pack_x, pack_xc]
    sg = list(lax.optimization_barrier((*sg, *rows_in))[: len(sg)])
    grads_in = spread(sg, experts)

    def pack_scratch(shards, copies):
        return [
            pltpu.VMEM((shards, 2 * model, hidden), BF),
            pltpu.SemaphoreType.DMA((copies,)),
        ]

    kept_shapes = [struct((4, own, hidden), BF)] * 2
    begun, act_a, slope_a = call(
        partial(expert_kernel, pieces, (1, 1, 1, 1), False),
        "expert_near",
        [struct((own, model), F32)] + kept_shapes,
        [VM] * pieces + [ANY] * 4,
        (*rows_in, *near),
        scratch=pack_scratch(4, 4),
        cost=7,
    )
    pack_d, begun = lax.optimization_barrier((pack_d, begun, *grads_in))[:2]
    far = [pack_y, pack_yc, pack_d, swap(pack_d, "gy", 1)]
    *result, act_b, slope_b = call(
        partial(expert_kernel, pieces, (1, 1, 1, 1), True),
        "expert_far",
        slot_shapes + kept_shapes,
        [VM] * (pieces + 1) + [ANY] * 4,
        (*rows_in, begun, *far),
        scratch=pack_scratch(4, 4),
        cost=7.5,
    )
    result_back = spread(result, experts)
    ours = ((0, 0), (0, 2), (1, 2), (1, 0))
    theirs = ((0, 1), (0, 3), (1, 3), (1, 1))
    (out_sent,) = call(
        partial(outer_sent_kernel, pieces, theirs, True),
        "outer_out_sent",
        [struct((4, hidden, model), BF)],
        [VM] * (pieces + 2),
        (*grads_in, act_a, act_b),
        cost=4.7,
    )
    out_arrived = swap(out_sent, "gy", 1)
    slope_b = after(slope_b, out_sent)
    *grad_rows, grad_pre = call(
        partial(expert_back_kernel, pieces, (1,) * 8),
        "expert_back",
        slot_shapes + [struct((8, own, hidden), BF)],
        [VM] * (pieces + 2) + [ANY] * 8,
        (*grads_in, slope_a, slope_b, *near, *far),
        scratch=pack_scratch(8, 8),
        cost=12,
    )
    rows_back = spread(grad_rows, experts)
    small_rows = -(-(2 + experts) // 8) * 8
    held_args = (*grads_in, act_a, act_b, out_arrived)
    sent_args = (*rows_in, grad_pre)
    deliver_args = (*result_back, residual, xs, gs, infos, router_prob, gate, extras, *h2)
    out_mine, out_by_x, out_far_y, out_by_y, in_sent, d1, grad_hidden, router_part = call(
        partial(
            joined_kernel,
            ((len(held_args), 4), (len(sent_args), 1), (len(deliver_args), 3)),
            (
                partial(outer_held_kernel, pieces, ours, True),
                partial(
                    outer_sent_kernel, pieces, tuple((0, 4 * a + b) for a, b in theirs), False
                ),
                partial(deliver_kernel, experts, pieces),
            ),
        ),
        "fill_rows",
        [
            struct((hidden, model), F32),
            struct((hidden, model), BF),
            struct((hidden, model), BF),
            struct((hidden, model), BF),
            struct((4, model, hidden), BF),
            struct((own, model), BF),
            struct((own, model), F32),
            struct((small_rows, model), F32),
        ],
        [VM] * (len(held_args) + len(sent_args) + len(deliver_args)),
        (*held_args, *sent_args, *deliver_args),
        cost=13,
    )
    out_far_y = swap(out_far_y, "gx", 1)
    in_arrived = swap(in_sent, "gy", 1)
    *mixed_grads, d2, small, project_keep, project_send = call(
        partial(combine_kernel, pieces),
        "combine",
        [struct((own, width), BF)] * 4
        + [
            struct((own, model), BF),
            struct((small_rows, model), F32),
            struct((model, 2 * width), BF),
            struct((model, 2 * width), BF),
        ],
        [VM] * (pieces + 13),
        (
            *rows_back,
            grad_hidden,
            residual,
            gs,
            router_part,
            extras,
            *out_pieces,
            *mixed_pieces,
        ),
        cost=40,
    )
    grads_mixed = [mixed_grads[0]] + [swap(mixed_grads[j], "gy", j) for j in (1, 2, 3)]
    project_other = swap(project_send, "gy", 1)
    in_mine, in_by_x, in_far_y, in_by_y = call(
        partial(outer_held_kernel, pieces, tuple((0, 4 * a + b) for a, b in ours), False),
        "outer_in_held",
        [
            struct((model, hidden), F32),
            struct((model, hidden), BF),
            struct((model, hidden), BF),
            struct((model, hidden), BF),
        ],
        [VM] * (pieces + 2),
        (*rows_in, after(grad_pre, mixed_grads[0]), in_arrived),
        cost=1,
    )
    in_far_y = swap(in_far_y, "gx", 1)
    out_sum_x = add(out_by_x, after(out_far_y, in_mine)).astype(BF)
    grads_mixed[0], in_by_x, out_sum_x = lax.optimization_barrier(
        (grads_mixed[0], in_by_x, out_sum_x)
    )
    out_from_x = swap(out_sum_x, "gy", 2)
    d1_x = swap(after(d1, *grads_mixed[1:]), "gy", 2)
    spare = -(-3 * width // LANES) * LANES - 3 * width
    count = 2 if n_gx == len(RING) and heads * bucket_count == shard else 1
    dw_shape = (model, 3 * width + spare) if count == 1 else (4, shard, 3 * width + spare)
    *dw, keep, send, table = call(
        partial(attend_back_kernel, count),
        "attend_back",
        [struct(dw_shape, BF)] * count
        + [
            struct((2, BLOCK, model), BF),
            struct((2, BLOCK, model), BF),
            struct((bucket_count, 8), F32),
        ],
        [SM, SM] + [VM] * 14,
        (
            gy,
            gx,
            *grads_mixed,
            pos_col,
            prob,
            qkv,
            h1,
            layer_input,
            w_full,
            extras,
            brev,
            d2,
            small,
        ),
        scratch=[
            pltpu.VMEM((seq, width), BF),
            pltpu.VMEM((seq, 3 * width), BF),
            pltpu.VMEM((model, 3 * width + spare), BF),
        ],
        cost=60,
    )
    keep, send, in_far_y, out_from_x, d1_x = lax.optimization_barrier(
        (keep, send, in_far_y, out_from_x, d1_x)
    )
    half = add(keep, swap(send, "gy", 1)).astype(BF)
    half, out_by_y, d1, d1_x, project_keep, *dw = lax.optimization_barrier(
        (half, out_by_y, d1, d1_x, project_keep, *dw)
    )
    out_from_y = swap(out_by_y, "gx", 1)
    d1s = [d1, swap(d1, "gy", 1), d1_x, swap(d1_x, "gy", 1)]
    projected = add(project_keep, project_other).astype(BF)
    projected = lax.all_to_all(projected, "gx", split_axis=0, concat_axis=0, tiled=True)
    total = add(half, swap(half, "gy", 2)[::-1]).astype(BF)
    other = swap(total, "gy", 1)
    summed = sum_rows(dw)
    projected = projected.reshape(n_gx, shard, 2 * width).astype(F32).sum(axis=0)
    small = summed[:, 3 * width :]
    small = small + swap(small, "gy", 1)
    line = swap(jnp.concatenate([small, projected[:, width:]], axis=1), "gy", 2)
    small = small + line[:, :spare]
    grad_out_proj = projected[:, :width] + line[:, spare:]
    if count == 1:
        grad_table = sum_all(table, "gx")[:, :heads].T
    else:
        grad_table = summed[:, -1].reshape(heads, bucket_count)
    (layer_output,) = call(
        unsort_kernel,
        "unsort",
        [struct((seq, model), F32)],
        [SM] + [VM] * 6,
        (gy, pos_col, layer_input, *d1s),
        cost=7,
    )
    (grad_input,) = call(
        finish_kernel,
        "finish",
        [struct((seq, model), F32)],
        [SM] + [VM] * 3,
        (gy, total, other, grad_out),
        cost=4,
    )
    in_sum_x = add(after(in_by_x, half), in_far_y).astype(BF)
    in_from_x = swap(in_sum_x, "gy", 2)
    in_from_y = swap(after(in_by_y, half), "gx", 1)
    grad_w_out = add(add(out_mine, out_from_y), out_from_x)
    grad_w_in = add(add(in_mine, in_from_y), in_from_x)

    return (
        layer_output,
        grad_input,
        summed[:, :width],
        summed[:, width : 2 * width],
        summed[:, 2 * width : 3 * width],
        grad_out_proj,
        small[:, 0],
        small[:, 1],
        small[:, 2 : 2 + experts],
        grad_table,
        grad_w_in[None],
        grad_w_out[None],
    )


def solution(mesh):
    return jax.shard_map(
        on_device,
        mesh=mesh,
        in_specs=(
            P("gx", None),
            P("gx", "gy"),
            P("gx", "gy"),
            P("gx", "gy"),
            P("gx", "gy"),
            P("gx"),
            P("gx"),
            P("gx", None),
            P("gy", None),
            P("gx", None, "gy"),
            P("gx", "gy", None),
            P("gx", None),
            P(),
            P(),
            P("gx", None),
        ),
        out_specs=(
            P("gx", None),
            P("gx", None),
            P("gx", "gy"),
            P("gx", "gy"),
            P("gx", "gy"),
            P("gx", "gy"),
            P("gx"),
            P("gx"),
            P("gx", None),
            P("gy", None),
            P("gx", None, "gy"),
            P("gx", "gy", None),
        ),
        check_vma=False,
    )
```

profile of v0, /device:TPU:0, one launch (start us, length us, event | category | flops | bytes accessed | tf_op | source)
XLA Modules:
  0.0 255.6 jit_solution(2459073925759889661)
XLA Ops:
  2.0 3.0 %collective-permute-start.7 = (bf16[1536,384]{1,0:T(8,128)(2,1)S(1)}, bf16[1536,384]{1,0:T(8,128)(2,1)S(1)}, u32[]{:S(2)}, u32[]{:S(2)}) collective-permute-start(bf16[1536,384]{1,0:T(8,128)(2,1)S(1)} %pad_maximum_fusion.refs_4_.refs_6_), channel_id=1, source_target_pairs={{0,2},{1,3},{2,0},{3,1},{4,6},{5,7},{6,4},{7,5},{8,10},{9,11},{10,... | collective-permute-start | bytes 3538952 | tf_op jit(solution)/shard_map/ppermute | solution.py:608
  5.8 1.7 pack.1
  7.4 1.5 collective-permute-start.1
  9.4 1.5 collective-permute-start.9
  11.5 2.1 place.1
  17.7 1.7 collective-permute-done.2.refs_4_
  25.7 2.3 collective-permute-done.5.refs_7_
  29.1 1.5 collective-permute-start.14
  31.3 2.1 unpack.1
  35.8 13.6 %attend.1 = (bf16[1024,768]{1,0:T(8,128)(2,1)}, bf16[1024,576]{1,0:T(8,128)(2,1)}, bf16[30,256,256]{2,1,0:T(8,128)(2,1)}, bf16[1024,192]{1,0:T(8,128)(2,1)}, bf1...) custom-call(s32[1]{0:T(128)} %bitcast.refs_0_.gy_ref, ...), custom_call_target="tpu_custom_call" | custom-call | flops 69000003584 | bytes 1 | tf_op jit(solution)/shard_map/attend/pallas_call | solution.py:46
  51.9 4.2 %presort.1 = (bf16[320,768]{1,0:T(8,128)(2,1)}, bf16[320,768]{1,0:T(8,128)(2,1)}, f32[320,128]{1,0:T(8,128)}) custom-call(s32[1]{0:T(128)} %bitcast.refs_0_.gy_ref, s32[1,1024]{1,0:T(1,128)} %get-tuple-element.136.refs_7_.pos_ref, bf16[1024,768]{1,0:T(8,128)(2,1)} %x_ref.3, bf16[1024,768]{1,0:T(8,128)(2,1)} %g_ref.3, ...), custom_call_target="tpu_custom_call" | custom-call | flops 5750000128 | bytes 1 | tf_op jit(solution)/shard_map/presort/pallas_call | solution.py:46
  56.1 1.5 collective-permute-start.29
  57.7 1.6 collective-permute-done.19.refs_3_.refs_16_
  60.1 4.7 %route.1 = (bf16[80,768]{1,0:T(8,128)(2,1)}, bf16[80,768]{1,0:T(8,128)(2,1)}, bf16[80,768]{1,0:T(8,128)(2,1)}, bf16[80,768]{1,0:T(8,128)(2,1)}, bf16[80,768]{1,0...) custom-call(bf16[320,192]{1,0:T(8,128)(2,1)} %get-tuple-element.130., ...), custom_call_target="tpu_custom_call" | custom-call | flops 5750000128 | bytes 1 | tf_op jit(solution)/shard_map/route/pallas_call | solution.py:46
  64.9 1.6 collective-permute-start.23
  66.5 2.6 %collective-permute-start.24 = (bf16[80,768]{1,0:T(8,128)(2,1)}, bf16[80,768]{1,0:T(8,128)(2,1)S(1)}, u32[]{:S(2)}, u32[]{:S(2)}) collective-permute-start(bf16[80,768]{1,0:T(8,128)(2,1)} %get-tuple-element.147.refs_25_), channel_id=1, source_target_pairs={{0,16},{4,20},{8,24},{12,28},{16,0},{20,4},{24,8},{28,12},{1,17},{... | collective-permute-start | bytes 368648 | tf_op jit(solution)/shard_map/ppermute | solution.py:608
  69.3 4.1 %collective-permute-done.23.refs_1_.refs_8_ = bf16[80,768]{1,0:T(8,128)(2,1)S(1)} collective-permute-done((bf16[80,768]{1,0:T(8,128)(2,1)}, bf16[80,768]{1,0:T(8,128)(2,1)S(1)}, u32[]{:S(2)}, u32[]{:S(2)}) %collective-permute-start.23) | collective-permute-done | bytes 122912 | tf_op jit(solution)/shard_map/ppermute | solution.py:608
  73.4 5.6 %collective-permute-done.24.refs_2_.refs_9_ = bf16[80,768]{1,0:T(8,128)(2,1)S(1)} collective-permute-done((bf16[80,768]{1,0:T(8,128)(2,1)}, bf16[80,768]{1,0:T(8,128)(2,1)S(1)}, u32[]{:S(2)}, u32[]{:S(2)}) %collective-permute-start.24) | collective-permute-done | bytes 122912 | tf_op jit(solution)/shard_map/ppermute | solution.py:608
  79.0 2.7 %collective-permute-start.26 = (bf16[80,768]{1,0:T(8,128)(2,1)}, bf16[80,768]{1,0:T(8,128)(2,1)S(1)}, u32[]{:S(2)}, u32[]{:S(2)}) collective-permute-start(bf16[80,768]{1,0:T(8,128)(2,1)} %get-tuple-element.150), channel_id=1, source_target_pairs={{0,8},{4,12},{8,0},{12,4},{16,24},{20,28},{24,16},{28,20},{1,9},{5... | collective-permute-start | bytes 368648 | tf_op jit(solution)/shard_map/ppermute | solution.py:608
  82.8 1.5 collective-permute-start.28
  84.3 7.4 %expert_near.1 = (f32[320,768]{1,0:T(8,128)}, bf16[4,320,384]{2,1,0:T(8,128)(2,1)}, bf16[4,320,384]{2,1,0:T(8,128)(2,1)}) custom-call(bf16[80,768]{1,0:T(8,128)(2,1)} %get-tuple-element.145.refs_0_.refs_7_.refs_23_, bf16[80,768]{1,0:T(8,128)(2,1)} %copy-done.11, bf16[80,768]{1,0:T(8,128)(2,1)} %copy-done.12, bf16[80,768]{1,0:T(8,128)(2,1)} %copy-done.13, ...), custom_call_target="tpu_custom_call" | custom-call | flops 8049999872 | bytes 1 | tf_op jit(solution)/shard_map/expert_near/pallas_call | solution.py:46
  91.8 2.4 collective-permute-done.27.refs_2_
  94.3 2.8 %collective-permute-done.32.refs_8_.refs_13_ = bf16[1536,384]{1,0:T(8,128)(2,1)S(1)} collective-permute-done((bf16[1536,384]{1,0:T(8,128)(2,1)S(1)}, bf16[1536,384]{1,0:T(8,128)(2,1)S(1)}, u32[]{:S(2)}, u32[]{:S(2)}) %collective-permute-start.32) | collective-permute-done | bytes 1179680 | tf_op jit(solution)/shard_map/ppermute | solution.py:608
  98.1 7.5 %expert_far.1 = (bf16[80,768]{1,0:T(8,128)(2,1)}, bf16[80,768]{1,0:T(8,128)(2,1)}, bf16[80,768]{1,0:T(8,128)(2,1)}, bf16[80,768]{1,0:T(8,128)(2,1)}, bf16[4,320,...) custom-call(bf16[80,768]{1,0:T(8,128)(2,1)} %get-tuple-element.145.refs_0_.refs_7_.refs_23_, bf16[80,768]{1,0:T(8,128)(2,1)} %copy-done.11, ...), custom_call_target="tpu_custom_call" | custom-call | flops 8625000448 | bytes 1 | tf_op jit(solution)/shard_map/expert_far/pallas_call | solution.py:46
  105.7 4.6 %outer_out_sent.1 = bf16[4,384,768]{2,1,0:T(8,128)(2,1)} custom-call(bf16[80,768]{1,0:T(8,128)(2,1)} %get-tuple-element.149.refs_0_, bf16[80,768]{1,0:T(8,128)(2,1)} %copy-done.43, bf16[80,768]{1,0:T(8,128)(2,1)} %copy-done.44, bf16[80,768]{1,0:T(8,128)(2,1)} %copy-done.46, bf16[4,320,384]{2,1,0:T(8,128)(2,1)} %get-tuple-element.163.refs_4_, ...), custom_call_target="tpu_custom_call" | custom-call | flops 5405000192 | bytes 1 | tf_op jit(solution)/shard_map/outer_out_sent/pallas_call | solution.py:46
  110.4 1.8 collective-permute-start.37
  113.3 1.5 collective-permute-start.39
  114.8 12.3 %expert_back.1 = (bf16[80,768]{1,0:T(8,128)(2,1)}, bf16[80,768]{1,0:T(8,128)(2,1)}, bf16[80,768]{1,0:T(8,128)(2,1)}, bf16[80,768]{1,0:T(8,128)(2,1)}, bf16[8,320,384]{2,1,0:T(8,128)(2,1)}) custom-call(bf16[80,768]{1,0:T(8,128)(2,1)} %get-tuple-element.149.refs_0_, bf16[80,768]{1,0:T(8,128)(2,1)} %copy-done.43, bf16[80,768]{1,0:T(8,128)(2,1)} %copy-done.44, ...), custom_call_target="tpu_custom_call" | custom-call | flops 13799999488 | bytes 1 | tf_op jit(solution)/shard_map/expert_back/pallas_call | solution.py:46
  128.1 1.9 collective-permute-start.34
  130.0 1.5 collective-permute-start.35
  133.0 9.0 %fill_rows.1 = (f32[384,768]{1,0:T(8,128)}, bf16[384,768]{1,0:T(8,128)(2,1)}, bf16[384,768]{1,0:T(8,128)(2,1)}, bf16[384,768]{1,0:T(8,128)(2,1)}, bf16[4,768,384...) custom-call(bf16[80,768]{1,0:T(8,128)(2,1)} %get-tuple-element.149.refs_0_, ...), custom_call_target="tpu_custom_call" | custom-call | flops 14949999616 | bytes 1 | tf_op jit(solution)/shard_map/fill_rows/pallas_call | solution.py:46
  142.1 1.5 collective-permute-start.41
  144.4 5.3 %combine.1 = (bf16[320,192]{1,0:T(8,128)(2,1)}, bf16[320,192]{1,0:T(8,128)(2,1)}, bf16[320,192]{1,0:T(8,128)(2,1)}, bf16[320,192]{1,0:T(8,128)(2,1)}, bf16[320,7...) custom-call(bf16[80,768]{1,0:T(8,128)(2,1)} %get-tuple-element.166.refs_0_, ...), custom_call_target="tpu_custom_call" | custom-call | flops 46000001024 | bytes 1 | tf_op jit(solution)/shard_map/combine/pallas_call | solution.py:46
  151.6 5.8 %collective-permute-done.43.refs_4_ = bf16[320,192]{1,0:T(8,128)(2,1)S(1)} collective-permute-done((bf16[320,192]{1,0:T(8,128)(2,1)}, bf16[320,192]{1,0:T(8,128)(2,1)S(1)}, u32[]{:S(2)}, u32[]{:S(2)}) %collective-permute-start.43) | collective-permute-done | bytes 122912 | tf_op jit(solution)/shard_map/ppermute | solution.py:608
  157.4 1.7 collective-permute-done.44.refs_5_
  161.6 5.0 %outer_in_held.1 = (f32[768,384]{1,0:T(8,128)}, bf16[768,384]{1,0:T(8,128)(2,1)}, bf16[768,384]{1,0:T(8,128)(2,1)}, bf16[768,384]{1,0:T(8,128)(2,1)}) custom-call(bf16[80,768]{1,0:T(8,128)(2,1)} %get-tuple-element.145.refs_0_.refs_7_.refs_23_, bf16[80,768]{1,0:T(8,128)(2,1)} %copy-done.11, bf16[80,768]{1,0:T(8,128)(2,1)} %copy-done.12, ...), custom_call_target="tpu_custom_call" | custom-call | flops 1150000000 | bytes 1 | tf_op jit(solution)/shard_map/outer_in_held/pallas_call | solution.py:46
  168.6 20.3 %attend_back.1 = (bf16[4,96,640]{2,1,0:T(8,128)(2,1)}, bf16[4,96,640]{2,1,0:T(8,128)(2,1)}, bf16[2,256,768]{2,1,0:T(8,128)(2,1)}, bf16[2,256,768]{2,1,0:T(8,128)(2,1)}, f32[32,8]{1,0:T(8,128)}) custom-call(s32[1]{0:T(128)} %bitcast.refs_0_.gy_ref, s32[1]{0:T(128)} %bitcast.1.gx_ref.refs_0_.refs_1_, bf16[320,192]{1,0:T(8,128)(2,1)} %get-tuple-element.188.refs_2_, ...), custom_call_target="tpu_custom_call" | custom-call | flops 69000003584 | bytes 1 | tf_op jit(solution)/shard_map/attend_back/pallas_call | solution.py:46
  189.8 1.8 collective-permute-done.48
  196.3 4.2 %all-to-all-start = ((bf16[8,96,384]{2,1,0:T(8,128)(2,1)}), bf16[8,96,384]{2,1,0:T(8,128)(2,1)S(1)}, u32[]{:S(2)}, u32[]{:S(2)}) async-start(bf16[8,96,384]{2,1,0:T(8,128)(2,1)} %bitcast.15), calls=%async_computation | async-start | bytes 1179648 | tf_op jit(solution)/shard_map/all_to_all | solution.py:1010
  201.1 2.0 collective-permute-start.60
  204.3 8.3 %collective-permute-done.53 = bf16[4,96,640]{2,1,0:T(8,128)(2,1)} collective-permute-done((bf16[4,96,640]{2,1,0:T(8,128)(2,1)}, bf16[4,96,640]{2,1,0:T(8,128)(2,1)}, u32[]{:S(2)}, u32[]{:S(2)}) %collective-permute-start.53) | collective-permute-done | bytes 491552 | tf_op jit(solution)/shard_map/ppermute | solution.py:608
  214.6 1.4 collective-permute-start.62
  216.8 7.3 %unsort.1 = f32[1024,768]{1,0:T(8,128)} custom-call(s32[1]{0:T(128)} %bitcast.refs_0_.gy_ref, s32[1024,1]{1,0:T(8,128)} %get-tuple-element.121.refs_6_.pos_ref, bf16[1024,768]{1,0:T(8,128)(2,1)} %x_ref.3, bf16[320,768]{1,0:T(8,128)(2,1)} %get-tuple-element.211.d0_ref, bf16[320,768]{1,0:T(8,128)(2,1)} %copy-done.30, bf16[320,768]{1,0:T(8,128)(2,1)} %copy-done.29, ...), custom_call_target="tpu_custom_call" | custom-call | flops 8049999872 | bytes 1 | tf_op jit(solution)/shard_map/unsort/pallas_call | solution.py:46
  224.2 3.4 %collective-permute-done.60 = bf16[768,384]{1,0:T(8,128)(2,1)S(1)} collective-permute-done((bf16[768,384]{1,0:T(8,128)(2,1)}, bf16[768,384]{1,0:T(8,128)(2,1)S(1)}, u32[]{:S(2)}, u32[]{:S(2)}) %collective-permute-start.60) | collective-permute-done | bytes 589856 | tf_op jit(solution)/shard_map/ppermute | solution.py:608
  227.6 2.3 collective-permute-start.56
  231.1 8.0 %collective-permute-done.62 = bf16[384,768]{1,0:T(8,128)(2,1)S(1)} collective-permute-done((bf16[384,768]{1,0:T(8,128)(2,1)}, bf16[384,768]{1,0:T(8,128)(2,1)S(1)}, u32[]{:S(2)}, u32[]{:S(2)}) %collective-permute-start.62) | collective-permute-done | bytes 589856 | tf_op jit(solution)/shard_map/ppermute | solution.py:608
  245.0 3.5 %collective-permute-done.59 = f32[96,256]{1,0:T(8,128)S(1)} collective-permute-done((f32[96,256]{1,0:T(8,128)S(1)}, f32[96,256]{1,0:T(8,128)S(1)}, u32[]{:S(2)}, u32[]{:S(2)}) %collective-permute-start.59) | collective-permute-done | bytes 98336 | tf_op jit(solution)/shard_map/ppermute | solution.py:608
  251.6 3.9 %finish.1 = f32[1024,768]{1,0:T(8,128)} custom-call(s32[1]{0:T(128)} %bitcast.refs_0_.gy_ref, bf16[2,256,768]{2,1,0:T(8,128)(2,1)} %copy-done.4, bf16[2,256,768]{2,1,0:T(8,128)(2,1)} %copy-done.25, bf16[1024,768]{1,0:T(8,128)(2,1)} %g_ref.3), custom_call_target="tpu_custom_call" | custom-call | flops 4600000000 | bytes 1 | tf_op jit(solution)/shard_map/finish/pallas_call | solution.py:46
  (260 shorter events, 54.0 us)
Async XLA Ops:
  2.0 32.2 %collective-permute-start.7 = (bf16[1536,384]{1,0:T(8,128)(2,1)S(1)}, bf16[1536,384]{1,0:T(8,128)(2,1)S(1)}, u32[]{:S(2)}, u32[]{:S(2)}) collective-permute-start(bf16[1536,384]{1,0:T(8,128)(2,1)S(1)} %pad_maximum_fusion.refs_4_.refs_6_), channel_id=1, source_target_pairs={{0,2},{1,3},{2,0},{3,1},{4,6},{5,7},{6,4},{7,5},{8,10},{9,11},{10,... | collective-permute-start | bytes 3538952 | tf_op jit(solution)/shard_map/ppermute | solution.py:608
  7.4 8.2 %collective-permute-start.1 = (bf16[96,320]{1,0:T(8,128)(2,1)}, bf16[96,320]{1,0:T(8,128)(2,1)S(1)}, u32[]{:S(2)}, u32[]{:S(2)}) collective-permute-start(bf16[96,320]{1,0:T(8,128)(2,1)} %get-tuple-element.122.refs_1_), channel_id=1, source_target_pairs={{8,0},{16,8},{24,16},{28,24},{20,28},{12,20},{4,12},{0,4},{9,1},{1... | collective-permute-start | bytes 184328 | tf_op jit(solution)/shard_map/ppermute | solution.py:631
  9.4 12.2 %collective-permute-start.9 = (bf16[96,576]{1,0:T(8,128)(2,1)}, bf16[96,576]{1,0:T(8,128)(2,1)S(1)}, u32[]{:S(2)}, u32[]{:S(2)}) collective-permute-start(bf16[96,576]{1,0:T(8,128)(2,1)} %get-tuple-element.119.refs_8_), channel_id=1, source_target_pairs={{8,0},{16,8},{24,16},{28,24},{20,28},{12,20},{4,12},{0,4},{9,1},{1... | collective-permute-start | bytes 331784 | tf_op jit(solution)/shard_map/ppermute | solution.py:631
  15.6 8.1 %collective-permute-start.3 = (bf16[96,320]{1,0:T(8,128)(2,1)S(1)}, bf16[96,320]{1,0:T(8,128)(2,1)S(1)}, u32[]{:S(2)}, u32[]{:S(2)}) collective-permute-start(bf16[96,320]{1,0:T(8,128)(2,1)S(1)} %collective-permute-done.1.refs_3_), channel_id=1, source_target_pairs={{8,0},{16,8},{24,16},{28,24},{20,28},{12,20},{4,12},{0,4},{9,1},{1... | collective-permute-start | bytes 184328 | tf_op jit(solution)/shard_map/ppermute | solution.py:631
  22.6 6.5 %collective-permute-start.12 = (bf16[96,576]{1,0:T(8,128)(2,1)S(1)}, bf16[96,576]{1,0:T(8,128)(2,1)}, u32[]{:S(2)}, u32[]{:S(2)}) collective-permute-start(bf16[96,576]{1,0:T(8,128)(2,1)S(1)} %collective-permute-done.10.refs_11_), channel_id=1, source_target_pairs={{0,8},{8,16},{16,24},{24,28},{28,20},{20,12},{12,4},{4,0},{1,9},{9... | collective-permute-start | bytes 331784 | tf_op jit(solution)/shard_map/ppermute | solution.py:630
  28.0 23.2 %collective-permute-start.15 = (bf16[1536,384]{1,0:T(8,128)(2,1)S(1)}, bf16[1536,384]{1,0:T(8,128)(2,1)S(1)}, u32[]{:S(2)}, u32[]{:S(2)}) collective-permute-start(bf16[1536,384]{1,0:T(8,128)(2,1)S(1)} %pad_maximum_fusion.refs_4_.refs_6_), channel_id=1, source_target_pairs={{0,1},{1,0},{2,3},{3,2},{4,5},{5,4},{6,7},{7,6},{8,9},{9,8},{10,11... | collective-permute-start | bytes 3538952 | tf_op jit(solution)/shard_map/ppermute | solution.py:608
  33.4 16.1 %collective-permute-start.21 = (bf16[768,192]{1,0:T(8,128)(2,1)}, bf16[768,192]{1,0:T(8,128)(2,1)S(1)}, u32[]{:S(2)}, u32[]{:S(2)}) collective-permute-start(bf16[768,192]{1,0:T(8,128)(2,1)} %get-tuple-element.134.refs_4_.refs_9_), channel_id=1, source_target_pairs={{0,2},{1,3},{2,0},{3,1},{4,6},{5,7},{6,4},{7,5},{8,10},{9,11},{10,... | collective-permute-start | bytes 884744 | tf_op jit(solution)/shard_map/ppermute | solution.py:608
  34.2 15.5 %collective-permute-start.20 = (bf16[768,192]{1,0:T(8,128)(2,1)}, bf16[768,192]{1,0:T(8,128)(2,1)S(1)}, u32[]{:S(2)}, u32[]{:S(2)}) collective-permute-start(bf16[768,192]{1,0:T(8,128)(2,1)} %get-tuple-element.134.refs_4_.refs_9_), channel_id=1, source_target_pairs={{0,1},{1,0},{2,3},{3,2},{4,5},{5,4},{6,7},{7,6},{8,9},{9,8},{10,11... | collective-permute-start | bytes 884744 | tf_op jit(solution)/shard_map/ppermute | solution.py:608
  34.2 35.1 %collective-permute-start.30 = (bf16[1536,384]{1,0:T(8,128)(2,1)S(1)}, bf16[1536,384]{1,0:T(8,128)(2,1)S(1)}, u32[]{:S(2)}, u32[]{:S(2)}) collective-permute-start(bf16[1536,384]{1,0:T(8,128)(2,1)S(1)} %pad_maximum_fusion.refs_4_.refs_6_), channel_id=1, source_target_pairs={{0,4},{4,0},{8,12},{12,8},{16,20},{20,16},{24,28},{28,24},{1,5},{5... | collective-permute-start | bytes 3538952 | tf_op jit(solution)/shard_map/ppermute | solution.py:608
  35.2 16.2 %collective-permute-start.16 = (bf16[1536,384]{1,0:T(8,128)(2,1)S(1)}, bf16[1536,384]{1,0:T(8,128)(2,1)S(1)}, u32[]{:S(2)}, u32[]{:S(2)}) collective-permute-start(bf16[1536,384]{1,0:T(8,128)(2,1)S(1)} %collective-permute-done.7.refs_6_.refs_8_), channel_id=1, source_target_pairs={{0,1},{1,0},{2,3},{3,2},{4,5},{5,4},{6,7},{7,6},{8,9},{9,8},{10,11... | collective-permute-start | bytes 3538952 | tf_op jit(solution)/shard_map/ppermute | solution.py:608
  49.5 6.6 %collective-permute-start.17 = (bf16[320,192]{1,0:T(8,128)(2,1)}, bf16[320,192]{1,0:T(8,128)(2,1)S(1)}, u32[]{:S(2)}, u32[]{:S(2)}) collective-permute-start(bf16[320,192]{1,0:T(8,128)(2,1)} %get-tuple-element.131), channel_id=1, source_target_pairs={{0,1},{1,0},{2,3},{3,2},{4,5},{5,4},{6,7},{7,6},{8,9},{9,8},{10,11... | collective-permute-start | bytes 368648 | tf_op jit(solution)/shard_map/ppermute | solution.py:608
  49.7 7.9 %collective-permute-start.18 = (bf16[320,192]{1,0:T(8,128)(2,1)}, bf16[320,192]{1,0:T(8,128)(2,1)S(1)}, u32[]{:S(2)}, u32[]{:S(2)}) collective-permute-start(bf16[320,192]{1,0:T(8,128)(2,1)} %get-tuple-element.132), channel_id=1, source_target_pairs={{0,2},{1,3},{2,0},{3,1},{4,6},{5,7},{6,4},{7,5},{8,10},{9,11},{10,... | collective-permute-start | bytes 368648 | tf_op jit(solution)/shard_map/ppermute | solution.py:608
  51.2 8.1 %collective-permute-start.19 = (bf16[320,192]{1,0:T(8,128)(2,1)}, bf16[320,192]{1,0:T(8,128)(2,1)S(1)}, u32[]{:S(2)}, u32[]{:S(2)}) collective-permute-start(bf16[320,192]{1,0:T(8,128)(2,1)} %get-tuple-element.133), channel_id=1, source_target_pairs={{0,3},{1,2},{2,1},{3,0},{4,7},{5,6},{6,5},{7,4},{8,11},{9,10},{10,... | collective-permute-start | bytes 368648 | tf_op jit(solution)/shard_map/ppermute | solution.py:608
  51.4 7.9 %collective-permute-start.22 = (bf16[768,192]{1,0:T(8,128)(2,1)S(1)}, bf16[768,192]{1,0:T(8,128)(2,1)S(1)}, u32[]{:S(2)}, u32[]{:S(2)}) collective-permute-start(bf16[768,192]{1,0:T(8,128)(2,1)S(1)} %collective-permute-done.21.refs_6_.refs_11_), channel_id=1, source_target_pairs={{0,1},{1,0},{2,3},{3,2},{4,5},{5,4},{6,7},{7,6},{8,9},{9,8},{10,11... | collective-permute-start | bytes 884744 | tf_op jit(solution)/shard_map/ppermute | solution.py:608
  56.1 35.6 %collective-permute-start.29 = (bf16[1536,384]{1,0:T(8,128)(2,1)S(1)}, bf16[1536,384]{1,0:T(8,128)(2,1)S(1)}, u32[]{:S(2)}, u32[]{:S(2)}) collective-permute-start(bf16[1536,384]{1,0:T(8,128)(2,1)S(1)} %collective-permute-done.7.refs_6_.refs_8_), channel_id=1, source_target_pairs={{0,4},{4,0},{8,12},{12,8},{16,20},{20,16},{24,28},{28,24},{1,5},{5... | collective-permute-start | bytes 3538952 | tf_op jit(solution)/shard_map/ppermute | solution.py:608
  64.9 8.6 %collective-permute-start.23 = (bf16[80,768]{1,0:T(8,128)(2,1)}, bf16[80,768]{1,0:T(8,128)(2,1)S(1)}, u32[]{:S(2)}, u32[]{:S(2)}) collective-permute-start(bf16[80,768]{1,0:T(8,128)(2,1)} %get-tuple-element.146.refs_24_), channel_id=1, source_target_pairs={{0,8},{4,12},{8,0},{12,4},{16,24},{20,28},{24,16},{28,20},{1,9},{5... | collective-permute-start | bytes 368648 | tf_op jit(solution)/shard_map/ppermute | solution.py:608
  66.5 12.5 %collective-permute-start.24 = (bf16[80,768]{1,0:T(8,128)(2,1)}, bf16[80,768]{1,0:T(8,128)(2,1)S(1)}, u32[]{:S(2)}, u32[]{:S(2)}) collective-permute-start(bf16[80,768]{1,0:T(8,128)(2,1)} %get-tuple-element.147.refs_25_), channel_id=1, source_target_pairs={{0,16},{4,20},{8,24},{12,28},{16,0},{20,4},{24,8},{28,12},{1,17},{... | collective-permute-start | bytes 368648 | tf_op jit(solution)/shard_map/ppermute | solution.py:608
  69.1 9.9 %collective-permute-start.25 = (bf16[80,768]{1,0:T(8,128)(2,1)}, bf16[80,768]{1,0:T(8,128)(2,1)S(1)}, u32[]{:S(2)}, u32[]{:S(2)}) collective-permute-start(bf16[80,768]{1,0:T(8,128)(2,1)} %get-tuple-element.148.refs_26_), channel_id=1, source_target_pairs={{0,24},{4,28},{8,16},{12,20},{16,8},{20,12},{24,0},{28,4},{1,25},{... | collective-permute-start | bytes 368648 | tf_op jit(solution)/shard_map/ppermute | solution.py:608
  69.3 24.9 %collective-permute-start.31 = (bf16[1536,384]{1,0:T(8,128)(2,1)S(1)}, bf16[1536,384]{1,0:T(8,128)(2,1)S(1)}, u32[]{:S(2)}, u32[]{:S(2)}) collective-permute-start(bf16[1536,384]{1,0:T(8,128)(2,1)S(1)} %collective-permute-done.30.refs_5_.refs_10_), channel_id=1, source_target_pairs={{0,1},{1,0},{2,3},{3,2},{4,5},{5,4},{6,7},{7,6},{8,9},{9,8},{10,11... | collective-permute-start | bytes 3538952 | tf_op jit(solution)/shard_map/ppermute | solution.py:608
  79.0 12.7 %collective-permute-start.26 = (bf16[80,768]{1,0:T(8,128)(2,1)}, bf16[80,768]{1,0:T(8,128)(2,1)S(1)}, u32[]{:S(2)}, u32[]{:S(2)}) collective-permute-start(bf16[80,768]{1,0:T(8,128)(2,1)} %get-tuple-element.150), channel_id=1, source_target_pairs={{0,8},{4,12},{8,0},{12,4},{16,24},{20,28},{24,16},{28,20},{1,9},{5... | collective-permute-start | bytes 368648 | tf_op jit(solution)/shard_map/ppermute | solution.py:608
  81.8 12.4 %collective-permute-start.27 = (bf16[80,768]{1,0:T(8,128)(2,1)}, bf16[80,768]{1,0:T(8,128)(2,1)S(1)}, u32[]{:S(2)}, u32[]{:S(2)}) collective-permute-start(bf16[80,768]{1,0:T(8,128)(2,1)} %get-tuple-element.151), channel_id=1, source_target_pairs={{0,16},{4,20},{8,24},{12,28},{16,0},{20,4},{24,8},{28,12},{1,17},{... | collective-permute-start | bytes 368648 | tf_op jit(solution)/shard_map/ppermute | solution.py:608
  82.8 11.3 %collective-permute-start.28 = (bf16[80,768]{1,0:T(8,128)(2,1)}, bf16[80,768]{1,0:T(8,128)(2,1)S(1)}, u32[]{:S(2)}, u32[]{:S(2)}) collective-permute-start(bf16[80,768]{1,0:T(8,128)(2,1)} %get-tuple-element.152), channel_id=1, source_target_pairs={{0,24},{4,28},{8,16},{12,20},{16,8},{20,12},{24,0},{28,4},{1,25},{... | collective-permute-start | bytes 368648 | tf_op jit(solution)/shard_map/ppermute | solution.py:608
  110.3 21.3 %collective-permute-start.36 = (bf16[4,384,768]{2,1,0:T(8,128)(2,1)}, bf16[4,384,768]{2,1,0:T(8,128)(2,1)S(1)}, u32[]{:S(2)}, u32[]{:S(2)}) collective-permute-start(bf16[4,384,768]{2,1,0:T(8,128)(2,1)} %outer_out_sent.1), channel_id=1, source_target_pairs={{0,1},{1,0},{2,3},{3,2},{4,5},{5,4},{6,7},{7,6},{8,9},{9,8},{10,11... | collective-permute-start | bytes 7077896 | tf_op jit(solution)/shard_map/ppermute | solution.py:608
  110.4 17.7 %collective-permute-start.37 = (bf16[80,768]{1,0:T(8,128)(2,1)S(1)}, bf16[80,768]{1,0:T(8,128)(2,1)S(1)}, u32[]{:S(2)}, u32[]{:S(2)}) collective-permute-start(bf16[80,768]{1,0:T(8,128)(2,1)S(1)} %copy-done.57), channel_id=1, source_target_pairs={{0,8},{4,12},{8,0},{12,4},{16,24},{20,28},{24,16},{28,20},{1,9},{5... | collective-permute-start | bytes 368648 | tf_op jit(solution)/shard_map/ppermute | solution.py:608
  112.2 17.8 %collective-permute-start.38 = (bf16[80,768]{1,0:T(8,128)(2,1)S(1)}, bf16[80,768]{1,0:T(8,128)(2,1)S(1)}, u32[]{:S(2)}, u32[]{:S(2)}) collective-permute-start(bf16[80,768]{1,0:T(8,128)(2,1)S(1)} %copy-done.56), channel_id=1, source_target_pairs={{0,16},{4,20},{8,24},{12,28},{16,0},{20,4},{24,8},{28,12},{1,17},{... | collective-permute-start | bytes 368648 | tf_op jit(solution)/shard_map/ppermute | solution.py:608
  113.3 18.3 %collective-permute-start.39 = (bf16[80,768]{1,0:T(8,128)(2,1)S(1)}, bf16[80,768]{1,0:T(8,128)(2,1)S(1)}, u32[]{:S(2)}, u32[]{:S(2)}) collective-permute-start(bf16[80,768]{1,0:T(8,128)(2,1)S(1)} %copy-done.55), channel_id=1, source_target_pairs={{0,24},{4,28},{8,16},{12,20},{16,8},{20,12},{24,0},{28,4},{1,25},{... | collective-permute-start | bytes 368648 | tf_op jit(solution)/shard_map/ppermute | solution.py:608
  127.1 16.5 %collective-permute-start.33 = (bf16[80,768]{1,0:T(8,128)(2,1)}, bf16[80,768]{1,0:T(8,128)(2,1)S(1)}, u32[]{:S(2)}, u32[]{:S(2)}) collective-permute-start(bf16[80,768]{1,0:T(8,128)(2,1)} %get-tuple-element.167), channel_id=1, source_target_pairs={{0,8},{4,12},{8,0},{12,4},{16,24},{20,28},{24,16},{28,20},{1,9},{5... | collective-permute-start | bytes 368648 | tf_op jit(solution)/shard_map/ppermute | solution.py:608
  128.1 15.5 %collective-permute-start.34 = (bf16[80,768]{1,0:T(8,128)(2,1)}, bf16[80,768]{1,0:T(8,128)(2,1)S(1)}, u32[]{:S(2)}, u32[]{:S(2)}) collective-permute-start(bf16[80,768]{1,0:T(8,128)(2,1)} %get-tuple-element.168), channel_id=1, source_target_pairs={{0,16},{4,20},{8,24},{12,28},{16,0},{20,4},{24,8},{28,12},{1,17},{... | collective-permute-start | bytes 368648 | tf_op jit(solution)/shard_map/ppermute | solution.py:608
  130.0 13.6 %collective-permute-start.35 = (bf16[80,768]{1,0:T(8,128)(2,1)}, bf16[80,768]{1,0:T(8,128)(2,1)S(1)}, u32[]{:S(2)}, u32[]{:S(2)}) collective-permute-start(bf16[80,768]{1,0:T(8,128)(2,1)} %get-tuple-element.169), channel_id=1, source_target_pairs={{0,24},{4,28},{8,16},{12,20},{16,8},{20,12},{24,0},{28,4},{1,25},{... | collective-permute-start | bytes 368648 | tf_op jit(solution)/shard_map/ppermute | solution.py:608
  142.1 24.6 %collective-permute-start.41 = (bf16[384,768]{1,0:T(8,128)(2,1)}, bf16[384,768]{1,0:T(8,128)(2,1)S(1)}, u32[]{:S(2)}, u32[]{:S(2)}) collective-permute-start(bf16[384,768]{1,0:T(8,128)(2,1)} %get-tuple-element.185), channel_id=1, source_target_pairs={{0,4},{4,0},{8,12},{12,8},{16,20},{20,16},{24,28},{28,24},{1,5},{5... | collective-permute-start | bytes 1769480 | tf_op jit(solution)/shard_map/ppermute | solution.py:608
  143.6 16.7 %collective-permute-start.40 = (bf16[4,768,384]{2,1,0:T(8,128)(2,1)}, bf16[4,768,384]{2,1,0:T(8,128)(2,1)S(1)}, u32[]{:S(2)}, u32[]{:S(2)}) collective-permute-start(bf16[4,768,384]{2,1,0:T(8,128)(2,1)} %get-tuple-element.182), channel_id=1, source_target_pairs={{0,1},{1,0},{2,3},{3,2},{4,5},{5,4},{6,7},{7,6},{8,9},{9,8},{10,11... | collective-permute-start | bytes 7077896 | tf_op jit(solution)/shard_map/ppermute | solution.py:608
  150.2 7.3 %collective-permute-start.43 = (bf16[320,192]{1,0:T(8,128)(2,1)}, bf16[320,192]{1,0:T(8,128)(2,1)S(1)}, u32[]{:S(2)}, u32[]{:S(2)}) collective-permute-start(bf16[320,192]{1,0:T(8,128)(2,1)} %get-tuple-element.190), channel_id=1, source_target_pairs={{0,2},{1,3},{2,0},{3,1},{4,6},{5,7},{6,4},{7,5},{8,10},{9,11},{10,... | collective-permute-start | bytes 368648 | tf_op jit(solution)/shard_map/ppermute | solution.py:608
  151.2 8.0 %collective-permute-start.44 = (bf16[320,192]{1,0:T(8,128)(2,1)}, bf16[320,192]{1,0:T(8,128)(2,1)S(1)}, u32[]{:S(2)}, u32[]{:S(2)}) collective-permute-start(bf16[320,192]{1,0:T(8,128)(2,1)} %get-tuple-element.191), channel_id=1, source_target_pairs={{0,3},{1,2},{2,1},{3,0},{4,7},{5,6},{6,5},{7,4},{8,11},{9,10},{10,... | collective-permute-start | bytes 368648 | tf_op jit(solution)/shard_map/ppermute | solution.py:608
  159.2 29.8 %collective-permute-start.47 = (bf16[320,768]{1,0:T(8,128)(2,1)S(1)}, bf16[320,768]{1,0:T(8,128)(2,1)S(1)}, u32[]{:S(2)}, u32[]{:S(2)}) collective-permute-start(bf16[320,768]{1,0:T(8,128)(2,1)S(1)} %copy-done.28), channel_id=1, source_target_pairs={{0,2},{1,3},{2,0},{3,1},{4,6},{5,7},{6,4},{7,5},{8,10},{9,11},{10,... | collective-permute-start | bytes 1474568 | tf_op jit(solution)/shard_map/ppermute | solution.py:608
  166.8 22.2 %collective-permute-start.46 = (bf16[384,768]{1,0:T(8,128)(2,1)S(1)}, bf16[384,768]{1,0:T(8,128)(2,1)S(1)}, u32[]{:S(2)}, u32[]{:S(2)}) collective-permute-start(bf16[384,768]{1,0:T(8,128)(2,1)S(1)} %add_convert_fusion.4), channel_id=1, source_target_pairs={{0,2},{1,3},{2,0},{3,1},{4,6},{5,7},{6,4},{7,5},{8,10},{9,11},{10,... | collective-permute-start | bytes 1769480 | tf_op jit(solution)/shard_map/ppermute | solution.py:608
  167.8 21.2 %collective-permute-start.45 = (bf16[768,384]{1,0:T(8,128)(2,1)S(1)}, bf16[768,384]{1,0:T(8,128)(2,1)S(1)}, u32[]{:S(2)}, u32[]{:S(2)}) collective-permute-start(bf16[768,384]{1,0:T(8,128)(2,1)S(1)} %copy-done.27), channel_id=1, source_target_pairs={{0,4},{4,0},{8,12},{12,8},{16,20},{20,16},{24,28},{28,24},{1,5},{5... | collective-permute-start | bytes 1769480 | tf_op jit(solution)/shard_map/ppermute | solution.py:608
  192.9 49.7 %collective-permute-start.51 = (bf16[2,256,768]{2,1,0:T(8,128)(2,1)S(1)}, bf16[2,256,768]{2,1,0:T(8,128)(2,1)S(1)}, u32[]{:S(2)}, u32[]{:S(2)}) collective-permute-start(bf16[2,256,768]{2,1,0:T(8,128)(2,1)S(1)} %add_convert_fusion.1), channel_id=1, source_target_pairs={{0,2},{1,3},{2,0},{3,1},{4,6},{5,7},{6,4},{7,5},{8,10},{9,11},{10,... | collective-permute-start | bytes 2359304 | tf_op jit(solution)/shard_map/ppermute | solution.py:608
  194.3 18.4 %collective-permute-start.53 = (bf16[4,96,640]{2,1,0:T(8,128)(2,1)}, bf16[4,96,640]{2,1,0:T(8,128)(2,1)}, u32[]{:S(2)}, u32[]{:S(2)}) collective-permute-start(bf16[4,96,640]{2,1,0:T(8,128)(2,1)} %get-tuple-element.215), channel_id=1, source_target_pairs={{0,4},{4,0},{8,12},{12,8},{16,20},{20,16},{24,28},{28,24},{1,5},{5... | collective-permute-start | bytes 1474568 | tf_op jit(solution)/shard_map/ppermute | solution.py:608
  196.3 46.7 %all-to-all-start = ((bf16[8,96,384]{2,1,0:T(8,128)(2,1)}), bf16[8,96,384]{2,1,0:T(8,128)(2,1)S(1)}, u32[]{:S(2)}, u32[]{:S(2)}) async-start(bf16[8,96,384]{2,1,0:T(8,128)(2,1)} %bitcast.15), calls=%async_computation | async-start | bytes 1179648 | tf_op jit(solution)/shard_map/all_to_all | solution.py:1010
  200.5 14.0 %collective-permute-start.49 = (bf16[320,768]{1,0:T(8,128)(2,1)}, bf16[320,768]{1,0:T(8,128)(2,1)S(1)}, u32[]{:S(2)}, u32[]{:S(2)}) collective-permute-start(bf16[320,768]{1,0:T(8,128)(2,1)} %get-tuple-element.211.d0_ref), channel_id=1, source_target_pairs={{0,1},{1,0},{2,3},{3,2},{4,5},{5,4},{6,7},{7,6},{8,9},{9,8},{10,11... | collective-permute-start | bytes 1474568 | tf_op jit(solution)/shard_map/ppermute | solution.py:608
  200.6 15.4 %collective-permute-start.50 = (bf16[320,768]{1,0:T(8,128)(2,1)}, bf16[320,768]{1,0:T(8,128)(2,1)S(1)}, u32[]{:S(2)}, u32[]{:S(2)}) collective-permute-start(bf16[320,768]{1,0:T(8,128)(2,1)} %copy-done.29), channel_id=1, source_target_pairs={{0,1},{1,0},{2,3},{3,2},{4,5},{5,4},{6,7},{7,6},{8,9},{9,8},{10,11... | collective-permute-start | bytes 1474568 | tf_op jit(solution)/shard_map/ppermute | solution.py:608
  201.1 26.5 %collective-permute-start.60 = (bf16[768,384]{1,0:T(8,128)(2,1)}, bf16[768,384]{1,0:T(8,128)(2,1)S(1)}, u32[]{:S(2)}, u32[]{:S(2)}) collective-permute-start(bf16[768,384]{1,0:T(8,128)(2,1)} %get-tuple-element.219), channel_id=1, source_target_pairs={{0,4},{4,0},{8,12},{12,8},{16,20},{20,16},{24,28},{28,24},{1,5},{5... | collective-permute-start | bytes 1769480 | tf_op jit(solution)/shard_map/ppermute | solution.py:608
  212.7 17.2 %collective-permute-start.61 = (bf16[768,384]{1,0:T(8,128)(2,1)S(1)}, bf16[768,384]{1,0:T(8,128)(2,1)S(1)}, u32[]{:S(2)}, u32[]{:S(2)}) collective-permute-start(bf16[768,384]{1,0:T(8,128)(2,1)S(1)} %add_convert_fusion.2), channel_id=1, source_target_pairs={{0,2},{1,3},{2,0},{3,1},{4,6},{5,7},{6,4},{7,5},{8,10},{9,11},{10,... | collective-permute-start | bytes 1769480 | tf_op jit(solution)/shard_map/ppermute | solution.py:608
  214.6 24.5 %collective-permute-start.62 = (bf16[384,768]{1,0:T(8,128)(2,1)}, bf16[384,768]{1,0:T(8,128)(2,1)S(1)}, u32[]{:S(2)}, u32[]{:S(2)}) collective-permute-start(bf16[384,768]{1,0:T(8,128)(2,1)} %get-tuple-element.224), channel_id=1, source_target_pairs={{0,4},{4,0},{8,12},{12,8},{16,20},{20,16},{24,28},{28,24},{1,5},{5... | collective-permute-start | bytes 1769480 | tf_op jit(solution)/shard_map/ppermute | solution.py:608
  216.8 23.5 %collective-permute-start.54 = (bf16[96,640]{1,0:T(8,128)(2,1)S(1)}, bf16[96,640]{1,0:T(8,128)(2,1)}, u32[]{:S(2)}, u32[]{:S(2)}) collective-permute-start(bf16[96,640]{1,0:T(8,128)(2,1)S(1)} %get-tuple-element.256), channel_id=1, source_target_pairs={{0,8},{4,12},{8,0},{12,4},{16,24},{20,28},{24,16},{28,20},{1,9},{5... | collective-permute-start | bytes 368648 | tf_op jit(solution)/shard_map/ppermute | solution.py:608
  227.6 12.7 %collective-permute-start.56 = (bf16[96,640]{1,0:T(8,128)(2,1)S(1)}, bf16[96,640]{1,0:T(8,128)(2,1)S(1)}, u32[]{:S(2)}, u32[]{:S(2)}) collective-permute-start(bf16[96,640]{1,0:T(8,128)(2,1)S(1)} %get-tuple-element.257), channel_id=1, source_target_pairs={{0,24},{4,28},{8,16},{12,20},{16,8},{20,12},{24,0},{28,4},{1,25},{... | collective-permute-start | bytes 368648 | tf_op jit(solution)/shard_map/ppermute | solution.py:608
  229.9 10.4 %collective-permute-start.55 = (bf16[96,640]{1,0:T(8,128)(2,1)S(1)}, bf16[96,640]{1,0:T(8,128)(2,1)S(1)}, u32[]{:S(2)}, u32[]{:S(2)}) collective-permute-start(bf16[96,640]{1,0:T(8,128)(2,1)S(1)} %get-tuple-element.258), channel_id=1, source_target_pairs={{0,16},{4,20},{8,24},{12,28},{16,0},{20,4},{24,8},{28,12},{1,17},{... | collective-permute-start | bytes 368648 | tf_op jit(solution)/shard_map/ppermute | solution.py:608
  242.9 7.8 %collective-permute-start.52 = (bf16[2,256,768]{2,1,0:T(8,128)(2,1)S(1)}, bf16[2,256,768]{2,1,0:T(8,128)(2,1)S(1)}, u32[]{:S(2)}, u32[]{:S(2)}) collective-permute-start(bf16[2,256,768]{2,1,0:T(8,128)(2,1)S(1)} %add_convert_fusion.own_ref), channel_id=1, source_target_pairs={{0,1},{1,0},{2,3},{3,2},{4,5},{5,4},{6,7},{7,6},{8,9},{9,8},{10,11... | collective-permute-start | bytes 2359304 | tf_op jit(solution)/shard_map/ppermute | solution.py:608
  (81 other events, 545.4 us)
where the time goes:
time: 259 us; the launch traced here: 256 us
  Pallas kernels  111 us (43%)
  starting transfers between devices  63.8 us (25%)
  waiting for transfers between devices  54.5 us (21%)
  local copies, waits for them, and re-layouts  14.7 us (6%)
  other arithmetic  9.98 us (4%)
    pallas_call x16, Pallas kernels, call(): pl.pallas_call(kernel, name=name, out_shape=list(outs), in_specs=in_specs...  111 us
    ppermute x49, waiting for transfers between devices, swap(): return lax.ppermute(x, axis, [(i, i ^ bit) for i in range(size)])  49.7 us
    ppermute x49, starting transfers between devices, swap(): return lax.ppermute(x, axis, [(i, i ^ bit) for i in range(size)])  45.1 us
    unnamed x132, local copies, waits for them, and re-layouts  9.96 us
    ppermute x6, starting transfers between devices, gather_rows(): down[n] = lax.ppermute(down[n], 'gx', back)  6.86 us
    ppermute x6, starting transfers between devices, gather_rows(): up[n] = lax.ppermute(up[n], 'gx', ahead)  5.2 us
  transfers between devices with their start and end apart: 64, of which 17 were waited for; matrix products, arithmetic and copies ran while one was open for 6% of the time, Pallas kernels for 37%

commit v1 on v0

--- a/solution.py
+++ b/solution.py
@@ -73,22 +73,20 @@
 
 def pack_kernel(q_ref, k_ref, v_ref, o_ref, attn_ref, moe_ref, router_ref, qkv_ref, extras_ref):
     qkv_ref[...] = jnp.concatenate([q_ref[...], k_ref[...], v_ref[...]], axis=1)
-    rows, experts = router_ref.shape
-    blank = jnp.zeros((1, LANES - rows), F32)
-    row = lax.broadcasted_iota(jnp.int32, (LANES, LANES), 0)
-    first = jnp.concatenate([attn_ref[...].astype(F32), blank], axis=1)
-    second = jnp.concatenate([moe_ref[...].astype(F32), blank], axis=1)
-    gains = jnp.where(row == 0, first, jnp.where(row == 1, second, 0.0))
-    gains = jnp.transpose(gains)[:rows]
-    route = jnp.concatenate(
+    experts, rows = router_ref.shape
+    lines = jnp.concatenate(
         [
-            jnp.zeros((rows, 2), F32),
+            attn_ref[...].astype(F32),
+            moe_ref[...].astype(F32),
             router_ref[...].astype(F32),
-            jnp.zeros((rows, LANES - 2 - experts), F32),
+            jnp.zeros((LANES - 2 - experts, rows), F32),
         ],
-        axis=1,
-    )
-    extras_ref[...] = jnp.concatenate([(gains + route).astype(BF), o_ref[...]], axis=1)
+        axis=0,
+    )
+    lines = jnp.concatenate([lines, jnp.zeros((LANES, LANES - rows), F32)], axis=1)
+    extras_ref[...] = jnp.concatenate(
+        [jnp.transpose(lines)[:rows].astype(BF), o_ref[...]], axis=1
+    )
 
 
 def lane_prefix(values):
@@ -603,6 +601,21 @@
         out_ref[rows, :] = g_ref[rows, :].astype(F32) + source[j // 2].astype(F32)
 
 
+def close_kernel(experts, small_ref, line_ref, project_ref, *outs):
+    first_ref, second_ref, route_ref, out_ref = outs
+    rows, spare = small_ref.shape
+    width = out_ref.shape[1]
+    line = line_ref[...]
+    out_ref[...] = project_ref[...][:, :width] + line[:, spare:]
+    small = small_ref[...] + line[:, :spare]
+    small = jnp.concatenate([small, jnp.zeros((rows, LANES - spare), F32)], axis=1)
+    small = jnp.concatenate([small, jnp.zeros((LANES - rows, LANES), F32)], axis=0)
+    small = jnp.transpose(small)[:, :rows]
+    first_ref[...] = small[0:1]
+    second_ref[...] = small[1:2]
+    route_ref[...] = small[2 : 2 + experts]
+
+
 def swap(x, axis, bit):
     size = lax.axis_size(axis)
     return lax.ppermute(x, axis, [(i, i ^ bit) for i in range(size)])
@@ -643,17 +656,14 @@
     return [jnp.concatenate(spread(cut, experts), axis=0)]
 
 
-def sum_rows(parts):
+def sum_begin(parts, *fill):
     if len(parts) == 1:
         size = lax.axis_size("gx")
         arrived = lax.all_to_all(parts[0], "gx", split_axis=0, concat_axis=0, tiled=True)
         arrived = arrived.reshape(size, parts[0].shape[0] // size, parts[0].shape[1])
-        return arrived.astype(F32).sum(axis=0)
-    pair = add(parts[0], swap(parts[1], "gx", 1))
-    total = pair[0]
-    for n in range(1, pair.shape[0]):
-        total = total + swap(pair[n].astype(BF), "gx", 2 * n).astype(F32)
-    return total
+        return [arrived.astype(F32).sum(axis=0)], fill[0]
+    pair = add(parts[0], after(swap(parts[1], "gx", 1), *fill)).astype(BF)
+    return [pair[0]] + [swap(pair[n], "gx", 2 * n) for n in range(1, pair.shape[0])], pair
 
 
 def sum_all(x, axis):
@@ -720,12 +730,13 @@
             w_output,
             attn_gain.reshape(1, shard),
             moe_gain.reshape(1, shard),
-            router,
+            router.T,
         ),
         cost=1,
     )
     half_model = model // 2
-    pack = jnp.concatenate([w_in[0], w_out[0][:, :half_model], w_out[0][:, half_model:]], axis=0)
+    rear = after(w_out, qkv_w)[0]
+    pack = jnp.concatenate([w_in[0], rear[:, :half_model], rear[:, half_model:]], axis=0)
     pack_x = swap(pack, "gy", 2)
 
     pos_row, pos_col, info = call(
@@ -955,12 +966,16 @@
         (*rows_in, after(grad_pre, mixed_grads[0]), in_arrived),
         cost=1,
     )
+    grads_mixed[1:] = lax.optimization_barrier((*grads_mixed[1:], in_mine))[:-1]
     in_far_y = swap(in_far_y, "gx", 1)
     out_sum_x = add(out_by_x, after(out_far_y, in_mine)).astype(BF)
-    grads_mixed[0], in_by_x, out_sum_x = lax.optimization_barrier(
-        (grads_mixed[0], in_by_x, out_sum_x)
-    )
+    projected = add(after(project_keep, in_mine), project_other).astype(BF)
+    grads_mixed[0], in_by_x, out_sum_x, projected = lax.optimization_barrier(
+        (grads_mixed[0], in_by_x, out_sum_x, projected)
+    )
+    projected = lax.all_to_all(projected, "gx", split_axis=0, concat_axis=0, tiled=True)
     out_from_x = swap(out_sum_x, "gy", 2)
+    out_from_y = swap(out_by_y, "gx", 1)
     d1_x = swap(after(d1, *grads_mixed[1:]), "gy", 2)
     spare = -(-3 * width // LANES) * LANES - 3 * width
     count = 2 if n_gx == len(RING) and heads * bucket_count == shard else 1
@@ -997,51 +1012,65 @@
         ],
         cost=60,
     )
-    keep, send, in_far_y, out_from_x, d1_x = lax.optimization_barrier(
-        (keep, send, in_far_y, out_from_x, d1_x)
+    keep, send, in_far_y, out_from_x, out_from_y, d1_x, projected, *dw = lax.optimization_barrier(
+        (keep, send, in_far_y, out_from_x, out_from_y, d1_x, projected, *dw)
     )
     half = add(keep, swap(send, "gy", 1)).astype(BF)
-    half, out_by_y, d1, d1_x, project_keep, *dw = lax.optimization_barrier(
-        (half, out_by_y, d1, d1_x, project_keep, *dw)
-    )
-    out_from_y = swap(out_by_y, "gx", 1)
-    d1s = [d1, swap(d1, "gy", 1), d1_x, swap(d1_x, "gy", 1)]
-    projected = add(project_keep, project_other).astype(BF)
-    projected = lax.all_to_all(projected, "gx", split_axis=0, concat_axis=0, tiled=True)
-    total = add(half, swap(half, "gy", 2)[::-1]).astype(BF)
-    other = swap(total, "gy", 1)
-    summed = sum_rows(dw)
-    projected = projected.reshape(n_gx, shard, 2 * width).astype(F32).sum(axis=0)
-    small = summed[:, 3 * width :]
-    small = small + swap(small, "gy", 1)
-    line = swap(jnp.concatenate([small, projected[:, width:]], axis=1), "gy", 2)
-    small = small + line[:, :spare]
-    grad_out_proj = projected[:, :width] + line[:, spare:]
-    if count == 1:
-        grad_table = sum_all(table, "gx")[:, :heads].T
-    else:
-        grad_table = summed[:, -1].reshape(heads, bucket_count)
+    half, d1, d1_x, in_by_x = lax.optimization_barrier((half, d1, d1_x, in_by_x))
+    half_far = swap(half, "gy", 2)
+    in_sum_x = add(in_by_x, in_far_y).astype(BF)
+    in_from_x = swap(in_sum_x, "gy", 2)
+    d1s = [after(d1, in_sum_x), swap(d1, "gy", 1), d1_x, swap(d1_x, "gy", 1)]
     (layer_output,) = call(
         unsort_kernel,
         "unsort",
         [struct((seq, model), F32)],
         [SM] + [VM] * 6,
         (gy, pos_col, layer_input, *d1s),
-        cost=7,
-    )
+        cost=1,
+    )
+    projected = projected.reshape(n_gx, shard, 2 * width).astype(F32).sum(axis=0)
+    sums, dw_done = sum_begin(dw, layer_output)
+    in_from_y = swap(after(in_by_y, dw_done), "gx", 1)
+    half_far, *sums = lax.optimization_barrier((half_far, layer_output, *sums))
+    sums = sums[1:]
+    total = add(half, half_far[::-1]).astype(BF)
+    other = swap(total, "gy", 1)
     (grad_input,) = call(
         finish_kernel,
         "finish",
         [struct((seq, model), F32)],
         [SM] + [VM] * 3,
         (gy, total, other, grad_out),
-        cost=4,
-    )
-    in_sum_x = add(after(in_by_x, half), in_far_y).astype(BF)
-    in_from_x = swap(in_sum_x, "gy", 2)
-    in_from_y = swap(after(in_by_y, half), "gx", 1)
+        cost=1,
+    )
+    summed = sums[0].astype(F32)
+    for part in sums[1:]:
+        summed = summed + part.astype(F32)
+    small = summed[:, 3 * width :]
+    small = small + swap(small, "gy", 1)
+    line = swap(jnp.concatenate([small, projected[:, width:]], axis=1), "gy", 2)
+    line = after(line, grad_input)
+    grad_first, grad_second, grad_route, grad_out_proj = call(
+        partial(close_kernel, experts),
+        "close",
+        [
+            struct((1, shard), F32),
+            struct((1, shard), F32),
+            struct((experts, shard), F32),
+            struct((shard, width), F32),
+        ],
+        [VM] * 3,
+        (small, line, projected),
+        cost=1,
+    )
     grad_w_out = add(add(out_mine, out_from_y), out_from_x)
+    in_from_x, in_from_y = lax.optimization_barrier((in_from_x, in_from_y, grad_input))[:2]
     grad_w_in = add(add(in_mine, in_from_y), in_from_x)
+    if count == 1:
+        grad_table = sum_all(table, "gx")[:, :heads].T
+    else:
+        grad_table = summed[:, -1].reshape(heads, bucket_count)
 
     return (
         layer_output,
@@ -1050,9 +1079,9 @@
         summed[:, width : 2 * width],
         summed[:, 2 * width : 3 * width],
         grad_out_proj,
-        small[:, 0],
-        small[:, 1],
-        small[:, 2 : 2 + experts],
+        grad_first.reshape(shard),
+        grad_second.reshape(shard),
+        grad_route.T,
         grad_table,
         grad_w_in[None],
         grad_w_out[None],

time: 259 us -> 239 us (0.923)
  waiting for transfers between devices: 54.5 us -> 33.7 us
  starting transfers between devices: 63.8 us -> 66.8 us
  other arithmetic: 9.98 us -> 7.31 us
    ppermute x49, waiting for transfers between devices: 49.7 us -> 29.3 us  [swap(): return lax.ppermute(x, axis, [(i, i ^ bit) for i in range(size)])]
    ppermute x49, starting transfers between devices: 45.1 us -> 47.8 us  [swap(): return lax.ppermute(x, axis, [(i, i ^ bit) for i in range(size)])]
    pallas_call x16 -> x17, Pallas kernels: 111 us -> 113 us  [call(): pl.pallas_call(kernel, name=name, out_shape=list(outs), in_specs=in_specs...]
    unnamed x132 -> x138, local copies, waits for them, and re-layouts: 9.96 us -> 10.7 us
  transfers between devices with their start and end apart: 64 -> 64, of which waited for: 17 -> 18; matrix products, arithmetic and copies ran while one was open for 6% -> 3% of each run, Pallas kernels for 37% -> 41%
where the time goes in v1:
time: 239 us; the launch traced here: 236 us
  Pallas kernels  113 us (47%)
  starting transfers between devices  66.8 us (28%)
  waiting for transfers between devices  33.7 us (14%)
  local copies, waits for them, and re-layouts  13.5 us (6%)
  other arithmetic  7.31 us (3%)
    pallas_call x17, Pallas kernels, call(): pl.pallas_call(kernel, name=name, out_shape=list(outs), in_specs=in_specs...  113 us
    ppermute x49, starting transfers between devices, swap(): return lax.ppermute(x, axis, [(i, i ^ bit) for i in range(size)])  47.8 us
    ppermute x49, waiting for transfers between devices, swap(): return lax.ppermute(x, axis, [(i, i ^ bit) for i in range(size)])  29.3 us
    unnamed x138, local copies, waits for them, and re-layouts  10.7 us
    ppermute x6, starting transfers between devices, gather_rows(): up[n] = lax.ppermute(up[n], 'gx', ahead)  6.04 us
    ppermute x6, starting transfers between devices, gather_rows(): down[n] = lax.ppermute(down[n], 'gx', back)  6.02 us
  transfers between devices with their start and end apart: 64, of which 18 were waited for; matrix products, arithmetic and copies ran while one was open for 3% of the time, Pallas kernels for 41%

profile of v1, /device:TPU:0, one launch (start us, length us, event | category | flops | bytes accessed | tf_op | source)
XLA Modules:
  0.0 236.1 jit_solution(17771153960444775895)
XLA Ops:
  0.7 1.7 pack.1
  3.6 3.0 %collective-permute-start.7 = (bf16[1536,384]{1,0:T(8,128)(2,1)S(1)}, bf16[1536,384]{1,0:T(8,128)(2,1)S(1)}, u32[]{:S(2)}, u32[]{:S(2)}) collective-permute-start(bf16[1536,384]{1,0:T(8,128)(2,1)S(1)} %pad_maximum_fusion.refs_4_.refs_6_), channel_id=1, source_target_pairs={{0,2},{1,3},{2,0},{3,1},{4,6},{5,7},{6,4},{7,5},{8,10},{9,11},{10,... | collective-permute-start | bytes 3538952 | tf_op jit(solution)/shard_map/ppermute | solution.py:621
  6.6 1.5 collective-permute-start.1
  8.6 1.5 collective-permute-start.9
  10.6 2.1 place.1
  13.2 1.5 collective-permute-start.2
  16.8 1.5 collective-permute-done.2.refs_4_
  24.8 2.3 collective-permute-done.5.refs_7_
  28.0 1.5 collective-permute-start.14
  30.2 2.1 unpack.1
  35.1 13.6 %attend.1 = (bf16[1024,768]{1,0:T(8,128)(2,1)}, bf16[1024,576]{1,0:T(8,128)(2,1)}, bf16[30,256,256]{2,1,0:T(8,128)(2,1)}, bf16[1024,192]{1,0:T(8,128)(2,1)}, bf1...) custom-call(s32[1]{0:T(128)} %bitcast.refs_0_.gy_ref, ...), custom_call_target="tpu_custom_call" | custom-call | flops 69000003584 | bytes 1 | tf_op jit(solution)/shard_map/attend/pallas_call | solution.py:46
  49.0 1.5 collective-permute-start.18
  51.1 4.3 %presort.1 = (bf16[320,768]{1,0:T(8,128)(2,1)}, bf16[320,768]{1,0:T(8,128)(2,1)}, f32[320,128]{1,0:T(8,128)}) custom-call(s32[1]{0:T(128)} %bitcast.refs_0_.gy_ref, s32[1,1024]{1,0:T(1,128)} %get-tuple-element.157.refs_7_.pos_ref, bf16[1024,768]{1,0:T(8,128)(2,1)} %x_ref.3, bf16[1024,768]{1,0:T(8,128)(2,1)} %g_ref.3, ...), custom_call_target="tpu_custom_call" | custom-call | flops 5750000128 | bytes 1 | tf_op jit(solution)/shard_map/presort/pallas_call | solution.py:46
  56.4 2.1 collective-permute-done.19.refs_3_.refs_16_
  59.4 4.8 %route.1 = (bf16[80,768]{1,0:T(8,128)(2,1)}, bf16[80,768]{1,0:T(8,128)(2,1)}, bf16[80,768]{1,0:T(8,128)(2,1)}, bf16[80,768]{1,0:T(8,128)(2,1)}, bf16[80,768]{1,0...) custom-call(bf16[320,192]{1,0:T(8,128)(2,1)} %get-tuple-element.151., ...), custom_call_target="tpu_custom_call" | custom-call | flops 5750000128 | bytes 1 | tf_op jit(solution)/shard_map/route/pallas_call | solution.py:46
  64.1 1.6 collective-permute-start.23
  65.8 2.6 %collective-permute-start.24 = (bf16[80,768]{1,0:T(8,128)(2,1)}, bf16[80,768]{1,0:T(8,128)(2,1)S(1)}, u32[]{:S(2)}, u32[]{:S(2)}) collective-permute-start(bf16[80,768]{1,0:T(8,128)(2,1)} %get-tuple-element.168.refs_25_), channel_id=1, source_target_pairs={{0,16},{4,20},{8,24},{12,28},{16,0},{20,4},{24,8},{28,12},{1,17},{... | collective-permute-start | bytes 368648 | tf_op jit(solution)/shard_map/ppermute | solution.py:621
  68.6 4.1 %collective-permute-done.23.refs_1_.refs_8_ = bf16[80,768]{1,0:T(8,128)(2,1)S(1)} collective-permute-done((bf16[80,768]{1,0:T(8,128)(2,1)}, bf16[80,768]{1,0:T(8,128)(2,1)S(1)}, u32[]{:S(2)}, u32[]{:S(2)}) %collective-permute-start.23) | collective-permute-done | bytes 122912 | tf_op jit(solution)/shard_map/ppermute | solution.py:621
  72.7 5.6 %collective-permute-done.24.refs_2_.refs_9_ = bf16[80,768]{1,0:T(8,128)(2,1)S(1)} collective-permute-done((bf16[80,768]{1,0:T(8,128)(2,1)}, bf16[80,768]{1,0:T(8,128)(2,1)S(1)}, u32[]{:S(2)}, u32[]{:S(2)}) %collective-permute-start.24) | collective-permute-done | bytes 122912 | tf_op jit(solution)/shard_map/ppermute | solution.py:621
  78.3 2.7 %collective-permute-start.26 = (bf16[80,768]{1,0:T(8,128)(2,1)}, bf16[80,768]{1,0:T(8,128)(2,1)S(1)}, u32[]{:S(2)}, u32[]{:S(2)}) collective-permute-start(bf16[80,768]{1,0:T(8,128)(2,1)} %get-tuple-element.171), channel_id=1, source_target_pairs={{0,8},{4,12},{8,0},{12,4},{16,24},{20,28},{24,16},{28,20},{1,9},{5... | collective-permute-start | bytes 368648 | tf_op jit(solution)/shard_map/ppermute | solution.py:621
  82.1 1.5 collective-permute-start.28
  83.6 7.8 %expert_near.1 = (f32[320,768]{1,0:T(8,128)}, bf16[4,320,384]{2,1,0:T(8,128)(2,1)}, bf16[4,320,384]{2,1,0:T(8,128)(2,1)}) custom-call(bf16[80,768]{1,0:T(8,128)(2,1)} %get-tuple-element.166.refs_0_.refs_7_.refs_23_, bf16[80,768]{1,0:T(8,128)(2,1)} %copy-done.19, bf16[80,768]{1,0:T(8,128)(2,1)} %copy-done.20, bf16[80,768]{1,0:T(8,128)(2,1)} %copy-done.21, ...), custom_call_target="tpu_custom_call" | custom-call | flops 8049999872 | bytes 1 | tf_op jit(solution)/shard_map/expert_near/pallas_call | solution.py:46
  91.4 2.0 collective-permute-done.27.refs_2_
  93.5 2.8 %collective-permute-done.32.refs_8_.refs_13_ = bf16[1536,384]{1,0:T(8,128)(2,1)S(1)} collective-permute-done((bf16[1536,384]{1,0:T(8,128)(2,1)S(1)}, bf16[1536,384]{1,0:T(8,128)(2,1)S(1)}, u32[]{:S(2)}, u32[]{:S(2)}) %collective-permute-start.32) | collective-permute-done | bytes 1179680 | tf_op jit(solution)/shard_map/ppermute | solution.py:621
  97.4 7.5 %expert_far.1 = (bf16[80,768]{1,0:T(8,128)(2,1)}, bf16[80,768]{1,0:T(8,128)(2,1)}, bf16[80,768]{1,0:T(8,128)(2,1)}, bf16[80,768]{1,0:T(8,128)(2,1)}, bf16[4,320,...) custom-call(bf16[80,768]{1,0:T(8,128)(2,1)} %get-tuple-element.166.refs_0_.refs_7_.refs_23_, bf16[80,768]{1,0:T(8,128)(2,1)} %copy-done.19, ...), custom_call_target="tpu_custom_call" | custom-call | flops 8625000448 | bytes 1 | tf_op jit(solution)/shard_map/expert_far/pallas_call | solution.py:46
  104.9 4.6 %outer_out_sent.1 = bf16[4,384,768]{2,1,0:T(8,128)(2,1)} custom-call(bf16[80,768]{1,0:T(8,128)(2,1)} %get-tuple-element.170.refs_0_, bf16[80,768]{1,0:T(8,128)(2,1)} %copy-done.44, bf16[80,768]{1,0:T(8,128)(2,1)} %copy-done.45, bf16[80,768]{1,0:T(8,128)(2,1)} %copy-done.47, bf16[4,320,384]{2,1,0:T(8,128)(2,1)} %get-tuple-element.184.refs_4_, ...), custom_call_target="tpu_custom_call" | custom-call | flops 5405000192 | bytes 1 | tf_op jit(solution)/shard_map/outer_out_sent/pallas_call | solution.py:46
  109.7 1.8 collective-permute-start.37
  112.6 1.5 collective-permute-start.39
  114.1 12.3 %expert_back.1 = (bf16[80,768]{1,0:T(8,128)(2,1)}, bf16[80,768]{1,0:T(8,128)(2,1)}, bf16[80,768]{1,0:T(8,128)(2,1)}, bf16[80,768]{1,0:T(8,128)(2,1)}, bf16[8,320,384]{2,1,0:T(8,128)(2,1)}) custom-call(bf16[80,768]{1,0:T(8,128)(2,1)} %get-tuple-element.170.refs_0_, bf16[80,768]{1,0:T(8,128)(2,1)} %copy-done.44, bf16[80,768]{1,0:T(8,128)(2,1)} %copy-done.45, ...), custom_call_target="tpu_custom_call" | custom-call | flops 13799999488 | bytes 1 | tf_op jit(solution)/shard_map/expert_back/pallas_call | solution.py:46
  127.4 2.0 collective-permute-start.34
  129.4 1.5 collective-permute-start.35
  132.3 9.0 %fill_rows.1 = (f32[384,768]{1,0:T(8,128)}, bf16[384,768]{1,0:T(8,128)(2,1)}, bf16[384,768]{1,0:T(8,128)(2,1)}, bf16[384,768]{1,0:T(8,128)(2,1)}, bf16[4,768,384...) custom-call(bf16[80,768]{1,0:T(8,128)(2,1)} %get-tuple-element.170.refs_0_, ...), custom_call_target="tpu_custom_call" | custom-call | flops 14949999616 | bytes 1 | tf_op jit(solution)/shard_map/fill_rows/pallas_call | solution.py:46
  143.2 5.3 %combine.1 = (bf16[320,192]{1,0:T(8,128)(2,1)}, bf16[320,192]{1,0:T(8,128)(2,1)}, bf16[320,192]{1,0:T(8,128)(2,1)}, bf16[320,192]{1,0:T(8,128)(2,1)}, bf16[320,7...) custom-call(bf16[80,768]{1,0:T(8,128)(2,1)} %get-tuple-element.187.refs_0_, ...), custom_call_target="tpu_custom_call" | custom-call | flops 46000001024 | bytes 1 | tf_op jit(solution)/shard_map/combine/pallas_call | solution.py:46
  151.5 5.1 %outer_in_held.1 = (f32[768,384]{1,0:T(8,128)}, bf16[768,384]{1,0:T(8,128)(2,1)}, bf16[768,384]{1,0:T(8,128)(2,1)}, bf16[768,384]{1,0:T(8,128)(2,1)}) custom-call(bf16[80,768]{1,0:T(8,128)(2,1)} %get-tuple-element.166.refs_0_.refs_7_.refs_23_, bf16[80,768]{1,0:T(8,128)(2,1)} %copy-done.19, bf16[80,768]{1,0:T(8,128)(2,1)} %copy-done.20, ...), custom_call_target="tpu_custom_call" | custom-call | flops 1150000000 | bytes 1 | tf_op jit(solution)/shard_map/outer_in_held/pallas_call | solution.py:46
  160.6 4.2 %all-to-all-start = ((bf16[8,96,384]{2,1,0:T(8,128)(2,1)}), bf16[8,96,384]{2,1,0:T(8,128)(2,1)S(1)}, u32[]{:S(2)}, u32[]{:S(2)}) async-start(bf16[8,96,384]{2,1,0:T(8,128)(2,1)} %bitcast.12), calls=%async_computation | async-start | bytes 1179648 | tf_op jit(solution)/shard_map/all_to_all | solution.py:976
  164.8 1.5 collective-permute-start.49
  166.9 2.0 collective-permute-start.46
  168.9 20.2 %attend_back.1 = (bf16[4,96,640]{2,1,0:T(8,128)(2,1)}, bf16[4,96,640]{2,1,0:T(8,128)(2,1)}, bf16[2,256,768]{2,1,0:T(8,128)(2,1)}, bf16[2,256,768]{2,1,0:T(8,128)(2,1)}, f32[32,8]{1,0:T(8,128)}) custom-call(s32[1]{0:T(128)} %bitcast.refs_0_.gy_ref, s32[1]{0:T(128)} %bitcast.1.gx_ref.refs_0_.refs_1_, bf16[320,192]{1,0:T(8,128)(2,1)} %get-tuple-element.212.refs_2_, ...), custom_call_target="tpu_custom_call" | custom-call | flops 69000003584 | bytes 1 | tf_op jit(solution)/shard_map/attend_back/pallas_call | solution.py:46
  189.2 1.5 collective-permute-done.47
  191.3 1.4 collective-permute-start.54
  199.5 7.2 %unsort.1 = f32[1024,768]{1,0:T(8,128)} custom-call(s32[1]{0:T(128)} %bitcast.refs_0_.gy_ref, s32[1024,1]{1,0:T(8,128)} %get-tuple-element.141.refs_6_.pos_ref, bf16[1024,768]{1,0:T(8,128)(2,1)} %x_ref.3, bf16[320,768]{1,0:T(8,128)(2,1)} %get-tuple-element.242.d0_ref, bf16[320,768]{1,0:T(8,128)(2,1)} %copy-done.14, bf16[320,768]{1,0:T(8,128)(2,1)} %copy-done.12, ...), custom_call_target="tpu_custom_call" | custom-call | flops 1150000000 | bytes 1 | tf_op jit(solution)/shard_map/unsort/pallas_call | solution.py:46
  207.0 3.6 %collective-permute-start.57 = (bf16[96,640]{1,0:T(8,128)(2,1)S(1)}, bf16[96,640]{1,0:T(8,128)(2,1)S(1)}, u32[]{:S(2)}, u32[]{:S(2)}) collective-permute-start(bf16[96,640]{1,0:T(8,128)(2,1)S(1)} %get-tuple-element.268), channel_id=1, source_target_pairs={{0,24},{4,28},{8,16},{12,20},{16,8},{20,12},{24,0},{28,4},{1,25},{... | collective-permute-start | bytes 368648 | tf_op jit(solution)/shard_map/ppermute | solution.py:621
  212.8 2.3 collective-permute-done.57
  215.1 1.7 collective-permute-start.62
  216.8 4.4 %collective-permute-done.56 = bf16[96,640]{1,0:T(8,128)(2,1)S(1)} collective-permute-done((bf16[96,640]{1,0:T(8,128)(2,1)S(1)}, bf16[96,640]{1,0:T(8,128)(2,1)S(1)}, u32[]{:S(2)}, u32[]{:S(2)}) %collective-permute-start.56) | collective-permute-done | bytes 122912 | tf_op jit(solution)/shard_map/ppermute | solution.py:621
  225.5 3.9 %finish.1 = f32[1024,768]{1,0:T(8,128)} custom-call(s32[1]{0:T(128)} %bitcast.refs_0_.gy_ref, bf16[2,256,768]{2,1,0:T(8,128)(2,1)} %copy-done, bf16[2,256,768]{2,1,0:T(8,128)(2,1)} %copy-done.5, bf16[1024,768]{1,0:T(8,128)(2,1)} %g_ref.3), custom_call_target="tpu_custom_call" | custom-call | flops 1150000000 | bytes 1 | tf_op jit(solution)/shard_map/finish/pallas_call | solution.py:46
  231.9 1.7 close.1
  233.6 2.2 add_bitcast_fusion.1
  (263 shorter events, 50.1 us)
Async XLA Ops:
  3.6 29.7 %collective-permute-start.7 = (bf16[1536,384]{1,0:T(8,128)(2,1)S(1)}, bf16[1536,384]{1,0:T(8,128)(2,1)S(1)}, u32[]{:S(2)}, u32[]{:S(2)}) collective-permute-start(bf16[1536,384]{1,0:T(8,128)(2,1)S(1)} %pad_maximum_fusion.refs_4_.refs_6_), channel_id=1, source_target_pairs={{0,2},{1,3},{2,0},{3,1},{4,6},{5,7},{6,4},{7,5},{8,10},{9,11},{10,... | collective-permute-start | bytes 3538952 | tf_op jit(solution)/shard_map/ppermute | solution.py:621
  6.6 8.2 %collective-permute-start.1 = (bf16[96,320]{1,0:T(8,128)(2,1)S(1)}, bf16[96,320]{1,0:T(8,128)(2,1)S(1)}, u32[]{:S(2)}, u32[]{:S(2)}) collective-permute-start(bf16[96,320]{1,0:T(8,128)(2,1)S(1)} %copy-done.61), channel_id=1, source_target_pairs={{8,0},{16,8},{24,16},{28,24},{20,28},{12,20},{4,12},{0,4},{9,1},{1... | collective-permute-start | bytes 184328 | tf_op jit(solution)/shard_map/ppermute | solution.py:644
  8.6 12.1 %collective-permute-start.9 = (bf16[96,576]{1,0:T(8,128)(2,1)S(1)}, bf16[96,576]{1,0:T(8,128)(2,1)S(1)}, u32[]{:S(2)}, u32[]{:S(2)}) collective-permute-start(bf16[96,576]{1,0:T(8,128)(2,1)S(1)} %copy-done.41), channel_id=1, source_target_pairs={{8,0},{16,8},{24,16},{28,24},{20,28},{12,20},{4,12},{0,4},{9,1},{1... | collective-permute-start | bytes 331784 | tf_op jit(solution)/shard_map/ppermute | solution.py:644
  14.8 8.0 %collective-permute-start.3 = (bf16[96,320]{1,0:T(8,128)(2,1)S(1)}, bf16[96,320]{1,0:T(8,128)(2,1)S(1)}, u32[]{:S(2)}, u32[]{:S(2)}) collective-permute-start(bf16[96,320]{1,0:T(8,128)(2,1)S(1)} %collective-permute-done.1.refs_3_), channel_id=1, source_target_pairs={{8,0},{16,8},{24,16},{28,24},{20,28},{12,20},{4,12},{0,4},{9,1},{1... | collective-permute-start | bytes 184328 | tf_op jit(solution)/shard_map/ppermute | solution.py:644
  21.5 6.5 %collective-permute-start.12 = (bf16[96,576]{1,0:T(8,128)(2,1)S(1)}, bf16[96,576]{1,0:T(8,128)(2,1)}, u32[]{:S(2)}, u32[]{:S(2)}) collective-permute-start(bf16[96,576]{1,0:T(8,128)(2,1)S(1)} %collective-permute-done.10.refs_11_), channel_id=1, source_target_pairs={{0,8},{8,16},{16,24},{24,28},{28,20},{20,12},{12,4},{4,0},{1,9},{9... | collective-permute-start | bytes 331784 | tf_op jit(solution)/shard_map/ppermute | solution.py:643
  27.2 23.3 %collective-permute-start.15 = (bf16[1536,384]{1,0:T(8,128)(2,1)S(1)}, bf16[1536,384]{1,0:T(8,128)(2,1)S(1)}, u32[]{:S(2)}, u32[]{:S(2)}) collective-permute-start(bf16[1536,384]{1,0:T(8,128)(2,1)S(1)} %pad_maximum_fusion.refs_4_.refs_6_), channel_id=1, source_target_pairs={{0,1},{1,0},{2,3},{3,2},{4,5},{5,4},{6,7},{7,6},{8,9},{9,8},{10,11... | collective-permute-start | bytes 3538952 | tf_op jit(solution)/shard_map/ppermute | solution.py:621
  32.3 16.4 %collective-permute-start.21 = (bf16[768,192]{1,0:T(8,128)(2,1)}, bf16[768,192]{1,0:T(8,128)(2,1)S(1)}, u32[]{:S(2)}, u32[]{:S(2)}) collective-permute-start(bf16[768,192]{1,0:T(8,128)(2,1)} %get-tuple-element.155.refs_4_.refs_9_), channel_id=1, source_target_pairs={{0,2},{1,3},{2,0},{3,1},{4,6},{5,7},{6,4},{7,5},{8,10},{9,11},{10,... | collective-permute-start | bytes 884744 | tf_op jit(solution)/shard_map/ppermute | solution.py:621
  33.3 15.7 %collective-permute-start.20 = (bf16[768,192]{1,0:T(8,128)(2,1)}, bf16[768,192]{1,0:T(8,128)(2,1)S(1)}, u32[]{:S(2)}, u32[]{:S(2)}) collective-permute-start(bf16[768,192]{1,0:T(8,128)(2,1)} %get-tuple-element.155.refs_4_.refs_9_), channel_id=1, source_target_pairs={{0,1},{1,0},{2,3},{3,2},{4,5},{5,4},{6,7},{7,6},{8,9},{9,8},{10,11... | collective-permute-start | bytes 884744 | tf_op jit(solution)/shard_map/ppermute | solution.py:621
  33.3 35.3 %collective-permute-start.30 = (bf16[1536,384]{1,0:T(8,128)(2,1)S(1)}, bf16[1536,384]{1,0:T(8,128)(2,1)S(1)}, u32[]{:S(2)}, u32[]{:S(2)}) collective-permute-start(bf16[1536,384]{1,0:T(8,128)(2,1)S(1)} %pad_maximum_fusion.refs_4_.refs_6_), channel_id=1, source_target_pairs={{0,4},{4,0},{8,12},{12,8},{16,20},{20,16},{24,28},{28,24},{1,5},{5... | collective-permute-start | bytes 3538952 | tf_op jit(solution)/shard_map/ppermute | solution.py:621
  34.4 16.2 %collective-permute-start.16 = (bf16[1536,384]{1,0:T(8,128)(2,1)S(1)}, bf16[1536,384]{1,0:T(8,128)(2,1)S(1)}, u32[]{:S(2)}, u32[]{:S(2)}) collective-permute-start(bf16[1536,384]{1,0:T(8,128)(2,1)S(1)} %collective-permute-done.7.refs_6_.refs_8_), channel_id=1, source_target_pairs={{0,1},{1,0},{2,3},{3,2},{4,5},{5,4},{6,7},{7,6},{8,9},{9,8},{10,11... | collective-permute-start | bytes 3538952 | tf_op jit(solution)/shard_map/ppermute | solution.py:621
  48.7 6.7 %collective-permute-start.17 = (bf16[320,192]{1,0:T(8,128)(2,1)}, bf16[320,192]{1,0:T(8,128)(2,1)S(1)}, u32[]{:S(2)}, u32[]{:S(2)}) collective-permute-start(bf16[320,192]{1,0:T(8,128)(2,1)} %get-tuple-element.152), channel_id=1, source_target_pairs={{0,1},{1,0},{2,3},{3,2},{4,5},{5,4},{6,7},{7,6},{8,9},{9,8},{10,11... | collective-permute-start | bytes 368648 | tf_op jit(solution)/shard_map/ppermute | solution.py:621
  49.0 7.4 %collective-permute-start.18 = (bf16[320,192]{1,0:T(8,128)(2,1)}, bf16[320,192]{1,0:T(8,128)(2,1)S(1)}, u32[]{:S(2)}, u32[]{:S(2)}) collective-permute-start(bf16[320,192]{1,0:T(8,128)(2,1)} %get-tuple-element.153), channel_id=1, source_target_pairs={{0,2},{1,3},{2,0},{3,1},{4,6},{5,7},{6,4},{7,5},{8,10},{9,11},{10,... | collective-permute-start | bytes 368648 | tf_op jit(solution)/shard_map/ppermute | solution.py:621
  50.5 8.0 %collective-permute-start.19 = (bf16[320,192]{1,0:T(8,128)(2,1)}, bf16[320,192]{1,0:T(8,128)(2,1)S(1)}, u32[]{:S(2)}, u32[]{:S(2)}) collective-permute-start(bf16[320,192]{1,0:T(8,128)(2,1)} %get-tuple-element.154), channel_id=1, source_target_pairs={{0,3},{1,2},{2,1},{3,0},{4,7},{5,6},{6,5},{7,4},{8,11},{9,10},{10,... | collective-permute-start | bytes 368648 | tf_op jit(solution)/shard_map/ppermute | solution.py:621
  50.7 7.9 %collective-permute-start.22 = (bf16[768,192]{1,0:T(8,128)(2,1)S(1)}, bf16[768,192]{1,0:T(8,128)(2,1)S(1)}, u32[]{:S(2)}, u32[]{:S(2)}) collective-permute-start(bf16[768,192]{1,0:T(8,128)(2,1)S(1)} %collective-permute-done.21.refs_6_.refs_11_), channel_id=1, source_target_pairs={{0,1},{1,0},{2,3},{3,2},{4,5},{5,4},{6,7},{7,6},{8,9},{9,8},{10,11... | collective-permute-start | bytes 884744 | tf_op jit(solution)/shard_map/ppermute | solution.py:621
  55.5 35.9 %collective-permute-start.29 = (bf16[1536,384]{1,0:T(8,128)(2,1)S(1)}, bf16[1536,384]{1,0:T(8,128)(2,1)S(1)}, u32[]{:S(2)}, u32[]{:S(2)}) collective-permute-start(bf16[1536,384]{1,0:T(8,128)(2,1)S(1)} %collective-permute-done.7.refs_6_.refs_8_), channel_id=1, source_target_pairs={{0,4},{4,0},{8,12},{12,8},{16,20},{20,16},{24,28},{28,24},{1,5},{5... | collective-permute-start | bytes 3538952 | tf_op jit(solution)/shard_map/ppermute | solution.py:621
  64.1 8.6 %collective-permute-start.23 = (bf16[80,768]{1,0:T(8,128)(2,1)}, bf16[80,768]{1,0:T(8,128)(2,1)S(1)}, u32[]{:S(2)}, u32[]{:S(2)}) collective-permute-start(bf16[80,768]{1,0:T(8,128)(2,1)} %get-tuple-element.167.refs_24_), channel_id=1, source_target_pairs={{0,8},{4,12},{8,0},{12,4},{16,24},{20,28},{24,16},{28,20},{1,9},{5... | collective-permute-start | bytes 368648 | tf_op jit(solution)/shard_map/ppermute | solution.py:621
  65.8 12.5 %collective-permute-start.24 = (bf16[80,768]{1,0:T(8,128)(2,1)}, bf16[80,768]{1,0:T(8,128)(2,1)S(1)}, u32[]{:S(2)}, u32[]{:S(2)}) collective-permute-start(bf16[80,768]{1,0:T(8,128)(2,1)} %get-tuple-element.168.refs_25_), channel_id=1, source_target_pairs={{0,16},{4,20},{8,24},{12,28},{16,0},{20,4},{24,8},{28,12},{1,17},{... | collective-permute-start | bytes 368648 | tf_op jit(solution)/shard_map/ppermute | solution.py:621
  68.4 10.0 %collective-permute-start.25 = (bf16[80,768]{1,0:T(8,128)(2,1)}, bf16[80,768]{1,0:T(8,128)(2,1)S(1)}, u32[]{:S(2)}, u32[]{:S(2)}) collective-permute-start(bf16[80,768]{1,0:T(8,128)(2,1)} %get-tuple-element.169.refs_26_), channel_id=1, source_target_pairs={{0,24},{4,28},{8,16},{12,20},{16,8},{20,12},{24,0},{28,4},{1,25},{... | collective-permute-start | bytes 368648 | tf_op jit(solution)/shard_map/ppermute | solution.py:621
  68.6 24.9 %collective-permute-start.31 = (bf16[1536,384]{1,0:T(8,128)(2,1)S(1)}, bf16[1536,384]{1,0:T(8,128)(2,1)S(1)}, u32[]{:S(2)}, u32[]{:S(2)}) collective-permute-start(bf16[1536,384]{1,0:T(8,128)(2,1)S(1)} %collective-permute-done.30.refs_5_.refs_10_), channel_id=1, source_target_pairs={{0,1},{1,0},{2,3},{3,2},{4,5},{5,4},{6,7},{7,6},{8,9},{9,8},{10,11... | collective-permute-start | bytes 3538952 | tf_op jit(solution)/shard_map/ppermute | solution.py:621
  78.3 13.0 %collective-permute-start.26 = (bf16[80,768]{1,0:T(8,128)(2,1)}, bf16[80,768]{1,0:T(8,128)(2,1)S(1)}, u32[]{:S(2)}, u32[]{:S(2)}) collective-permute-start(bf16[80,768]{1,0:T(8,128)(2,1)} %get-tuple-element.171), channel_id=1, source_target_pairs={{0,8},{4,12},{8,0},{12,4},{16,24},{20,28},{24,16},{28,20},{1,9},{5... | collective-permute-start | bytes 368648 | tf_op jit(solution)/shard_map/ppermute | solution.py:621
  81.1 12.3 %collective-permute-start.27 = (bf16[80,768]{1,0:T(8,128)(2,1)}, bf16[80,768]{1,0:T(8,128)(2,1)S(1)}, u32[]{:S(2)}, u32[]{:S(2)}) collective-permute-start(bf16[80,768]{1,0:T(8,128)(2,1)} %get-tuple-element.172), channel_id=1, source_target_pairs={{0,16},{4,20},{8,24},{12,28},{16,0},{20,4},{24,8},{28,12},{1,17},{... | collective-permute-start | bytes 368648 | tf_op jit(solution)/shard_map/ppermute | solution.py:621
  82.1 11.3 %collective-permute-start.28 = (bf16[80,768]{1,0:T(8,128)(2,1)}, bf16[80,768]{1,0:T(8,128)(2,1)S(1)}, u32[]{:S(2)}, u32[]{:S(2)}) collective-permute-start(bf16[80,768]{1,0:T(8,128)(2,1)} %get-tuple-element.173), channel_id=1, source_target_pairs={{0,24},{4,28},{8,16},{12,20},{16,8},{20,12},{24,0},{28,4},{1,25},{... | collective-permute-start | bytes 368648 | tf_op jit(solution)/shard_map/ppermute | solution.py:621
  109.5 21.3 %collective-permute-start.36 = (bf16[4,384,768]{2,1,0:T(8,128)(2,1)}, bf16[4,384,768]{2,1,0:T(8,128)(2,1)S(1)}, u32[]{:S(2)}, u32[]{:S(2)}) collective-permute-start(bf16[4,384,768]{2,1,0:T(8,128)(2,1)} %outer_out_sent.1), channel_id=1, source_target_pairs={{0,1},{1,0},{2,3},{3,2},{4,5},{5,4},{6,7},{7,6},{8,9},{9,8},{10,11... | collective-permute-start | bytes 7077896 | tf_op jit(solution)/shard_map/ppermute | solution.py:621
  109.7 17.7 %collective-permute-start.37 = (bf16[80,768]{1,0:T(8,128)(2,1)S(1)}, bf16[80,768]{1,0:T(8,128)(2,1)S(1)}, u32[]{:S(2)}, u32[]{:S(2)}) collective-permute-start(bf16[80,768]{1,0:T(8,128)(2,1)S(1)} %copy-done.59), channel_id=1, source_target_pairs={{0,8},{4,12},{8,0},{12,4},{16,24},{20,28},{24,16},{28,20},{1,9},{5... | collective-permute-start | bytes 368648 | tf_op jit(solution)/shard_map/ppermute | solution.py:621
  111.5 17.8 %collective-permute-start.38 = (bf16[80,768]{1,0:T(8,128)(2,1)S(1)}, bf16[80,768]{1,0:T(8,128)(2,1)S(1)}, u32[]{:S(2)}, u32[]{:S(2)}) collective-permute-start(bf16[80,768]{1,0:T(8,128)(2,1)S(1)} %copy-done.58), channel_id=1, source_target_pairs={{0,16},{4,20},{8,24},{12,28},{16,0},{20,4},{24,8},{28,12},{1,17},{... | collective-permute-start | bytes 368648 | tf_op jit(solution)/shard_map/ppermute | solution.py:621
  112.6 18.3 %collective-permute-start.39 = (bf16[80,768]{1,0:T(8,128)(2,1)S(1)}, bf16[80,768]{1,0:T(8,128)(2,1)S(1)}, u32[]{:S(2)}, u32[]{:S(2)}) collective-permute-start(bf16[80,768]{1,0:T(8,128)(2,1)S(1)} %copy-done.57), channel_id=1, source_target_pairs={{0,24},{4,28},{8,16},{12,20},{16,8},{20,12},{24,0},{28,4},{1,25},{... | collective-permute-start | bytes 368648 | tf_op jit(solution)/shard_map/ppermute | solution.py:621
  126.4 16.0 %collective-permute-start.33 = (bf16[80,768]{1,0:T(8,128)(2,1)}, bf16[80,768]{1,0:T(8,128)(2,1)S(1)}, u32[]{:S(2)}, u32[]{:S(2)}) collective-permute-start(bf16[80,768]{1,0:T(8,128)(2,1)} %get-tuple-element.188), channel_id=1, source_target_pairs={{0,8},{4,12},{8,0},{12,4},{16,24},{20,28},{24,16},{28,20},{1,9},{5... | collective-permute-start | bytes 368648 | tf_op jit(solution)/shard_map/ppermute | solution.py:621
  127.4 15.1 %collective-permute-start.34 = (bf16[80,768]{1,0:T(8,128)(2,1)}, bf16[80,768]{1,0:T(8,128)(2,1)S(1)}, u32[]{:S(2)}, u32[]{:S(2)}) collective-permute-start(bf16[80,768]{1,0:T(8,128)(2,1)} %get-tuple-element.189), channel_id=1, source_target_pairs={{0,16},{4,20},{8,24},{12,28},{16,0},{20,4},{24,8},{28,12},{1,17},{... | collective-permute-start | bytes 368648 | tf_op jit(solution)/shard_map/ppermute | solution.py:621
  129.4 13.1 %collective-permute-start.35 = (bf16[80,768]{1,0:T(8,128)(2,1)}, bf16[80,768]{1,0:T(8,128)(2,1)S(1)}, u32[]{:S(2)}, u32[]{:S(2)}) collective-permute-start(bf16[80,768]{1,0:T(8,128)(2,1)} %get-tuple-element.190), channel_id=1, source_target_pairs={{0,24},{4,28},{8,16},{12,20},{16,8},{20,12},{24,0},{28,4},{1,25},{... | collective-permute-start | bytes 368648 | tf_op jit(solution)/shard_map/ppermute | solution.py:621
  141.3 17.5 %collective-permute-start.41 = (bf16[384,768]{1,0:T(8,128)(2,1)}, bf16[384,768]{1,0:T(8,128)(2,1)S(1)}, u32[]{:S(2)}, u32[]{:S(2)}) collective-permute-start(bf16[384,768]{1,0:T(8,128)(2,1)} %get-tuple-element.206), channel_id=1, source_target_pairs={{0,4},{4,0},{8,12},{12,8},{16,20},{20,16},{24,28},{28,24},{1,5},{5... | collective-permute-start | bytes 1769480 | tf_op jit(solution)/shard_map/ppermute | solution.py:621
  142.4 7.7 %collective-permute-start.40 = (bf16[4,768,384]{2,1,0:T(8,128)(2,1)}, bf16[4,768,384]{2,1,0:T(8,128)(2,1)S(1)}, u32[]{:S(2)}, u32[]{:S(2)}) collective-permute-start(bf16[4,768,384]{2,1,0:T(8,128)(2,1)} %get-tuple-element.203), channel_id=1, source_target_pairs={{0,1},{1,0},{2,3},{3,2},{4,5},{5,4},{6,7},{7,6},{8,9},{9,8},{10,11... | collective-permute-start | bytes 7077896 | tf_op jit(solution)/shard_map/ppermute | solution.py:621
  148.4 11.2 %collective-permute-start.42 = (bf16[768,384]{1,0:T(8,128)(2,1)}, bf16[768,384]{1,0:T(8,128)(2,1)S(1)}, u32[]{:S(2)}, u32[]{:S(2)}) collective-permute-start(bf16[768,384]{1,0:T(8,128)(2,1)} %get-tuple-element.211), channel_id=1, source_target_pairs={{0,1},{1,0},{2,3},{3,2},{4,5},{5,4},{6,7},{7,6},{8,9},{9,8},{10,11... | collective-permute-start | bytes 1769480 | tf_op jit(solution)/shard_map/ppermute | solution.py:621
  148.9 7.7 %collective-permute-start.43 = (bf16[320,192]{1,0:T(8,128)(2,1)}, bf16[320,192]{1,0:T(8,128)(2,1)S(1)}, u32[]{:S(2)}, u32[]{:S(2)}) collective-permute-start(bf16[320,192]{1,0:T(8,128)(2,1)} %get-tuple-element.213), channel_id=1, source_target_pairs={{0,1},{1,0},{2,3},{3,2},{4,5},{5,4},{6,7},{7,6},{8,9},{9,8},{10,11... | collective-permute-start | bytes 368648 | tf_op jit(solution)/shard_map/ppermute | solution.py:621
  149.0 9.0 %collective-permute-start.44 = (bf16[320,192]{1,0:T(8,128)(2,1)}, bf16[320,192]{1,0:T(8,128)(2,1)S(1)}, u32[]{:S(2)}, u32[]{:S(2)}) collective-permute-start(bf16[320,192]{1,0:T(8,128)(2,1)} %get-tuple-element.214), channel_id=1, source_target_pairs={{0,2},{1,3},{2,0},{3,1},{4,6},{5,7},{6,4},{7,5},{8,10},{9,11},{10,... | collective-permute-start | bytes 368648 | tf_op jit(solution)/shard_map/ppermute | solution.py:621
  150.1 8.7 %collective-permute-start.45 = (bf16[320,192]{1,0:T(8,128)(2,1)}, bf16[320,192]{1,0:T(8,128)(2,1)S(1)}, u32[]{:S(2)}, u32[]{:S(2)}) collective-permute-start(bf16[320,192]{1,0:T(8,128)(2,1)} %get-tuple-element.215), channel_id=1, source_target_pairs={{0,3},{1,2},{2,1},{3,0},{4,7},{5,6},{6,5},{7,4},{8,11},{9,10},{10,... | collective-permute-start | bytes 368648 | tf_op jit(solution)/shard_map/ppermute | solution.py:621
  156.6 32.5 %collective-permute-start.48 = (bf16[384,768]{1,0:T(8,128)(2,1)}, bf16[384,768]{1,0:T(8,128)(2,1)S(1)}, u32[]{:S(2)}, u32[]{:S(2)}) collective-permute-start(bf16[384,768]{1,0:T(8,128)(2,1)} %get-tuple-element.229), channel_id=1, source_target_pairs={{0,4},{4,0},{8,12},{12,8},{16,20},{20,16},{24,28},{28,24},{1,5},{5... | collective-permute-start | bytes 1769480 | tf_op jit(solution)/shard_map/ppermute | solution.py:621
  160.6 30.6 %all-to-all-start = ((bf16[8,96,384]{2,1,0:T(8,128)(2,1)}), bf16[8,96,384]{2,1,0:T(8,128)(2,1)S(1)}, u32[]{:S(2)}, u32[]{:S(2)}) async-start(bf16[8,96,384]{2,1,0:T(8,128)(2,1)} %bitcast.12), calls=%async_computation | async-start | bytes 1179648 | tf_op jit(solution)/shard_map/all_to_all | solution.py:976
  164.8 24.3 %collective-permute-start.49 = (bf16[320,768]{1,0:T(8,128)(2,1)S(1)}, bf16[320,768]{1,0:T(8,128)(2,1)S(1)}, u32[]{:S(2)}, u32[]{:S(2)}) collective-permute-start(bf16[320,768]{1,0:T(8,128)(2,1)S(1)} %copy-done.11), channel_id=1, source_target_pairs={{0,2},{1,3},{2,0},{3,1},{4,6},{5,7},{6,4},{7,5},{8,10},{9,11},{10,... | collective-permute-start | bytes 1474568 | tf_op jit(solution)/shard_map/ppermute | solution.py:621
  166.4 24.3 %collective-permute-start.47 = (bf16[384,768]{1,0:T(8,128)(2,1)S(1)}, bf16[384,768]{1,0:T(8,128)(2,1)S(1)}, u32[]{:S(2)}, u32[]{:S(2)}) collective-permute-start(bf16[384,768]{1,0:T(8,128)(2,1)S(1)} %add_convert_fusion.4), channel_id=1, source_target_pairs={{0,2},{1,3},{2,0},{3,1},{4,6},{5,7},{6,4},{7,5},{8,10},{9,11},{10,... | collective-permute-start | bytes 1769480 | tf_op jit(solution)/shard_map/ppermute | solution.py:621
  166.9 24.3 %collective-permute-start.46 = (bf16[768,384]{1,0:T(8,128)(2,1)}, bf16[768,384]{1,0:T(8,128)(2,1)S(1)}, u32[]{:S(2)}, u32[]{:S(2)}) collective-permute-start(bf16[768,384]{1,0:T(8,128)(2,1)} %get-tuple-element.227), channel_id=1, source_target_pairs={{0,4},{4,0},{8,12},{12,8},{16,20},{20,16},{24,28},{28,24},{1,5},{5... | collective-permute-start | bytes 1769480 | tf_op jit(solution)/shard_map/ppermute | solution.py:621
  191.3 15.5 %collective-permute-start.54 = (bf16[4,96,640]{2,1,0:T(8,128)(2,1)}, bf16[4,96,640]{2,1,0:T(8,128)(2,1)S(1)}, u32[]{:S(2)}, u32[]{:S(2)}) collective-permute-start(bf16[4,96,640]{2,1,0:T(8,128)(2,1)} %get-tuple-element.246), channel_id=1, source_target_pairs={{0,4},{4,0},{8,12},{12,8},{16,20},{20,16},{24,28},{28,24},{1,5},{5... | collective-permute-start | bytes 1474568 | tf_op jit(solution)/shard_map/ppermute | solution.py:621
  196.9 24.3 %collective-permute-start.53 = (bf16[2,256,768]{2,1,0:T(8,128)(2,1)S(1)}, bf16[2,256,768]{2,1,0:T(8,128)(2,1)S(1)}, u32[]{:S(2)}, u32[]{:S(2)}) collective-permute-start(bf16[2,256,768]{2,1,0:T(8,128)(2,1)S(1)} %add_convert_fusion.1), channel_id=1, source_target_pairs={{0,2},{1,3},{2,0},{3,1},{4,6},{5,7},{6,4},{7,5},{8,10},{9,11},{10,... | collective-permute-start | bytes 2359304 | tf_op jit(solution)/shard_map/ppermute | solution.py:621
  207.0 8.1 %collective-permute-start.57 = (bf16[96,640]{1,0:T(8,128)(2,1)S(1)}, bf16[96,640]{1,0:T(8,128)(2,1)S(1)}, u32[]{:S(2)}, u32[]{:S(2)}) collective-permute-start(bf16[96,640]{1,0:T(8,128)(2,1)S(1)} %get-tuple-element.268), channel_id=1, source_target_pairs={{0,24},{4,28},{8,16},{12,20},{16,8},{20,12},{24,0},{28,4},{1,25},{... | collective-permute-start | bytes 368648 | tf_op jit(solution)/shard_map/ppermute | solution.py:621
  210.6 10.6 %collective-permute-start.56 = (bf16[96,640]{1,0:T(8,128)(2,1)S(1)}, bf16[96,640]{1,0:T(8,128)(2,1)S(1)}, u32[]{:S(2)}, u32[]{:S(2)}) collective-permute-start(bf16[96,640]{1,0:T(8,128)(2,1)S(1)} %get-tuple-element.269), channel_id=1, source_target_pairs={{0,16},{4,20},{8,24},{12,28},{16,0},{20,4},{24,8},{28,12},{1,17},{... | collective-permute-start | bytes 368648 | tf_op jit(solution)/shard_map/ppermute | solution.py:621
  210.6 10.6 %collective-permute-start.55 = (bf16[96,640]{1,0:T(8,128)(2,1)S(1)}, bf16[96,640]{1,0:T(8,128)(2,1)S(1)}, u32[]{:S(2)}, u32[]{:S(2)}) collective-permute-start(bf16[96,640]{1,0:T(8,128)(2,1)S(1)} %get-tuple-element.270), channel_id=1, source_target_pairs={{0,8},{4,12},{8,0},{12,4},{16,24},{20,28},{24,16},{28,20},{1,9},{5... | collective-permute-start | bytes 368648 | tf_op jit(solution)/shard_map/ppermute | solution.py:621
  211.6 18.3 %collective-permute-start.61 = (bf16[768,384]{1,0:T(8,128)(2,1)S(1)}, bf16[768,384]{1,0:T(8,128)(2,1)S(1)}, u32[]{:S(2)}, u32[]{:S(2)}) collective-permute-start(bf16[768,384]{1,0:T(8,128)(2,1)S(1)} %add_convert_fusion.2), channel_id=1, source_target_pairs={{0,2},{1,3},{2,0},{3,1},{4,6},{5,7},{6,4},{7,5},{8,10},{9,11},{10,... | collective-permute-start | bytes 1769480 | tf_op jit(solution)/shard_map/ppermute | solution.py:621
  215.1 14.8 %collective-permute-start.62 = (bf16[768,384]{1,0:T(8,128)(2,1)}, bf16[768,384]{1,0:T(8,128)(2,1)}, u32[]{:S(2)}, u32[]{:S(2)}) collective-permute-start(bf16[768,384]{1,0:T(8,128)(2,1)} %get-tuple-element.260), channel_id=1, source_target_pairs={{0,4},{4,0},{8,12},{12,8},{16,20},{20,16},{24,28},{28,24},{1,5},{5... | collective-permute-start | bytes 1769480 | tf_op jit(solution)/shard_map/ppermute | solution.py:621
  224.0 7.2 %collective-permute-start.60 = (f32[96,256]{1,0:T(8,128)S(1)}, f32[96,256]{1,0:T(8,128)S(1)}, u32[]{:S(2)}, u32[]{:S(2)}) collective-permute-start(f32[96,256]{1,0:T(8,128)S(1)} %pad_maximum_fusion.1), channel_id=1, source_target_pairs={{0,2},{1,3},{2,0},{3,1},{4,6},{5,7},{6,4},{7,5},{8,10},{9,11},{10,... | collective-permute-start | bytes 294920 | tf_op jit(solution)/shard_map/ppermute | solution.py:621
  (85 other events, 472.2 us)

commit v2 on v1

--- a/solution.py
+++ b/solution.py
@@ -243,11 +243,11 @@
                 part = mm(prob, value)
                 acc = part if acc is None else acc + part
             mixed_ref[pl.ds(i * BLOCK, BLOCK), at : at + head] = acc.astype(BF)
-    own = s0_ref.shape[0]
+    own = s0_ref.shape[0] * 2 // 3
     mixed = mixed_ref[...]
     for j, ref in enumerate((s0_ref, s1_ref, s2_ref, s3_ref)):
         start = jnp.bitwise_xor(gy_ref[0], j) * own
-        ref[...] = mm(one_hot_rows(pos_ref[...], start, own), mixed).astype(BF)
+        ref[...] = fold(mm(one_hot_rows(pos_ref[...], start, own), mixed).astype(BF))
 
 
 def route_kernel(experts, pieces, *refs):
@@ -257,7 +257,7 @@
     res_ref, prob_ref, gate_ref = refs[12 + 2 * pieces :]
     attn = None
     for j in range(4):
-        part = mm_nt(mixed_refs[j][...], out_refs[j][...])
+        part = mm_nt(unfold(mixed_refs[j][...]), out_refs[j][...])
         attn = part if attn is None else attn + part
     extras = extras_ref[...]
     gain = jnp.transpose(extras.astype(F32))[1:2]
@@ -282,6 +282,21 @@
     split(sg, sg_refs)
 
 
+def fold(value):
+    rows = value.shape[0]
+    edge = value[:, LANES:]
+    edge = jnp.concatenate([edge[: rows // 2], edge[rows // 2 :]], axis=1)
+    return jnp.concatenate([value[:, :LANES], edge], axis=0)
+
+
+def unfold(value):
+    rows = value.shape[0] * 2 // 3
+    edge = value[rows:]
+    half = LANES // 2
+    edge = jnp.concatenate([edge[:, :half], edge[:, half:]], axis=0)
+    return jnp.concatenate([value[:rows], edge], axis=1)
+
+
 def split(value, refs):
     rows = refs[0].shape[0]
     for n, ref in enumerate(refs):
@@ -294,85 +309,80 @@
     return jnp.concatenate([ref[...] for ref in refs], axis=0)
 
 
-def fetch(packs, buf, sems, first):
+def fetch(packs, win_buf, wout_buf, sems):
     copies = []
-    at = 0
-    for n, pack in enumerate(packs):
-        rows = pack.shape[0]
-        copy = pltpu.make_async_copy(pack, buf.at[pl.ds(at, rows), :], sems.at[first + n])
-        copy.start()
-        copies.append(copy)
-        at += rows
+    model, hidden = win_buf.shape[0], packs[0].shape[1]
+    for j, pack in enumerate(packs):
+        place = pl.ds(j * hidden, hidden)
+        cuts = (
+            (pack.at[pl.ds(0, model), :], win_buf.at[:, place]),
+            (pack.at[pl.ds(model, hidden), :], wout_buf.at[place, pl.ds(0, hidden)]),
+            (pack.at[pl.ds(model + hidden, hidden), :], wout_buf.at[place, pl.ds(hidden, hidden)]),
+        )
+        for n, (source, target) in enumerate(cuts):
+            copies.append(pltpu.make_async_copy(source, target, sems.at[3 * j + n]))
     return copies
 
 
-def out_half(buf, j, n, hidden):
-    model = buf.shape[1] // 2
-    return buf[j, model + n * hidden : model + (n + 1) * hidden, :]
-
-
-def expert_kernel(pieces, groups, last, *refs):
+def expert_kernel(pieces, last, *refs):
     row_refs = refs[:pieces]
     refs = refs[pieces:]
     if last:
         before_ref, refs = refs[0], refs[1:]
-    total = sum(groups)
-    packs, refs = refs[:total], refs[total:]
+    packs, refs = refs[:4], refs[4:]
     outs = refs[: pieces if last else 1]
-    act_ref, slope_ref, buf, sems = refs[len(outs) :]
-    hidden = act_ref.shape[2]
-    copies = []
-    first = 0
-    for j, size in enumerate(groups):
-        copies.append(fetch(packs[first : first + size], buf.at[j], sems, first))
-        first += size
+    act_ref, slope_ref, win_buf, wout_buf, sems = refs[len(outs) :]
+    pair = 2 * packs[0].shape[1]
+    copies = fetch(packs, win_buf, wout_buf, sems)
+    for copy in copies:
+        copy.start()
     rows = joined(row_refs)
-    left = before_ref[:, : rows.shape[1] // 2] if last else None
-    right = before_ref[:, rows.shape[1] // 2 :] if last else None
-    for j in range(len(groups)):
-        for copy in copies[j]:
-            copy.wait()
-        pre = mm(rows, buf[j, : rows.shape[1], :])
+    acc = before_ref[...] if last else None
+    for j in range(2):
+        place = slice(j * pair, (j + 1) * pair)
+        mine = copies[6 * j : 6 * j + 6]
+        mine[0].wait()
+        mine[3].wait()
+        pre = mm(rows, win_buf[:, place])
         cdf = 0.5 * (1.0 + lax.erf(pre * 0.7071067811865476))
         slope = cdf + pre * (0.3989422804014327 * jnp.exp(-0.5 * pre * pre))
         act = (pre * cdf).astype(BF)
-        act_ref[j] = act
-        slope_ref[j] = slope.astype(BF)
-        a = mm(act, out_half(buf, j, 0, hidden))
-        b = mm(act, out_half(buf, j, 1, hidden))
-        left = a if left is None else left + a
-        right = b if right is None else right + b
-    whole = jnp.concatenate([left, right], axis=1)
+        act_ref[:, place] = act
+        slope_ref[:, place] = slope.astype(BF)
+        for n in (1, 2, 4, 5):
+            mine[n].wait()
+        part = mm(act, wout_buf[place, :])
+        acc = part if acc is None else acc + part
     if last:
-        split(whole.astype(BF), outs)
+        split(acc.astype(BF), outs)
     else:
-        outs[0][...] = whole
-
-
-def expert_back_kernel(pieces, groups, *refs):
-    sg_refs = refs[:pieces]
-    slopes = refs[pieces : pieces + 2]
-    total = sum(groups)
-    refs = refs[pieces + 2 :]
-    packs, gr_refs = refs[:total], refs[total : total + pieces]
-    gp_ref, buf, sems = refs[total + pieces :]
-    hidden = gp_ref.shape[2]
-    copies = []
-    first = 0
-    for j, size in enumerate(groups):
-        copies.append(fetch(packs[first : first + size], buf.at[j], sems, first))
-        first += size
+        outs[0][...] = acc
+
+
+def expert_back_kernel(pieces, *refs):
+    sg_refs, slopes = refs[:pieces], refs[pieces : pieces + 2]
+    packs, refs = refs[pieces + 2 : pieces + 10], refs[pieces + 10 :]
+    gr_refs = refs[:pieces]
+    gp_ref, win_buf, wout_buf, sems = refs[pieces:]
+    pair = 2 * packs[0].shape[1]
+    copies = fetch(packs, win_buf, wout_buf, sems)
+    for j in range(4):
+        for n in (1, 2, 4, 5, 0, 3):
+            copies[6 * j + n].start()
     sg = joined(sg_refs)
-    model = sg.shape[1]
     acc = None
-    for j in range(len(groups)):
-        for copy in copies[j]:
-            copy.wait()
-        grad = mm_nt(sg[:, : model // 2], out_half(buf, j, 0, hidden))
-        grad = grad + mm_nt(sg[:, model // 2 :], out_half(buf, j, 1, hidden))
-        grad = (grad * slopes[j // 4][j % 4].astype(F32)).astype(BF)
-        gp_ref[j] = grad
-        part = mm_nt(grad, buf[j, :model, :])
+    for j in range(4):
+        place = slice(j * pair, (j + 1) * pair)
+        near = slice(j % 2 * pair, (j % 2 + 1) * pair)
+        mine = copies[6 * j : 6 * j + 6]
+        for n in (1, 2, 4, 5):
+            mine[n].wait()
+        grad = mm_nt(sg, wout_buf[place, :])
+        grad = (grad * slopes[j // 2][:, near].astype(F32)).astype(BF)
+        gp_ref[:, place] = grad
+        mine[0].wait()
+        mine[3].wait()
+        part = mm_nt(grad, win_buf[:, place])
         acc = part if acc is None else acc + part
     split(acc.astype(BF), gr_refs)
 
@@ -380,8 +390,9 @@
 def outer_sent_kernel(pieces, picks, flip, *refs):
     wide = joined(refs[:pieces])
     sources, out_ref = refs[pieces:-1], refs[-1]
+    hidden = out_ref.shape[1 if flip else 2]
     for n, (a, b) in enumerate(picks):
-        thin = sources[a][b]
+        thin = sources[a][:, b * hidden : (b + 1) * hidden]
         out_ref[n] = (mm_tn(thin, wide) if flip else mm_tn(wide, thin)).astype(BF)
 
 
@@ -389,8 +400,9 @@
     wide = joined(refs[:pieces])
     sources, arrived_ref = refs[pieces:-5], refs[-5]
     out_refs = refs[-4:]
+    hidden = out_refs[0].shape[0 if flip else 1]
     for n, (a, b) in enumerate(picks):
-        thin = sources[a][b]
+        thin = sources[a][:, b * hidden : (b + 1) * hidden]
         value = mm_tn(thin, wide) if flip else mm_tn(wide, thin)
         value = value + arrived_ref[n].astype(F32)
         out_refs[n][...] = value.astype(out_refs[n].dtype)
@@ -442,9 +454,11 @@
     d2_ref[...] = d2
     grad_attn = (g + d2.astype(F32)).astype(BF)
     for j in range(4):
-        gm_refs[j][...] = mm(grad_attn, out_refs[j][...]).astype(BF)
+        gm_refs[j][...] = fold(mm(grad_attn, out_refs[j][...]).astype(BF))
     for target, j in ((keep_ref, 0), (send_ref, 1)):
-        mixed = jnp.concatenate([mixed_refs[j][...], mixed_refs[j + 2][...]], axis=1)
+        mixed = jnp.concatenate(
+            [unfold(mixed_refs[j][...]), unfold(mixed_refs[j + 2][...])], axis=1
+        )
         target[...] = mm_tn(grad_attn, mixed).astype(BF)
     grad_gain = jnp.sum(grad_h2 * unit, axis=0, keepdims=True)
     small = router_ref[...]
@@ -478,14 +492,15 @@
     blocks = seq // BLOCK
     head = 64
     heads = width // head
-    own = g0_ref.shape[0]
+    own = g0_ref.shape[0] * 2 // 3
     gy = gy_ref[0]
+    pieces = [unfold(ref[...]) for ref in (g0_ref, g1_ref, g2_ref, g3_ref)]
     for i in range(blocks):
         rows = pl.ds(i * BLOCK, BLOCK)
         pos = pos_ref[rows, :]
         acc = None
-        for j, ref in enumerate((g0_ref, g1_ref, g2_ref, g3_ref)):
-            part = mm(one_hot_cols(pos, jnp.bitwise_xor(gy, j) * own, own), ref[...])
+        for j, piece in enumerate(pieces):
+            part = mm(one_hot_cols(pos, jnp.bitwise_xor(gy, j) * own, own), piece)
             acc = part if acc is None else acc + part
         gm_ref[rows, :] = acc.astype(BF)
     sums = [[None] * heads for _ in range(blocks)]
@@ -789,7 +804,7 @@
             struct((heads * pairs, BLOCK, BLOCK), BF),
             struct((seq, width), BF),
         ]
-        + [struct((own, width), BF)] * 4
+        + [struct((own * 3 // 2, LANES), BF)] * 4
         + [struct((model, 3 * width), BF)],
         [SM, SM, SM] + [VM] * 5 + [ANY] * parts,
         (
@@ -845,31 +860,32 @@
     sg = list(lax.optimization_barrier((*sg, *rows_in))[: len(sg)])
     grads_in = spread(sg, experts)
 
-    def pack_scratch(shards, copies):
+    def pack_scratch(shards):
         return [
-            pltpu.VMEM((shards, 2 * model, hidden), BF),
-            pltpu.SemaphoreType.DMA((copies,)),
+            pltpu.VMEM((model, shards * hidden), BF),
+            pltpu.VMEM((shards * hidden, model), BF),
+            pltpu.SemaphoreType.DMA((3 * shards,)),
         ]
 
-    kept_shapes = [struct((4, own, hidden), BF)] * 2
+    kept_shapes = [struct((own, 4 * hidden), BF)] * 2
     begun, act_a, slope_a = call(
-        partial(expert_kernel, pieces, (1, 1, 1, 1), False),
+        partial(expert_kernel, pieces, False),
         "expert_near",
         [struct((own, model), F32)] + kept_shapes,
         [VM] * pieces + [ANY] * 4,
         (*rows_in, *near),
-        scratch=pack_scratch(4, 4),
+        scratch=pack_scratch(4),
         cost=7,
     )
     pack_d, begun = lax.optimization_barrier((pack_d, begun, *grads_in))[:2]
     far = [pack_y, pack_yc, pack_d, swap(pack_d, "gy", 1)]
     *result, act_b, slope_b = call(
-        partial(expert_kernel, pieces, (1, 1, 1, 1), True),
+        partial(expert_kernel, pieces, True),
         "expert_far",
         slot_shapes + kept_shapes,
         [VM] * (pieces + 1) + [ANY] * 4,
         (*rows_in, begun, *far),
-        scratch=pack_scratch(4, 4),
+        scratch=pack_scratch(4),
         cost=7.5,
     )
     result_back = spread(result, experts)
@@ -886,12 +902,12 @@
     out_arrived = swap(out_sent, "gy", 1)
     slope_b = after(slope_b, out_sent)
     *grad_rows, grad_pre = call(
-        partial(expert_back_kernel, pieces, (1,) * 8),
+        partial(expert_back_kernel, pieces),
         "expert_back",
-        slot_shapes + [struct((8, own, hidden), BF)],
+        slot_shapes + [struct((own, 8 * hidden), BF)],
         [VM] * (pieces + 2) + [ANY] * 8,
         (*grads_in, slope_a, slope_b, *near, *far),
-        scratch=pack_scratch(8, 8),
+        scratch=pack_scratch(8),
         cost=12,
     )
     rows_back = spread(grad_rows, experts)
@@ -931,7 +947,7 @@
     *mixed_grads, d2, small, project_keep, project_send = call(
         partial(combine_kernel, pieces),
         "combine",
-        [struct((own, width), BF)] * 4
+        [struct((own * 3 // 2, LANES), BF)] * 4
         + [
             struct((own, model), BF),
             struct((small_rows, model), F32),

time: 239 us -> 234 us (0.979)
  Pallas kernels: 113 us -> 108 us
    pallas_call x17, Pallas kernels: 113 us -> 108 us  [call(): pl.pallas_call(kernel, name=name, out_shape=list(outs), in_specs=in_specs...]
  transfers between devices with their start and end apart: 64 -> 64, of which waited for: 18 -> 17; matrix products, arithmetic and copies ran while one was open for 3% -> 3% of each run, Pallas kernels for 41% -> 41%
where the time goes in v2:
time: 234 us; the launch traced here: 231 us
  Pallas kernels  108 us (46%)
  starting transfers between devices  66.3 us (28%)
  waiting for transfers between devices  33.8 us (14%)
  local copies, waits for them, and re-layouts  13.4 us (6%)
  other arithmetic  7.31 us (3%)
    pallas_call x17, Pallas kernels, call(): pl.pallas_call(kernel, name=name, out_shape=list(outs), in_specs=in_specs...  108 us
    ppermute x49, starting transfers between devices, swap(): return lax.ppermute(x, axis, [(i, i ^ bit) for i in range(size)])  48.1 us
    ppermute x49, waiting for transfers between devices, swap(): return lax.ppermute(x, axis, [(i, i ^ bit) for i in range(size)])  29.4 us
    unnamed x138, local copies, waits for them, and re-layouts  10.5 us
    ppermute x6, starting transfers between devices, gather_rows(): up[n] = lax.ppermute(up[n], 'gx', ahead)  6.04 us
    ppermute x6, starting transfers between devices, gather_rows(): down[n] = lax.ppermute(down[n], 'gx', back)  6.02 us
  transfers between devices with their start and end apart: 64, of which 17 were waited for; matrix products, arithmetic and copies ran while one was open for 3% of the time, Pallas kernels for 41%

profile of v2, /device:TPU:0, one launch (start us, length us, event | category | flops | bytes accessed | tf_op | source)
XLA Modules:
  0.0 230.7 jit_solution(1250117635008446201)
XLA Ops:
  0.7 1.7 pack.1
  3.6 3.0 %collective-permute-start.7 = (bf16[1536,384]{1,0:T(8,128)(2,1)S(1)}, bf16[1536,384]{1,0:T(8,128)(2,1)S(1)}, u32[]{:S(2)}, u32[]{:S(2)}) collective-permute-start(bf16[1536,384]{1,0:T(8,128)(2,1)S(1)} %pad_maximum_fusion.refs_4_.refs_6_), channel_id=1, source_target_pairs={{0,2},{1,3},{2,0},{3,1},{4,6},{5,7},{6,4},{7,5},{8,10},{9,11},{10,... | collective-permute-start | bytes 3538952 | tf_op jit(solution)/shard_map/ppermute | solution.py:636
  6.6 1.5 collective-permute-start.1
  8.6 1.5 collective-permute-start.9
  10.6 2.1 place.1
  13.2 1.5 collective-permute-start.2
  16.8 1.5 collective-permute-done.2.refs_4_
  24.8 2.3 %collective-permute-done.5.refs_7_ = bf16[96,320]{1,0:T(8,128)(2,1)S(1)} collective-permute-done((bf16[96,320]{1,0:T(8,128)(2,1)S(1)}, bf16[96,320]{1,0:T(8,128)(2,1)S(1)}, u32[]{:S(2)}, u32[]{:S(2)}) %collective-permute-start.5) | collective-permute-done | bytes 61472 | tf_op jit(solution)/shard_map/ppermute | solution.py:659
  30.1 2.1 unpack.1
  35.0 13.7 %attend.1 = (bf16[1024,768]{1,0:T(8,128)(2,1)}, bf16[1024,576]{1,0:T(8,128)(2,1)}, bf16[30,256,256]{2,1,0:T(8,128)(2,1)}, bf16[1024,192]{1,0:T(8,128)(2,1)}, bf1...) custom-call(s32[1]{0:T(128)} %bitcast.refs_0_.gy_ref, ...), custom_call_target="tpu_custom_call" | custom-call | flops 69000003584 | bytes 1 | tf_op jit(solution)/shard_map/attend/pallas_call | solution.py:46
  49.0 1.5 collective-permute-start.18
  51.1 4.3 %presort.1 = (bf16[320,768]{1,0:T(8,128)(2,1)}, bf16[320,768]{1,0:T(8,128)(2,1)}, f32[320,128]{1,0:T(8,128)}) custom-call(s32[1]{0:T(128)} %bitcast.refs_0_.gy_ref, s32[1,1024]{1,0:T(1,128)} %get-tuple-element.157.refs_7_.pos_ref, bf16[1024,768]{1,0:T(8,128)(2,1)} %x_ref.3, bf16[1024,768]{1,0:T(8,128)(2,1)} %g_ref.3, ...), custom_call_target="tpu_custom_call" | custom-call | flops 5750000128 | bytes 1 | tf_op jit(solution)/shard_map/presort/pallas_call | solution.py:46
  57.6 4.7 %route.1 = (bf16[80,768]{1,0:T(8,128)(2,1)}, bf16[80,768]{1,0:T(8,128)(2,1)}, bf16[80,768]{1,0:T(8,128)(2,1)}, bf16[80,768]{1,0:T(8,128)(2,1)}, bf16[80,768]{1,0...) custom-call(bf16[480,128]{1,0:T(8,128)(2,1)} %get-tuple-element.151., ...), custom_call_target="tpu_custom_call" | custom-call | flops 5750000128 | bytes 1 | tf_op jit(solution)/shard_map/route/pallas_call | solution.py:46
  62.4 1.6 collective-permute-start.23
  64.0 2.6 %collective-permute-start.24 = (bf16[80,768]{1,0:T(8,128)(2,1)}, bf16[80,768]{1,0:T(8,128)(2,1)S(1)}, u32[]{:S(2)}, u32[]{:S(2)}) collective-permute-start(bf16[80,768]{1,0:T(8,128)(2,1)} %get-tuple-element.168.refs_25_), channel_id=1, source_target_pairs={{0,16},{4,20},{8,24},{12,28},{16,0},{20,4},{24,8},{28,12},{1,17},{... | collective-permute-start | bytes 368648 | tf_op jit(solution)/shard_map/ppermute | solution.py:636
  66.8 4.1 %collective-permute-done.23.refs_1_.refs_8_ = bf16[80,768]{1,0:T(8,128)(2,1)S(1)} collective-permute-done((bf16[80,768]{1,0:T(8,128)(2,1)}, bf16[80,768]{1,0:T(8,128)(2,1)S(1)}, u32[]{:S(2)}, u32[]{:S(2)}) %collective-permute-start.23) | collective-permute-done | bytes 122912 | tf_op jit(solution)/shard_map/ppermute | solution.py:636
  70.9 5.6 %collective-permute-done.24.refs_2_.refs_9_ = bf16[80,768]{1,0:T(8,128)(2,1)S(1)} collective-permute-done((bf16[80,768]{1,0:T(8,128)(2,1)}, bf16[80,768]{1,0:T(8,128)(2,1)S(1)}, u32[]{:S(2)}, u32[]{:S(2)}) %collective-permute-start.24) | collective-permute-done | bytes 122912 | tf_op jit(solution)/shard_map/ppermute | solution.py:636
  76.5 2.8 %collective-permute-start.26 = (bf16[80,768]{1,0:T(8,128)(2,1)}, bf16[80,768]{1,0:T(8,128)(2,1)S(1)}, u32[]{:S(2)}, u32[]{:S(2)}) collective-permute-start(bf16[80,768]{1,0:T(8,128)(2,1)} %get-tuple-element.171), channel_id=1, source_target_pairs={{0,8},{4,12},{8,0},{12,4},{16,24},{20,28},{24,16},{28,20},{1,9},{5... | collective-permute-start | bytes 368648 | tf_op jit(solution)/shard_map/ppermute | solution.py:636
  80.3 1.5 collective-permute-start.28
  81.8 6.8 %expert_near.1 = (f32[320,768]{1,0:T(8,128)}, bf16[320,1536]{1,0:T(8,128)(2,1)}, bf16[320,1536]{1,0:T(8,128)(2,1)}) custom-call(bf16[80,768]{1,0:T(8,128)(2,1)} %get-tuple-element.166.refs_0_.refs_7_.refs_23_, bf16[80,768]{1,0:T(8,128)(2,1)} %copy-done.19, bf16[80,768]{1,0:T(8,128)(2,1)} %copy-done.20, bf16[80,768]{1,0:T(8,128)(2,1)} %copy-done.21, ...), custom_call_target="tpu_custom_call" | custom-call | flops 8049999872 | bytes 1 | tf_op jit(solution)/shard_map/expert_near/pallas_call | solution.py:46
  88.6 3.0 %collective-permute-done.27.refs_2_ = bf16[80,768]{1,0:T(8,128)(2,1)S(1)} collective-permute-done((bf16[80,768]{1,0:T(8,128)(2,1)}, bf16[80,768]{1,0:T(8,128)(2,1)S(1)}, u32[]{:S(2)}, u32[]{:S(2)}) %collective-permute-start.27) | collective-permute-done | bytes 122912 | tf_op jit(solution)/shard_map/ppermute | solution.py:636
  91.7 2.8 %collective-permute-done.32.refs_8_.refs_13_ = bf16[1536,384]{1,0:T(8,128)(2,1)S(1)} collective-permute-done((bf16[1536,384]{1,0:T(8,128)(2,1)S(1)}, bf16[1536,384]{1,0:T(8,128)(2,1)S(1)}, u32[]{:S(2)}, u32[]{:S(2)}) %collective-permute-start.32) | collective-permute-done | bytes 1179680 | tf_op jit(solution)/shard_map/ppermute | solution.py:636
  95.6 6.8 %expert_far.1 = (bf16[80,768]{1,0:T(8,128)(2,1)}, bf16[80,768]{1,0:T(8,128)(2,1)}, bf16[80,768]{1,0:T(8,128)(2,1)}, bf16[80,768]{1,0:T(8,128)(2,1)}, bf16[320,15...) custom-call(bf16[80,768]{1,0:T(8,128)(2,1)} %get-tuple-element.166.refs_0_.refs_7_.refs_23_, bf16[80,768]{1,0:T(8,128)(2,1)} %copy-done.19, ...), custom_call_target="tpu_custom_call" | custom-call | flops 8625000448 | bytes 1 | tf_op jit(solution)/shard_map/expert_far/pallas_call | solution.py:46
  102.5 4.6 %outer_out_sent.1 = bf16[4,384,768]{2,1,0:T(8,128)(2,1)} custom-call(bf16[80,768]{1,0:T(8,128)(2,1)} %get-tuple-element.170.refs_0_, bf16[80,768]{1,0:T(8,128)(2,1)} %copy-done.41, bf16[80,768]{1,0:T(8,128)(2,1)} %copy-done.42, bf16[80,768]{1,0:T(8,128)(2,1)} %copy-done.44, bf16[320,1536]{1,0:T(8,128)(2,1)} %get-tuple-element.184.refs_4_, ...), custom_call_target="tpu_custom_call" | custom-call | flops 5405000192 | bytes 1 | tf_op jit(solution)/shard_map/outer_out_sent/pallas_call | solution.py:46
  107.2 1.8 collective-permute-start.37
  110.1 1.5 collective-permute-start.39
  111.7 9.8 %expert_back.1 = (bf16[80,768]{1,0:T(8,128)(2,1)}, bf16[80,768]{1,0:T(8,128)(2,1)}, bf16[80,768]{1,0:T(8,128)(2,1)}, bf16[80,768]{1,0:T(8,128)(2,1)}, bf16[320,3072]{1,0:T(8,128)(2,1)}) custom-call(bf16[80,768]{1,0:T(8,128)(2,1)} %get-tuple-element.170.refs_0_, bf16[80,768]{1,0:T(8,128)(2,1)} %copy-done.41, bf16[80,768]{1,0:T(8,128)(2,1)} %copy-done.42, ...), custom_call_target="tpu_custom_call" | custom-call | flops 13799999488 | bytes 1 | tf_op jit(solution)/shard_map/expert_back/pallas_call | solution.py:46
  122.4 1.9 collective-permute-start.34
  124.4 1.5 collective-permute-start.35
  127.4 9.0 %fill_rows.1 = (f32[384,768]{1,0:T(8,128)}, bf16[384,768]{1,0:T(8,128)(2,1)}, bf16[384,768]{1,0:T(8,128)(2,1)}, bf16[384,768]{1,0:T(8,128)(2,1)}, bf16[4,768,384...) custom-call(bf16[80,768]{1,0:T(8,128)(2,1)} %get-tuple-element.170.refs_0_, ...), custom_call_target="tpu_custom_call" | custom-call | flops 14949999616 | bytes 1 | tf_op jit(solution)/shard_map/fill_rows/pallas_call | solution.py:46
  138.1 5.2 %combine.1 = (bf16[480,128]{1,0:T(8,128)(2,1)}, bf16[480,128]{1,0:T(8,128)(2,1)}, bf16[480,128]{1,0:T(8,128)(2,1)}, bf16[480,128]{1,0:T(8,128)(2,1)}, bf16[320,7...) custom-call(bf16[80,768]{1,0:T(8,128)(2,1)} %get-tuple-element.187.refs_0_, ...), custom_call_target="tpu_custom_call" | custom-call | flops 46000001024 | bytes 1 | tf_op jit(solution)/shard_map/combine/pallas_call | solution.py:46
  146.2 5.1 %outer_in_held.1 = (f32[768,384]{1,0:T(8,128)}, bf16[768,384]{1,0:T(8,128)(2,1)}, bf16[768,384]{1,0:T(8,128)(2,1)}, bf16[768,384]{1,0:T(8,128)(2,1)}) custom-call(bf16[80,768]{1,0:T(8,128)(2,1)} %get-tuple-element.166.refs_0_.refs_7_.refs_23_, bf16[80,768]{1,0:T(8,128)(2,1)} %copy-done.19, bf16[80,768]{1,0:T(8,128)(2,1)} %copy-done.20, ...), custom_call_target="tpu_custom_call" | custom-call | flops 1150000000 | bytes 1 | tf_op jit(solution)/shard_map/outer_in_held/pallas_call | solution.py:46
  151.3 1.7 collective-permute-start.48
  154.9 3.6 %all-to-all-start = ((bf16[8,96,384]{2,1,0:T(8,128)(2,1)}), bf16[8,96,384]{2,1,0:T(8,128)(2,1)S(1)}, u32[]{:S(2)}, u32[]{:S(2)}) async-start(bf16[8,96,384]{2,1,0:T(8,128)(2,1)} %bitcast.12), calls=%async_computation | async-start | bytes 1179648 | tf_op jit(solution)/shard_map/all_to_all | solution.py:992
  160.6 2.0 collective-permute-start.46
  162.5 19.6 %attend_back.1 = (bf16[4,96,640]{2,1,0:T(8,128)(2,1)}, bf16[4,96,640]{2,1,0:T(8,128)(2,1)}, bf16[2,256,768]{2,1,0:T(8,128)(2,1)}, bf16[2,256,768]{2,1,0:T(8,128)(2,1)}, f32[32,8]{1,0:T(8,128)}) custom-call(s32[1]{0:T(128)} %bitcast.refs_0_.gy_ref, s32[1]{0:T(128)} %bitcast.1.gx_ref.refs_0_.refs_1_, bf16[480,128]{1,0:T(8,128)(2,1)} %get-tuple-element.212.refs_2_, ...), custom_call_target="tpu_custom_call" | custom-call | flops 69000003584 | bytes 1 | tf_op jit(solution)/shard_map/attend_back/pallas_call | solution.py:46
  182.2 2.0 collective-permute-done.47
  184.2 1.8 collective-permute-done.46
  186.0 1.7 collective-permute-start.54
  194.4 7.2 %unsort.1 = f32[1024,768]{1,0:T(8,128)} custom-call(s32[1]{0:T(128)} %bitcast.refs_0_.gy_ref, s32[1024,1]{1,0:T(8,128)} %get-tuple-element.141.refs_6_.pos_ref, bf16[1024,768]{1,0:T(8,128)(2,1)} %x_ref.3, bf16[320,768]{1,0:T(8,128)(2,1)} %get-tuple-element.242.d0_ref, bf16[320,768]{1,0:T(8,128)(2,1)} %copy-done.14, bf16[320,768]{1,0:T(8,128)(2,1)} %copy-done.12, ...), custom_call_target="tpu_custom_call" | custom-call | flops 1150000000 | bytes 1 | tf_op jit(solution)/shard_map/unsort/pallas_call | solution.py:46
  201.8 2.4 %collective-permute-start.57 = (bf16[96,640]{1,0:T(8,128)(2,1)S(1)}, bf16[96,640]{1,0:T(8,128)(2,1)S(1)}, u32[]{:S(2)}, u32[]{:S(2)}) collective-permute-start(bf16[96,640]{1,0:T(8,128)(2,1)S(1)} %get-tuple-element.268), channel_id=1, source_target_pairs={{0,24},{4,28},{8,16},{12,20},{16,8},{20,12},{24,0},{28,4},{1,25},{... | collective-permute-start | bytes 368648 | tf_op jit(solution)/shard_map/ppermute | solution.py:636
  204.2 2.1 collective-permute-start.55
  207.5 2.5 %collective-permute-done.57 = bf16[96,640]{1,0:T(8,128)(2,1)S(1)} collective-permute-done((bf16[96,640]{1,0:T(8,128)(2,1)S(1)}, bf16[96,640]{1,0:T(8,128)(2,1)S(1)}, u32[]{:S(2)}, u32[]{:S(2)}) %collective-permute-start.57) | collective-permute-done | bytes 122912 | tf_op jit(solution)/shard_map/ppermute | solution.py:636
  211.1 3.2 %collective-permute-done.56 = bf16[96,640]{1,0:T(8,128)(2,1)S(1)} collective-permute-done((bf16[96,640]{1,0:T(8,128)(2,1)S(1)}, bf16[96,640]{1,0:T(8,128)(2,1)S(1)}, u32[]{:S(2)}, u32[]{:S(2)}) %collective-permute-start.56) | collective-permute-done | bytes 122912 | tf_op jit(solution)/shard_map/ppermute | solution.py:636
  219.0 3.9 %finish.1 = f32[1024,768]{1,0:T(8,128)} custom-call(s32[1]{0:T(128)} %bitcast.refs_0_.gy_ref, bf16[2,256,768]{2,1,0:T(8,128)(2,1)} %copy-done, bf16[2,256,768]{2,1,0:T(8,128)(2,1)} %copy-done.5, bf16[1024,768]{1,0:T(8,128)(2,1)} %g_ref.3), custom_call_target="tpu_custom_call" | custom-call | flops 1150000000 | bytes 1 | tf_op jit(solution)/shard_map/finish/pallas_call | solution.py:46
  222.9 1.7 collective-permute-done.61
  226.6 1.7 close.1
  228.3 2.2 add_bitcast_fusion.1
  (263 shorter events, 50.4 us)
Async XLA Ops:
  3.6 29.6 %collective-permute-start.7 = (bf16[1536,384]{1,0:T(8,128)(2,1)S(1)}, bf16[1536,384]{1,0:T(8,128)(2,1)S(1)}, u32[]{:S(2)}, u32[]{:S(2)}) collective-permute-start(bf16[1536,384]{1,0:T(8,128)(2,1)S(1)} %pad_maximum_fusion.refs_4_.refs_6_), channel_id=1, source_target_pairs={{0,2},{1,3},{2,0},{3,1},{4,6},{5,7},{6,4},{7,5},{8,10},{9,11},{10,... | collective-permute-start | bytes 3538952 | tf_op jit(solution)/shard_map/ppermute | solution.py:636
  6.6 8.2 %collective-permute-start.1 = (bf16[96,320]{1,0:T(8,128)(2,1)S(1)}, bf16[96,320]{1,0:T(8,128)(2,1)S(1)}, u32[]{:S(2)}, u32[]{:S(2)}) collective-permute-start(bf16[96,320]{1,0:T(8,128)(2,1)S(1)} %copy-done.61), channel_id=1, source_target_pairs={{8,0},{16,8},{24,16},{28,24},{20,28},{12,20},{4,12},{0,4},{9,1},{1... | collective-permute-start | bytes 184328 | tf_op jit(solution)/shard_map/ppermute | solution.py:659
  8.6 12.2 %collective-permute-start.9 = (bf16[96,576]{1,0:T(8,128)(2,1)S(1)}, bf16[96,576]{1,0:T(8,128)(2,1)S(1)}, u32[]{:S(2)}, u32[]{:S(2)}) collective-permute-start(bf16[96,576]{1,0:T(8,128)(2,1)S(1)} %copy-done.38), channel_id=1, source_target_pairs={{8,0},{16,8},{24,16},{28,24},{20,28},{12,20},{4,12},{0,4},{9,1},{1... | collective-permute-start | bytes 331784 | tf_op jit(solution)/shard_map/ppermute | solution.py:659
  14.8 8.0 %collective-permute-start.3 = (bf16[96,320]{1,0:T(8,128)(2,1)S(1)}, bf16[96,320]{1,0:T(8,128)(2,1)S(1)}, u32[]{:S(2)}, u32[]{:S(2)}) collective-permute-start(bf16[96,320]{1,0:T(8,128)(2,1)S(1)} %collective-permute-done.1.refs_3_), channel_id=1, source_target_pairs={{8,0},{16,8},{24,16},{28,24},{20,28},{12,20},{4,12},{0,4},{9,1},{1... | collective-permute-start | bytes 184328 | tf_op jit(solution)/shard_map/ppermute | solution.py:659
  20.8 6.4 %collective-permute-start.11 = (bf16[96,576]{1,0:T(8,128)(2,1)S(1)}, bf16[96,576]{1,0:T(8,128)(2,1)S(1)}, u32[]{:S(2)}, u32[]{:S(2)}) collective-permute-start(bf16[96,576]{1,0:T(8,128)(2,1)S(1)} %collective-permute-done.9.refs_10_), channel_id=1, source_target_pairs={{8,0},{16,8},{24,16},{28,24},{20,28},{12,20},{4,12},{0,4},{9,1},{1... | collective-permute-start | bytes 331784 | tf_op jit(solution)/shard_map/ppermute | solution.py:659
  21.6 6.5 %collective-permute-start.12 = (bf16[96,576]{1,0:T(8,128)(2,1)S(1)}, bf16[96,576]{1,0:T(8,128)(2,1)}, u32[]{:S(2)}, u32[]{:S(2)}) collective-permute-start(bf16[96,576]{1,0:T(8,128)(2,1)S(1)} %collective-permute-done.10.refs_11_), channel_id=1, source_target_pairs={{0,8},{8,16},{16,24},{24,28},{28,20},{20,12},{12,4},{4,0},{1,9},{9... | collective-permute-start | bytes 331784 | tf_op jit(solution)/shard_map/ppermute | solution.py:658
  27.2 23.3 %collective-permute-start.15 = (bf16[1536,384]{1,0:T(8,128)(2,1)S(1)}, bf16[1536,384]{1,0:T(8,128)(2,1)S(1)}, u32[]{:S(2)}, u32[]{:S(2)}) collective-permute-start(bf16[1536,384]{1,0:T(8,128)(2,1)S(1)} %pad_maximum_fusion.refs_4_.refs_6_), channel_id=1, source_target_pairs={{0,1},{1,0},{2,3},{3,2},{4,5},{5,4},{6,7},{7,6},{8,9},{9,8},{10,11... | collective-permute-start | bytes 3538952 | tf_op jit(solution)/shard_map/ppermute | solution.py:636
  28.0 6.4 %collective-permute-start.14 = (bf16[96,576]{1,0:T(8,128)(2,1)}, bf16[96,576]{1,0:T(8,128)(2,1)S(1)}, u32[]{:S(2)}, u32[]{:S(2)}) collective-permute-start(bf16[96,576]{1,0:T(8,128)(2,1)} %collective-permute-done.12.refs_13_), channel_id=1, source_target_pairs={{0,8},{8,16},{16,24},{24,28},{28,20},{20,12},{12,4},{4,0},{1,9},{9... | collective-permute-start | bytes 331784 | tf_op jit(solution)/shard_map/ppermute | solution.py:663
  32.2 16.5 %collective-permute-start.21 = (bf16[768,192]{1,0:T(8,128)(2,1)}, bf16[768,192]{1,0:T(8,128)(2,1)S(1)}, u32[]{:S(2)}, u32[]{:S(2)}) collective-permute-start(bf16[768,192]{1,0:T(8,128)(2,1)} %get-tuple-element.155.refs_4_.refs_9_), channel_id=1, source_target_pairs={{0,2},{1,3},{2,0},{3,1},{4,6},{5,7},{6,4},{7,5},{8,10},{9,11},{10,... | collective-permute-start | bytes 884744 | tf_op jit(solution)/shard_map/ppermute | solution.py:636
  33.2 15.8 %collective-permute-start.20 = (bf16[768,192]{1,0:T(8,128)(2,1)}, bf16[768,192]{1,0:T(8,128)(2,1)S(1)}, u32[]{:S(2)}, u32[]{:S(2)}) collective-permute-start(bf16[768,192]{1,0:T(8,128)(2,1)} %get-tuple-element.155.refs_4_.refs_9_), channel_id=1, source_target_pairs={{0,1},{1,0},{2,3},{3,2},{4,5},{5,4},{6,7},{7,6},{8,9},{9,8},{10,11... | collective-permute-start | bytes 884744 | tf_op jit(solution)/shard_map/ppermute | solution.py:636
  33.2 33.6 %collective-permute-start.30 = (bf16[1536,384]{1,0:T(8,128)(2,1)S(1)}, bf16[1536,384]{1,0:T(8,128)(2,1)S(1)}, u32[]{:S(2)}, u32[]{:S(2)}) collective-permute-start(bf16[1536,384]{1,0:T(8,128)(2,1)S(1)} %pad_maximum_fusion.refs_4_.refs_6_), channel_id=1, source_target_pairs={{0,4},{4,0},{8,12},{12,8},{16,20},{20,16},{24,28},{28,24},{1,5},{5... | collective-permute-start | bytes 3538952 | tf_op jit(solution)/shard_map/ppermute | solution.py:636
  34.4 16.3 %collective-permute-start.16 = (bf16[1536,384]{1,0:T(8,128)(2,1)S(1)}, bf16[1536,384]{1,0:T(8,128)(2,1)S(1)}, u32[]{:S(2)}, u32[]{:S(2)}) collective-permute-start(bf16[1536,384]{1,0:T(8,128)(2,1)S(1)} %collective-permute-done.7.refs_6_.refs_8_), channel_id=1, source_target_pairs={{0,1},{1,0},{2,3},{3,2},{4,5},{5,4},{6,7},{7,6},{8,9},{9,8},{10,11... | collective-permute-start | bytes 3538952 | tf_op jit(solution)/shard_map/ppermute | solution.py:636
  48.7 6.7 %collective-permute-start.17 = (bf16[480,128]{1,0:T(8,128)(2,1)}, bf16[480,128]{1,0:T(8,128)(2,1)S(1)}, u32[]{:S(2)}, u32[]{:S(2)}) collective-permute-start(bf16[480,128]{1,0:T(8,128)(2,1)} %get-tuple-element.152), channel_id=1, source_target_pairs={{0,1},{1,0},{2,3},{3,2},{4,5},{5,4},{6,7},{7,6},{8,9},{9,8},{10,11... | collective-permute-start | bytes 368648 | tf_op jit(solution)/shard_map/ppermute | solution.py:636
  49.0 7.3 %collective-permute-start.18 = (bf16[480,128]{1,0:T(8,128)(2,1)}, bf16[480,128]{1,0:T(8,128)(2,1)S(1)}, u32[]{:S(2)}, u32[]{:S(2)}) collective-permute-start(bf16[480,128]{1,0:T(8,128)(2,1)} %get-tuple-element.153), channel_id=1, source_target_pairs={{0,2},{1,3},{2,0},{3,1},{4,6},{5,7},{6,4},{7,5},{8,10},{9,11},{10,... | collective-permute-start | bytes 368648 | tf_op jit(solution)/shard_map/ppermute | solution.py:636
  55.5 33.1 %collective-permute-start.29 = (bf16[1536,384]{1,0:T(8,128)(2,1)S(1)}, bf16[1536,384]{1,0:T(8,128)(2,1)S(1)}, u32[]{:S(2)}, u32[]{:S(2)}) collective-permute-start(bf16[1536,384]{1,0:T(8,128)(2,1)S(1)} %collective-permute-done.7.refs_6_.refs_8_), channel_id=1, source_target_pairs={{0,4},{4,0},{8,12},{12,8},{16,20},{20,16},{24,28},{28,24},{1,5},{5... | collective-permute-start | bytes 3538952 | tf_op jit(solution)/shard_map/ppermute | solution.py:636
  62.4 8.6 %collective-permute-start.23 = (bf16[80,768]{1,0:T(8,128)(2,1)}, bf16[80,768]{1,0:T(8,128)(2,1)S(1)}, u32[]{:S(2)}, u32[]{:S(2)}) collective-permute-start(bf16[80,768]{1,0:T(8,128)(2,1)} %get-tuple-element.167.refs_24_), channel_id=1, source_target_pairs={{0,8},{4,12},{8,0},{12,4},{16,24},{20,28},{24,16},{28,20},{1,9},{5... | collective-permute-start | bytes 368648 | tf_op jit(solution)/shard_map/ppermute | solution.py:636
  64.0 12.5 %collective-permute-start.24 = (bf16[80,768]{1,0:T(8,128)(2,1)}, bf16[80,768]{1,0:T(8,128)(2,1)S(1)}, u32[]{:S(2)}, u32[]{:S(2)}) collective-permute-start(bf16[80,768]{1,0:T(8,128)(2,1)} %get-tuple-element.168.refs_25_), channel_id=1, source_target_pairs={{0,16},{4,20},{8,24},{12,28},{16,0},{20,4},{24,8},{28,12},{1,17},{... | collective-permute-start | bytes 368648 | tf_op jit(solution)/shard_map/ppermute | solution.py:636
  66.6 10.0 %collective-permute-start.25 = (bf16[80,768]{1,0:T(8,128)(2,1)}, bf16[80,768]{1,0:T(8,128)(2,1)S(1)}, u32[]{:S(2)}, u32[]{:S(2)}) collective-permute-start(bf16[80,768]{1,0:T(8,128)(2,1)} %get-tuple-element.169.refs_26_), channel_id=1, source_target_pairs={{0,24},{4,28},{8,16},{12,20},{16,8},{20,12},{24,0},{28,4},{1,25},{... | collective-permute-start | bytes 368648 | tf_op jit(solution)/shard_map/ppermute | solution.py:636
  66.8 24.9 %collective-permute-start.31 = (bf16[1536,384]{1,0:T(8,128)(2,1)S(1)}, bf16[1536,384]{1,0:T(8,128)(2,1)S(1)}, u32[]{:S(2)}, u32[]{:S(2)}) collective-permute-start(bf16[1536,384]{1,0:T(8,128)(2,1)S(1)} %collective-permute-done.30.refs_5_.refs_10_), channel_id=1, source_target_pairs={{0,1},{1,0},{2,3},{3,2},{4,5},{5,4},{6,7},{7,6},{8,9},{9,8},{10,11... | collective-permute-start | bytes 3538952 | tf_op jit(solution)/shard_map/ppermute | solution.py:636
  76.5 12.1 %collective-permute-start.26 = (bf16[80,768]{1,0:T(8,128)(2,1)}, bf16[80,768]{1,0:T(8,128)(2,1)S(1)}, u32[]{:S(2)}, u32[]{:S(2)}) collective-permute-start(bf16[80,768]{1,0:T(8,128)(2,1)} %get-tuple-element.171), channel_id=1, source_target_pairs={{0,8},{4,12},{8,0},{12,4},{16,24},{20,28},{24,16},{28,20},{1,9},{5... | collective-permute-start | bytes 368648 | tf_op jit(solution)/shard_map/ppermute | solution.py:636
  79.3 12.4 %collective-permute-start.27 = (bf16[80,768]{1,0:T(8,128)(2,1)}, bf16[80,768]{1,0:T(8,128)(2,1)S(1)}, u32[]{:S(2)}, u32[]{:S(2)}) collective-permute-start(bf16[80,768]{1,0:T(8,128)(2,1)} %get-tuple-element.172), channel_id=1, source_target_pairs={{0,16},{4,20},{8,24},{12,28},{16,0},{20,4},{24,8},{28,12},{1,17},{... | collective-permute-start | bytes 368648 | tf_op jit(solution)/shard_map/ppermute | solution.py:636
  80.3 11.3 %collective-permute-start.28 = (bf16[80,768]{1,0:T(8,128)(2,1)}, bf16[80,768]{1,0:T(8,128)(2,1)S(1)}, u32[]{:S(2)}, u32[]{:S(2)}) collective-permute-start(bf16[80,768]{1,0:T(8,128)(2,1)} %get-tuple-element.173), channel_id=1, source_target_pairs={{0,24},{4,28},{8,16},{12,20},{16,8},{20,12},{24,0},{28,4},{1,25},{... | collective-permute-start | bytes 368648 | tf_op jit(solution)/shard_map/ppermute | solution.py:636
  107.1 18.8 %collective-permute-start.36 = (bf16[4,384,768]{2,1,0:T(8,128)(2,1)}, bf16[4,384,768]{2,1,0:T(8,128)(2,1)S(1)}, u32[]{:S(2)}, u32[]{:S(2)}) collective-permute-start(bf16[4,384,768]{2,1,0:T(8,128)(2,1)} %outer_out_sent.1), channel_id=1, source_target_pairs={{0,1},{1,0},{2,3},{3,2},{4,5},{5,4},{6,7},{7,6},{8,9},{9,8},{10,11... | collective-permute-start | bytes 7077896 | tf_op jit(solution)/shard_map/ppermute | solution.py:636
  107.2 15.2 %collective-permute-start.37 = (bf16[80,768]{1,0:T(8,128)(2,1)S(1)}, bf16[80,768]{1,0:T(8,128)(2,1)S(1)}, u32[]{:S(2)}, u32[]{:S(2)}) collective-permute-start(bf16[80,768]{1,0:T(8,128)(2,1)S(1)} %copy-done.59), channel_id=1, source_target_pairs={{0,8},{4,12},{8,0},{12,4},{16,24},{20,28},{24,16},{28,20},{1,9},{5... | collective-permute-start | bytes 368648 | tf_op jit(solution)/shard_map/ppermute | solution.py:636
  109.1 15.3 %collective-permute-start.38 = (bf16[80,768]{1,0:T(8,128)(2,1)S(1)}, bf16[80,768]{1,0:T(8,128)(2,1)S(1)}, u32[]{:S(2)}, u32[]{:S(2)}) collective-permute-start(bf16[80,768]{1,0:T(8,128)(2,1)S(1)} %copy-done.58), channel_id=1, source_target_pairs={{0,16},{4,20},{8,24},{12,28},{16,0},{20,4},{24,8},{28,12},{1,17},{... | collective-permute-start | bytes 368648 | tf_op jit(solution)/shard_map/ppermute | solution.py:636
  110.1 15.8 %collective-permute-start.39 = (bf16[80,768]{1,0:T(8,128)(2,1)S(1)}, bf16[80,768]{1,0:T(8,128)(2,1)S(1)}, u32[]{:S(2)}, u32[]{:S(2)}) collective-permute-start(bf16[80,768]{1,0:T(8,128)(2,1)S(1)} %copy-done.57), channel_id=1, source_target_pairs={{0,24},{4,28},{8,16},{12,20},{16,8},{20,12},{24,0},{28,4},{1,25},{... | collective-permute-start | bytes 368648 | tf_op jit(solution)/shard_map/ppermute | solution.py:636
  121.5 15.9 %collective-permute-start.33 = (bf16[80,768]{1,0:T(8,128)(2,1)}, bf16[80,768]{1,0:T(8,128)(2,1)S(1)}, u32[]{:S(2)}, u32[]{:S(2)}) collective-permute-start(bf16[80,768]{1,0:T(8,128)(2,1)} %get-tuple-element.188), channel_id=1, source_target_pairs={{0,8},{4,12},{8,0},{12,4},{16,24},{20,28},{24,16},{28,20},{1,9},{5... | collective-permute-start | bytes 368648 | tf_op jit(solution)/shard_map/ppermute | solution.py:636
  122.4 14.9 %collective-permute-start.34 = (bf16[80,768]{1,0:T(8,128)(2,1)}, bf16[80,768]{1,0:T(8,128)(2,1)S(1)}, u32[]{:S(2)}, u32[]{:S(2)}) collective-permute-start(bf16[80,768]{1,0:T(8,128)(2,1)} %get-tuple-element.189), channel_id=1, source_target_pairs={{0,16},{4,20},{8,24},{12,28},{16,0},{20,4},{24,8},{28,12},{1,17},{... | collective-permute-start | bytes 368648 | tf_op jit(solution)/shard_map/ppermute | solution.py:636
  124.4 13.0 %collective-permute-start.35 = (bf16[80,768]{1,0:T(8,128)(2,1)}, bf16[80,768]{1,0:T(8,128)(2,1)S(1)}, u32[]{:S(2)}, u32[]{:S(2)}) collective-permute-start(bf16[80,768]{1,0:T(8,128)(2,1)} %get-tuple-element.190), channel_id=1, source_target_pairs={{0,24},{4,28},{8,16},{12,20},{16,8},{20,12},{24,0},{28,4},{1,25},{... | collective-permute-start | bytes 368648 | tf_op jit(solution)/shard_map/ppermute | solution.py:636
  136.4 16.7 %collective-permute-start.41 = (bf16[384,768]{1,0:T(8,128)(2,1)}, bf16[384,768]{1,0:T(8,128)(2,1)S(1)}, u32[]{:S(2)}, u32[]{:S(2)}) collective-permute-start(bf16[384,768]{1,0:T(8,128)(2,1)} %get-tuple-element.206), channel_id=1, source_target_pairs={{0,4},{4,0},{8,12},{12,8},{16,20},{20,16},{24,28},{28,24},{1,5},{5... | collective-permute-start | bytes 1769480 | tf_op jit(solution)/shard_map/ppermute | solution.py:636
  137.4 7.5 %collective-permute-start.40 = (bf16[4,768,384]{2,1,0:T(8,128)(2,1)}, bf16[4,768,384]{2,1,0:T(8,128)(2,1)S(1)}, u32[]{:S(2)}, u32[]{:S(2)}) collective-permute-start(bf16[4,768,384]{2,1,0:T(8,128)(2,1)} %get-tuple-element.203), channel_id=1, source_target_pairs={{0,1},{1,0},{2,3},{3,2},{4,5},{5,4},{6,7},{7,6},{8,9},{9,8},{10,11... | collective-permute-start | bytes 7077896 | tf_op jit(solution)/shard_map/ppermute | solution.py:636
  143.3 10.6 %collective-permute-start.42 = (bf16[768,384]{1,0:T(8,128)(2,1)}, bf16[768,384]{1,0:T(8,128)(2,1)S(1)}, u32[]{:S(2)}, u32[]{:S(2)}) collective-permute-start(bf16[768,384]{1,0:T(8,128)(2,1)} %get-tuple-element.211), channel_id=1, source_target_pairs={{0,1},{1,0},{2,3},{3,2},{4,5},{5,4},{6,7},{7,6},{8,9},{9,8},{10,11... | collective-permute-start | bytes 1769480 | tf_op jit(solution)/shard_map/ppermute | solution.py:636
  143.8 7.5 %collective-permute-start.43 = (bf16[480,128]{1,0:T(8,128)(2,1)}, bf16[480,128]{1,0:T(8,128)(2,1)S(1)}, u32[]{:S(2)}, u32[]{:S(2)}) collective-permute-start(bf16[480,128]{1,0:T(8,128)(2,1)} %get-tuple-element.213), channel_id=1, source_target_pairs={{0,1},{1,0},{2,3},{3,2},{4,5},{5,4},{6,7},{7,6},{8,9},{9,8},{10,11... | collective-permute-start | bytes 368648 | tf_op jit(solution)/shard_map/ppermute | solution.py:636
  143.9 9.2 %collective-permute-start.44 = (bf16[480,128]{1,0:T(8,128)(2,1)}, bf16[480,128]{1,0:T(8,128)(2,1)S(1)}, u32[]{:S(2)}, u32[]{:S(2)}) collective-permute-start(bf16[480,128]{1,0:T(8,128)(2,1)} %get-tuple-element.214), channel_id=1, source_target_pairs={{0,2},{1,3},{2,0},{3,1},{4,6},{5,7},{6,4},{7,5},{8,10},{9,11},{10,... | collective-permute-start | bytes 368648 | tf_op jit(solution)/shard_map/ppermute | solution.py:636
  144.8 8.2 %collective-permute-start.45 = (bf16[480,128]{1,0:T(8,128)(2,1)}, bf16[480,128]{1,0:T(8,128)(2,1)S(1)}, u32[]{:S(2)}, u32[]{:S(2)}) collective-permute-start(bf16[480,128]{1,0:T(8,128)(2,1)} %get-tuple-element.215), channel_id=1, source_target_pairs={{0,3},{1,2},{2,1},{3,0},{4,7},{5,6},{6,5},{7,4},{8,11},{9,10},{10,... | collective-permute-start | bytes 368648 | tf_op jit(solution)/shard_map/ppermute | solution.py:636
  151.3 30.8 %collective-permute-start.48 = (bf16[384,768]{1,0:T(8,128)(2,1)}, bf16[384,768]{1,0:T(8,128)(2,1)S(1)}, u32[]{:S(2)}, u32[]{:S(2)}) collective-permute-start(bf16[384,768]{1,0:T(8,128)(2,1)} %get-tuple-element.229), channel_id=1, source_target_pairs={{0,4},{4,0},{8,12},{12,8},{16,20},{20,16},{24,28},{28,24},{1,5},{5... | collective-permute-start | bytes 1769480 | tf_op jit(solution)/shard_map/ppermute | solution.py:636
  154.9 31.0 %all-to-all-start = ((bf16[8,96,384]{2,1,0:T(8,128)(2,1)}), bf16[8,96,384]{2,1,0:T(8,128)(2,1)S(1)}, u32[]{:S(2)}, u32[]{:S(2)}) async-start(bf16[8,96,384]{2,1,0:T(8,128)(2,1)} %bitcast.12), calls=%async_computation | async-start | bytes 1179648 | tf_op jit(solution)/shard_map/all_to_all | solution.py:992
  158.5 23.7 %collective-permute-start.49 = (bf16[320,768]{1,0:T(8,128)(2,1)S(1)}, bf16[320,768]{1,0:T(8,128)(2,1)S(1)}, u32[]{:S(2)}, u32[]{:S(2)}) collective-permute-start(bf16[320,768]{1,0:T(8,128)(2,1)S(1)} %copy-done.11), channel_id=1, source_target_pairs={{0,2},{1,3},{2,0},{3,1},{4,6},{5,7},{6,4},{7,5},{8,10},{9,11},{10,... | collective-permute-start | bytes 1474568 | tf_op jit(solution)/shard_map/ppermute | solution.py:636
  159.4 24.7 %collective-permute-start.47 = (bf16[384,768]{1,0:T(8,128)(2,1)S(1)}, bf16[384,768]{1,0:T(8,128)(2,1)S(1)}, u32[]{:S(2)}, u32[]{:S(2)}) collective-permute-start(bf16[384,768]{1,0:T(8,128)(2,1)S(1)} %add_convert_fusion.4), channel_id=1, source_target_pairs={{0,2},{1,3},{2,0},{3,1},{4,6},{5,7},{6,4},{7,5},{8,10},{9,11},{10,... | collective-permute-start | bytes 1769480 | tf_op jit(solution)/shard_map/ppermute | solution.py:636
  160.6 25.4 %collective-permute-start.46 = (bf16[768,384]{1,0:T(8,128)(2,1)}, bf16[768,384]{1,0:T(8,128)(2,1)S(1)}, u32[]{:S(2)}, u32[]{:S(2)}) collective-permute-start(bf16[768,384]{1,0:T(8,128)(2,1)} %get-tuple-element.227), channel_id=1, source_target_pairs={{0,4},{4,0},{8,12},{12,8},{16,20},{20,16},{24,28},{28,24},{1,5},{5... | collective-permute-start | bytes 1769480 | tf_op jit(solution)/shard_map/ppermute | solution.py:636
  186.0 15.6 %collective-permute-start.54 = (bf16[4,96,640]{2,1,0:T(8,128)(2,1)}, bf16[4,96,640]{2,1,0:T(8,128)(2,1)S(1)}, u32[]{:S(2)}, u32[]{:S(2)}) collective-permute-start(bf16[4,96,640]{2,1,0:T(8,128)(2,1)} %get-tuple-element.246), channel_id=1, source_target_pairs={{0,4},{4,0},{8,12},{12,8},{16,20},{20,16},{24,28},{28,24},{1,5},{5... | collective-permute-start | bytes 1474568 | tf_op jit(solution)/shard_map/ppermute | solution.py:636
  191.6 22.8 %collective-permute-start.53 = (bf16[2,256,768]{2,1,0:T(8,128)(2,1)S(1)}, bf16[2,256,768]{2,1,0:T(8,128)(2,1)S(1)}, u32[]{:S(2)}, u32[]{:S(2)}) collective-permute-start(bf16[2,256,768]{2,1,0:T(8,128)(2,1)S(1)} %add_convert_fusion.1), channel_id=1, source_target_pairs={{0,2},{1,3},{2,0},{3,1},{4,6},{5,7},{6,4},{7,5},{8,10},{9,11},{10,... | collective-permute-start | bytes 2359304 | tf_op jit(solution)/shard_map/ppermute | solution.py:636
  201.8 8.1 %collective-permute-start.57 = (bf16[96,640]{1,0:T(8,128)(2,1)S(1)}, bf16[96,640]{1,0:T(8,128)(2,1)S(1)}, u32[]{:S(2)}, u32[]{:S(2)}) collective-permute-start(bf16[96,640]{1,0:T(8,128)(2,1)S(1)} %get-tuple-element.268), channel_id=1, source_target_pairs={{0,24},{4,28},{8,16},{12,20},{16,8},{20,12},{24,0},{28,4},{1,25},{... | collective-permute-start | bytes 368648 | tf_op jit(solution)/shard_map/ppermute | solution.py:636
  204.2 10.1 %collective-permute-start.56 = (bf16[96,640]{1,0:T(8,128)(2,1)S(1)}, bf16[96,640]{1,0:T(8,128)(2,1)S(1)}, u32[]{:S(2)}, u32[]{:S(2)}) collective-permute-start(bf16[96,640]{1,0:T(8,128)(2,1)S(1)} %get-tuple-element.269), channel_id=1, source_target_pairs={{0,16},{4,20},{8,24},{12,28},{16,0},{20,4},{24,8},{28,12},{1,17},{... | collective-permute-start | bytes 368648 | tf_op jit(solution)/shard_map/ppermute | solution.py:636
  204.2 10.1 %collective-permute-start.55 = (bf16[96,640]{1,0:T(8,128)(2,1)S(1)}, bf16[96,640]{1,0:T(8,128)(2,1)S(1)}, u32[]{:S(2)}, u32[]{:S(2)}) collective-permute-start(bf16[96,640]{1,0:T(8,128)(2,1)S(1)} %get-tuple-element.270), channel_id=1, source_target_pairs={{0,8},{4,12},{8,0},{12,4},{16,24},{20,28},{24,16},{28,20},{1,9},{5... | collective-permute-start | bytes 368648 | tf_op jit(solution)/shard_map/ppermute | solution.py:636
  206.5 18.1 %collective-permute-start.61 = (bf16[768,384]{1,0:T(8,128)(2,1)S(1)}, bf16[768,384]{1,0:T(8,128)(2,1)S(1)}, u32[]{:S(2)}, u32[]{:S(2)}) collective-permute-start(bf16[768,384]{1,0:T(8,128)(2,1)S(1)} %add_convert_fusion.2), channel_id=1, source_target_pairs={{0,2},{1,3},{2,0},{3,1},{4,6},{5,7},{6,4},{7,5},{8,10},{9,11},{10,... | collective-permute-start | bytes 1769480 | tf_op jit(solution)/shard_map/ppermute | solution.py:636
  210.0 14.6 %collective-permute-start.62 = (bf16[768,384]{1,0:T(8,128)(2,1)}, bf16[768,384]{1,0:T(8,128)(2,1)}, u32[]{:S(2)}, u32[]{:S(2)}) collective-permute-start(bf16[768,384]{1,0:T(8,128)(2,1)} %get-tuple-element.260), channel_id=1, source_target_pairs={{0,4},{4,0},{8,12},{12,8},{16,20},{20,16},{24,28},{28,24},{1,5},{5... | collective-permute-start | bytes 1769480 | tf_op jit(solution)/shard_map/ppermute | solution.py:636
  217.2 8.8 %collective-permute-start.60 = (f32[96,256]{1,0:T(8,128)S(1)}, f32[96,256]{1,0:T(8,128)S(1)}, u32[]{:S(2)}, u32[]{:S(2)}) collective-permute-start(f32[96,256]{1,0:T(8,128)S(1)} %pad_maximum_fusion.1), channel_id=1, source_target_pairs={{0,2},{1,3},{2,0},{3,1},{4,6},{5,7},{6,4},{7,5},{8,10},{9,11},{10,... | collective-permute-start | bytes 294920 | tf_op jit(solution)/shard_map/ppermute | solution.py:636
  (85 other events, 466.1 us)

commit v3 on v2

--- a/solution.py
+++ b/solution.py
@@ -13,7 +13,9 @@
 BF = jnp.bfloat16
 F32 = jnp.float32
 HIGH = lax.Precision.HIGHEST
-VMEM_BYTES = 56 * 1024 * 1024
+VMEM_BYTES = 28 * 1024 * 1024
+VMEM_WHOLE = 56 * 1024 * 1024
+ALONE = ("pack", "unpack", "attend", "attend_back")
 PEAK = 1.15e9
 RING = (0, 2, 4, 6, 7, 5, 3, 1)
 RING_STEPS = (0, -1, 1, -2, 2, -3, 3, -4)
@@ -50,7 +52,9 @@
         in_specs=in_specs,
         out_specs=[VM] * len(outs),
         scratch_shapes=list(scratch),
-        compiler_params=pltpu.CompilerParams(vmem_limit_bytes=VMEM_BYTES),
+        compiler_params=pltpu.CompilerParams(
+            vmem_limit_bytes=VMEM_WHOLE if name in ALONE else VMEM_BYTES
+        ),
         cost_estimate=pl.CostEstimate(
             flops=int(cost * PEAK), bytes_accessed=1, transcendentals=0
         ),

time: 234 us -> 213 us (0.910)
  Pallas kernels: 108 us -> 73.8 us
  other arithmetic: 7.31 us -> 14.1 us
  waiting for transfers between devices: 33.8 us -> 38.9 us
  starting transfers between devices: 66.3 us -> 71.2 us
  local copies, waits for them, and re-layouts: 13.4 us -> 10.6 us
    pallas_call x17, Pallas kernels: 108 us -> 73.8 us  [call(): pl.pallas_call(kernel, name=name, out_shape=list(outs), in_specs=in_specs...]
    ppermute x49, waiting for transfers between devices: 29.4 us -> 35.4 us  [swap(): return lax.ppermute(x, axis, [(i, i ^ bit) for i in range(size)])]
    unnamed x138 -> x102, local copies, waits for them, and re-layouts: 10.5 us -> 6.53 us
    all_to_all x1, starting transfers between devices: 3.56 us -> 6.37 us  [on_device(): lax.all_to_all(projected, 'gx', split_axis=0, concat_axis=0, tiled=True)]
  transfers between devices with their start and end apart: 64 -> 64, of which waited for: 17 -> 18; matrix products, arithmetic and copies ran while one was open for 3% -> 7% of each run, Pallas kernels for 41% -> 32%
where the time goes in v3:
time: 213 us; the launch traced here: 210 us
  Pallas kernels  73.8 us (35%)
  starting transfers between devices  71.2 us (33%)
  waiting for transfers between devices  38.9 us (18%)
  other arithmetic  14.1 us (7%)
  local copies, waits for them, and re-layouts  10.6 us (5%)
    pallas_call x17, Pallas kernels, call(): pl.pallas_call(kernel, name=name, out_shape=list(outs), in_specs=in_specs...  73.8 us
    ppermute x49, starting transfers between devices, swap(): return lax.ppermute(x, axis, [(i, i ^ bit) for i in range(size)])  49.2 us
    ppermute x49, waiting for transfers between devices, swap(): return lax.ppermute(x, axis, [(i, i ^ bit) for i in range(size)])  35.4 us
    ppermute x6, starting transfers between devices, gather_rows(): up[n] = lax.ppermute(up[n], 'gx', ahead)  7.17 us
    unnamed x102, local copies, waits for them, and re-layouts  6.53 us
    all_to_all x1, starting transfers between devices, on_device(): lax.all_to_all(projected, 'gx', split_axis=0, concat_axis=0, tiled=True)  6.37 us
    ppermute x6, starting transfers between devices, gather_rows(): down[n] = lax.ppermute(down[n], 'gx', back)  5.22 us
  transfers between devices with their start and end apart: 64, of which 18 were waited for; matrix products, arithmetic and copies ran while one was open for 7% of the time, Pallas kernels for 32%

profile of v3, /device:TPU:0, one launch (start us, length us, event | category | flops | bytes accessed | tf_op | source)
XLA Modules:
  0.0 210.1 jit_solution(13696808759880064372)
XLA Ops:
  0.7 1.7 pack.1
  3.6 3.0 %collective-permute-start.7 = (bf16[1536,384]{1,0:T(8,128)(2,1)S(1)}, bf16[1536,384]{1,0:T(8,128)(2,1)}, u32[]{:S(2)}, u32[]{:S(2)}) collective-permute-start(bf16[1536,384]{1,0:T(8,128)(2,1)S(1)} %pad_maximum_fusion.refs_4_.refs_6_), channel_id=1, source_target_pairs={{0,2},{1,3},{2,0},{3,1},{4,6},{5,7},{6,4},{7,5},{8,10},{9,11},{10,... | collective-permute-start | bytes 3538952 | tf_op jit(solution)/shard_map/ppermute | solution.py:640
  6.6 1.5 collective-permute-start.1
  8.6 1.5 collective-permute-start.9
  13.6 1.6 collective-permute-start.2
  15.8 1.6 collective-permute-start.10
  21.7 1.5 collective-permute-start.12
  25.2 2.3 %collective-permute-done.5.refs_7_ = bf16[96,320]{1,0:T(8,128)(2,1)S(1)} collective-permute-done((bf16[96,320]{1,0:T(8,128)(2,1)S(1)}, bf16[96,320]{1,0:T(8,128)(2,1)S(1)}, u32[]{:S(2)}, u32[]{:S(2)}) %collective-permute-start.5) | collective-permute-done | bytes 61472 | tf_op jit(solution)/shard_map/ppermute | solution.py:663
  28.2 1.8 collective-permute-start.14
  30.6 2.1 %unpack.1 = (bf16[768,128]{1,0:T(8,128)(2,1)}, bf16[768,192]{1,0:T(8,128)(2,1)}) custom-call(s32[1]{0:T(128)} %bitcast.1.gx_ref.refs_0_.refs_1_, bf16[96,320]{1,0:T(8,128)(2,1)} %get-tuple-element.142.refs_1_, bf16[96,320]{1,0:T(8,128)(2,1)} %copy-done.45, bf16[96,320]{1,0:T(8,128)(2,1)} %copy-done.44, bf16[96,320]{1,0:T(8,128)(2,1)} %copy-done.46, ...), custom_call_target="tpu_custom_call" | custom-call | flops 2300000000 | bytes 1 | tf_op jit(solution)/shard_map/unpack/pallas_call | solution.py:48
  35.2 13.8 %attend.1 = (bf16[1024,768]{1,0:T(8,128)(2,1)}, bf16[1024,576]{1,0:T(8,128)(2,1)}, bf16[30,256,256]{2,1,0:T(8,128)(2,1)}, bf16[1024,192]{1,0:T(8,128)(2,1)}, bf1...) custom-call(s32[1]{0:T(128)} %bitcast.refs_0_.gy_ref, ...), custom_call_target="tpu_custom_call" | custom-call | flops 69000003584 | bytes 1 | tf_op jit(solution)/shard_map/attend/pallas_call | solution.py:48
  49.2 1.5 collective-permute-start.18
  55.5 1.5 collective-permute-done.19.refs_3_.refs_16_
  57.1 1.6 route.1
  58.7 1.6 collective-permute-start.23
  60.3 2.6 %collective-permute-start.24 = (bf16[80,768]{1,0:T(8,128)(2,1)S(1)}, bf16[80,768]{1,0:T(8,128)(2,1)S(1)}, u32[]{:S(2)}, u32[]{:S(2)}) collective-permute-start(bf16[80,768]{1,0:T(8,128)(2,1)S(1)} %get-tuple-element.168.refs_25_), channel_id=1, source_target_pairs={{0,16},{4,20},{8,24},{12,28},{16,0},{20,4},{24,8},{28,12},{1,17},{... | collective-permute-start | bytes 368648 | tf_op jit(solution)/shard_map/ppermute | solution.py:640
  63.1 3.8 %collective-permute-done.23.refs_1_.refs_8_ = bf16[80,768]{1,0:T(8,128)(2,1)S(1)} collective-permute-done((bf16[80,768]{1,0:T(8,128)(2,1)S(1)}, bf16[80,768]{1,0:T(8,128)(2,1)S(1)}, u32[]{:S(2)}, u32[]{:S(2)}) %collective-permute-start.23) | collective-permute-done | bytes 122912 | tf_op jit(solution)/shard_map/ppermute | solution.py:640
  66.9 5.7 %collective-permute-done.24.refs_2_.refs_9_ = bf16[80,768]{1,0:T(8,128)(2,1)S(1)} collective-permute-done((bf16[80,768]{1,0:T(8,128)(2,1)S(1)}, bf16[80,768]{1,0:T(8,128)(2,1)S(1)}, u32[]{:S(2)}, u32[]{:S(2)}) %collective-permute-start.24) | collective-permute-done | bytes 122912 | tf_op jit(solution)/shard_map/ppermute | solution.py:640
  72.6 2.7 %collective-permute-start.26 = (bf16[80,768]{1,0:T(8,128)(2,1)S(1)}, bf16[80,768]{1,0:T(8,128)(2,1)S(1)}, u32[]{:S(2)}, u32[]{:S(2)}) collective-permute-start(bf16[80,768]{1,0:T(8,128)(2,1)S(1)} %get-tuple-element.171), channel_id=1, source_target_pairs={{0,8},{4,12},{8,0},{12,4},{16,24},{20,28},{24,16},{28,20},{1,9},{5... | collective-permute-start | bytes 368648 | tf_op jit(solution)/shard_map/ppermute | solution.py:640
  77.9 4.2 %expert_near.1 = (f32[320,768]{1,0:T(8,128)S(1)}, bf16[320,1536]{1,0:T(8,128)(2,1)S(1)}, bf16[320,1536]{1,0:T(8,128)(2,1)S(1)}) custom-call(bf16[80,768]{1,0:T(8,128)(2,1)S(1)} %get-tuple-element.166.refs_0_.refs_7_.refs_23_, bf16[80,768]{1,0:T(8,128)(2,1)S(1)} %collective-permute-done.23.refs_1_.refs_8_, ...), custom_call_target="tpu_custom_call" | custom-call | flops 8049999872 | bytes 1 | tf_op jit(solution)/shard_map/expert_near/pallas_call | solution.py:48
  82.1 5.4 %collective-permute-done.29.refs_7_.refs_12_ = bf16[1536,384]{1,0:T(8,128)(2,1)S(1)} collective-permute-done((bf16[1536,384]{1,0:T(8,128)(2,1)}, bf16[1536,384]{1,0:T(8,128)(2,1)S(1)}, u32[]{:S(2)}, u32[]{:S(2)}) %collective-permute-start.29) | collective-permute-done | bytes 1179680 | tf_op jit(solution)/shard_map/ppermute | solution.py:640
  87.6 2.8 %collective-permute-done.32.refs_8_.refs_13_ = bf16[1536,384]{1,0:T(8,128)(2,1)S(1)} collective-permute-done((bf16[1536,384]{1,0:T(8,128)(2,1)S(1)}, bf16[1536,384]{1,0:T(8,128)(2,1)S(1)}, u32[]{:S(2)}, u32[]{:S(2)}) %collective-permute-start.32) | collective-permute-done | bytes 1179680 | tf_op jit(solution)/shard_map/ppermute | solution.py:640
  90.4 3.5 %expert_far.1 = (bf16[80,768]{1,0:T(8,128)(2,1)S(1)}, bf16[80,768]{1,0:T(8,128)(2,1)S(1)}, bf16[80,768]{1,0:T(8,128)(2,1)S(1)}, bf16[80,768]{1,0:T(8,128)(2,1)S(...) custom-call(bf16[80,768]{1,0:T(8,128)(2,1)S(1)} %get-tuple-element.166.refs_0_.refs_7_.refs_23_, ...), custom_call_target="tpu_custom_call" | custom-call | flops 8625000448 | bytes 1 | tf_op jit(solution)/shard_map/expert_far/pallas_call | solution.py:48
  95.5 1.8 collective-permute-start.37
  97.4 2.3 %collective-permute-start.38 = (bf16[80,768]{1,0:T(8,128)(2,1)S(1)}, bf16[80,768]{1,0:T(8,128)(2,1)S(1)}, u32[]{:S(2)}, u32[]{:S(2)}) collective-permute-start(bf16[80,768]{1,0:T(8,128)(2,1)S(1)} %get-tuple-element.194), channel_id=1, source_target_pairs={{0,16},{4,20},{8,24},{12,28},{16,0},{20,4},{24,8},{28,12},{1,17},{... | collective-permute-start | bytes 368648 | tf_op jit(solution)/shard_map/ppermute | solution.py:640
  100.0 6.8 %expert_back.1 = (bf16[80,768]{1,0:T(8,128)(2,1)S(1)}, bf16[80,768]{1,0:T(8,128)(2,1)S(1)}, bf16[80,768]{1,0:T(8,128)(2,1)S(1)}, bf16[80,768]{1,0:T(8,128)(2,1)S(1)}, bf16[320,3072]{1,0:T(8,128)(2,1)S(1)}) custom-call(bf16[80,768]{1,0:T(8,128)(2,1)S(1)} %get-tuple-element.170.refs_0_, bf16[80,768]{1,0:T(8,128)(2,1)S(1)} %collective-permute-done.26.refs_1_, ...), custom_call_target="tpu_custom_call" | custom-call | flops 13799999488 | bytes 1 | tf_op jit(solution)/shard_map/expert_back/pallas_call | solution.py:48
  107.7 3.2 %collective-permute-start.34 = (bf16[80,768]{1,0:T(8,128)(2,1)S(1)}, bf16[80,768]{1,0:T(8,128)(2,1)S(1)}, u32[]{:S(2)}, u32[]{:S(2)}) collective-permute-start(bf16[80,768]{1,0:T(8,128)(2,1)S(1)} %get-tuple-element.189), channel_id=1, source_target_pairs={{0,16},{4,20},{8,24},{12,28},{16,0},{20,4},{24,8},{28,12},{1,17},{... | collective-permute-start | bytes 368648 | tf_op jit(solution)/shard_map/ppermute | solution.py:640
  112.1 3.8 %fill_rows.1 = (f32[384,768]{1,0:T(8,128)S(1)}, bf16[384,768]{1,0:T(8,128)(2,1)S(1)}, bf16[384,768]{1,0:T(8,128)(2,1)S(1)}, bf16[384,768]{1,0:T(8,128)(2,1)}, bf...) custom-call(bf16[80,768]{1,0:T(8,128)(2,1)S(1)} %get-tuple-element.1, ...), custom_call_target="tpu_custom_call" | custom-call | flops 14949999616 | bytes 1 | tf_op jit(solution)/shard_map/fill_rows/pallas_call | solution.py:48
  117.3 2.9 %collective-permute-done.34.refs_2_ = bf16[80,768]{1,0:T(8,128)(2,1)S(1)} collective-permute-done((bf16[80,768]{1,0:T(8,128)(2,1)S(1)}, bf16[80,768]{1,0:T(8,128)(2,1)S(1)}, u32[]{:S(2)}, u32[]{:S(2)}) %collective-permute-start.34) | collective-permute-done | bytes 122912 | tf_op jit(solution)/shard_map/ppermute | solution.py:640
  120.3 1.9 combine.1
  123.3 1.5 collective-permute-start.44
  124.9 2.5 %outer_in_held.1 = (f32[768,384]{1,0:T(8,128)S(1)}, bf16[768,384]{1,0:T(8,128)(2,1)S(1)}, bf16[768,384]{1,0:T(8,128)(2,1)S(1)}, bf16[768,384]{1,0:T(8,128)(2,1)}) custom-call(bf16[80,768]{1,0:T(8,128)(2,1)S(1)} %get-tuple-element.166.refs_0_.refs_7_.refs_23_, bf16[80,768]{1,0:T(8,128)(2,1)S(1)} %collective-permute-done.23.refs_1_.refs_8_, ...), custom_call_target="tpu_custom_call" | custom-call | flops 1150000000 | bytes 1 | tf_op jit(solution)/shard_map/outer_in_held/pallas_call | solution.py:48
  132.4 6.4 %all-to-all-start = ((bf16[8,96,384]{2,1,0:T(8,128)(2,1)}), bf16[8,96,384]{2,1,0:T(8,128)(2,1)}, u32[]{:S(2)}, u32[]{:S(2)}) async-start(bf16[8,96,384]{2,1,0:T(8,128)(2,1)} %bitcast.32), calls=%async_computation | async-start | bytes 1179648 | tf_op jit(solution)/shard_map/all_to_all | solution.py:996
  138.8 1.6 collective-permute-start.49
  140.9 2.0 collective-permute-start.46
  142.9 19.6 %attend_back.1 = (bf16[4,96,640]{2,1,0:T(8,128)(2,1)}, bf16[4,96,640]{2,1,0:T(8,128)(2,1)}, bf16[2,256,768]{2,1,0:T(8,128)(2,1)}, bf16[2,256,768]{2,1,0:T(8,128)(2,1)}, f32[32,8]{1,0:T(8,128)}) custom-call(s32[1]{0:T(128)} %bitcast.refs_0_.gy_ref, s32[1]{0:T(128)} %bitcast.1.gx_ref.refs_0_.refs_1_, bf16[480,128]{1,0:T(8,128)(2,1)} %copy-done.22, ...), custom_call_target="tpu_custom_call" | custom-call | flops 69000003584 | bytes 1 | tf_op jit(solution)/shard_map/attend_back/pallas_call | solution.py:48
  163.3 1.5 collective-permute-done.47
  165.7 1.8 collective-permute-start.54
  170.1 2.3 %add_bitcast_fusion = f32[1,384,768]{2,1,0:T(8,128)} fusion(bf16[384,768]{1,0:T(8,128)(2,1)S(1)} %copy-done.26, f32[384,768]{1,0:T(8,128)S(1)} %get-tuple-element.263, bf16[384,768]{1,0:T(8,128)(2,1)} %collective-permute-done.48), kind=kLoop, calls=%fused_computation.4 | loop fusion | flops 1179648 | bytes 3538944 | tf_op jit(solution)/shard_map/broadcast_in_dim | solution.py:1107
  172.4 1.7 collective-permute-start.53
  174.1 2.0 add_convert_fusion.2
  176.2 5.1 %unsort.1 = f32[1024,768]{1,0:T(8,128)} custom-call(s32[1]{0:T(128)} %bitcast.refs_0_.gy_ref, s32[1024,1]{1,0:T(8,128)S(1)} %copy-done.5, bf16[1024,768]{1,0:T(8,128)(2,1)S(1)} %copy-done.1, bf16[320,768]{1,0:T(8,128)(2,1)S(1)} %copy-done.7, bf16[320,768]{1,0:T(8,128)(2,1)S(1)} %collective-permute-done.51.d1_ref, bf16[320,768]{1,0:T(8,128)(2,1)S(1)} %copy-done.9, ...), custom_call_target="tpu_custom_call" | custom-call | flops 1150000000 | bytes 1 | tf_op jit(solution)/shard_map/unsort/pallas_call | solution.py:48
  181.5 3.6 %collective-permute-start.57 = (bf16[96,640]{1,0:T(8,128)(2,1)S(1)}, bf16[96,640]{1,0:T(8,128)(2,1)S(1)}, u32[]{:S(2)}, u32[]{:S(2)}) collective-permute-start(bf16[96,640]{1,0:T(8,128)(2,1)S(1)} %get-tuple-element.268), channel_id=1, source_target_pairs={{0,24},{4,28},{8,16},{12,20},{16,8},{20,12},{24,0},{28,4},{1,25},{... | collective-permute-start | bytes 368648 | tf_op jit(solution)/shard_map/ppermute | solution.py:640
  189.7 1.7 collective-permute-start.62
  191.4 4.3 %collective-permute-done.56 = bf16[96,640]{1,0:T(8,128)(2,1)S(1)} collective-permute-done((bf16[96,640]{1,0:T(8,128)(2,1)S(1)}, bf16[96,640]{1,0:T(8,128)(2,1)S(1)}, u32[]{:S(2)}, u32[]{:S(2)}) %collective-permute-start.56) | collective-permute-done | bytes 122912 | tf_op jit(solution)/shard_map/ppermute | solution.py:640
  201.8 3.1 %finish.1 = f32[1024,768]{1,0:T(8,128)} custom-call(s32[1]{0:T(128)} %bitcast.refs_0_.gy_ref, bf16[2,256,768]{2,1,0:T(8,128)(2,1)S(1)} %add_convert_fusion.own_ref, bf16[2,256,768]{2,1,0:T(8,128)(2,1)} %collective-permute-done.58.other_ref, bf16[1024,768]{1,0:T(8,128)(2,1)S(1)} %copy-done.3), custom_call_target="tpu_custom_call" | custom-call | flops 1150000000 | bytes 1 | tf_op jit(solution)/shard_map/finish/pallas_call | solution.py:48
  205.1 1.7 collective-permute-done.60.line_ref
  207.5 2.4 %add_bitcast_fusion.1 = f32[1,768,384]{2,1,0:T(8,128)} fusion(bf16[768,384]{1,0:T(8,128)(2,1)} %collective-permute-done.61, f32[768,384]{1,0:T(8,128)S(1)} %get-tuple-element.207, bf16[768,384]{1,0:T(8,128)(2,1)} %collective-permute-done.62), kind=kLoop, calls=%fused_computation.5 | loop fusion | flops 1179648 | bytes 3538944 | tf_op jit(solution)/shard_map/broadcast_in_dim | solution.py:1106
  (227 shorter events, 51.5 us)
Async XLA Ops:
  3.6 30.2 %collective-permute-start.7 = (bf16[1536,384]{1,0:T(8,128)(2,1)S(1)}, bf16[1536,384]{1,0:T(8,128)(2,1)}, u32[]{:S(2)}, u32[]{:S(2)}) collective-permute-start(bf16[1536,384]{1,0:T(8,128)(2,1)S(1)} %pad_maximum_fusion.refs_4_.refs_6_), channel_id=1, source_target_pairs={{0,2},{1,3},{2,0},{3,1},{4,6},{5,7},{6,4},{7,5},{8,10},{9,11},{10,... | collective-permute-start | bytes 3538952 | tf_op jit(solution)/shard_map/ppermute | solution.py:640
  6.6 8.7 %collective-permute-start.1 = (bf16[96,320]{1,0:T(8,128)(2,1)S(1)}, bf16[96,320]{1,0:T(8,128)(2,1)S(1)}, u32[]{:S(2)}, u32[]{:S(2)}) collective-permute-start(bf16[96,320]{1,0:T(8,128)(2,1)S(1)} %copy-done.43), channel_id=1, source_target_pairs={{8,0},{16,8},{24,16},{28,24},{20,28},{12,20},{4,12},{0,4},{9,1},{1... | collective-permute-start | bytes 184328 | tf_op jit(solution)/shard_map/ppermute | solution.py:663
  8.6 12.6 %collective-permute-start.9 = (bf16[96,576]{1,0:T(8,128)(2,1)S(1)}, bf16[96,576]{1,0:T(8,128)(2,1)S(1)}, u32[]{:S(2)}, u32[]{:S(2)}) collective-permute-start(bf16[96,576]{1,0:T(8,128)(2,1)S(1)} %copy-done.32), channel_id=1, source_target_pairs={{8,0},{16,8},{24,16},{28,24},{20,28},{12,20},{4,12},{0,4},{9,1},{1... | collective-permute-start | bytes 331784 | tf_op jit(solution)/shard_map/ppermute | solution.py:663
  15.3 7.9 %collective-permute-start.3 = (bf16[96,320]{1,0:T(8,128)(2,1)S(1)}, bf16[96,320]{1,0:T(8,128)(2,1)S(1)}, u32[]{:S(2)}, u32[]{:S(2)}) collective-permute-start(bf16[96,320]{1,0:T(8,128)(2,1)S(1)} %collective-permute-done.1.refs_3_), channel_id=1, source_target_pairs={{8,0},{16,8},{24,16},{28,24},{20,28},{12,20},{4,12},{0,4},{9,1},{1... | collective-permute-start | bytes 184328 | tf_op jit(solution)/shard_map/ppermute | solution.py:663
  21.2 6.4 %collective-permute-start.11 = (bf16[96,576]{1,0:T(8,128)(2,1)S(1)}, bf16[96,576]{1,0:T(8,128)(2,1)S(1)}, u32[]{:S(2)}, u32[]{:S(2)}) collective-permute-start(bf16[96,576]{1,0:T(8,128)(2,1)S(1)} %collective-permute-done.9.refs_10_), channel_id=1, source_target_pairs={{8,0},{16,8},{24,16},{28,24},{20,28},{12,20},{4,12},{0,4},{9,1},{1... | collective-permute-start | bytes 331784 | tf_op jit(solution)/shard_map/ppermute | solution.py:663
  21.7 6.5 %collective-permute-start.12 = (bf16[96,576]{1,0:T(8,128)(2,1)S(1)}, bf16[96,576]{1,0:T(8,128)(2,1)S(1)}, u32[]{:S(2)}, u32[]{:S(2)}) collective-permute-start(bf16[96,576]{1,0:T(8,128)(2,1)S(1)} %collective-permute-done.10.refs_11_), channel_id=1, source_target_pairs={{0,8},{8,16},{16,24},{24,28},{28,20},{20,12},{12,4},{4,0},{1,9},{9... | collective-permute-start | bytes 331784 | tf_op jit(solution)/shard_map/ppermute | solution.py:662
  23.7 6.2 %collective-permute-start.6 = (bf16[96,320]{1,0:T(8,128)(2,1)S(1)}, bf16[96,320]{1,0:T(8,128)(2,1)S(1)}, u32[]{:S(2)}, u32[]{:S(2)}) collective-permute-start(bf16[96,320]{1,0:T(8,128)(2,1)S(1)} %collective-permute-done.4.refs_6_), channel_id=1, source_target_pairs={{0,8},{8,16},{16,24},{24,28},{28,20},{20,12},{12,4},{4,0},{1,9},{9... | collective-permute-start | bytes 184328 | tf_op jit(solution)/shard_map/ppermute | solution.py:667
  27.6 23.1 %collective-permute-start.15 = (bf16[1536,384]{1,0:T(8,128)(2,1)S(1)}, bf16[1536,384]{1,0:T(8,128)(2,1)S(1)}, u32[]{:S(2)}, u32[]{:S(2)}) collective-permute-start(bf16[1536,384]{1,0:T(8,128)(2,1)S(1)} %pad_maximum_fusion.refs_4_.refs_6_), channel_id=1, source_target_pairs={{0,1},{1,0},{2,3},{3,2},{4,5},{5,4},{6,7},{7,6},{8,9},{9,8},{10,11... | collective-permute-start | bytes 3538952 | tf_op jit(solution)/shard_map/ppermute | solution.py:640
  27.6 6.2 %collective-permute-start.13 = (bf16[96,576]{1,0:T(8,128)(2,1)S(1)}, bf16[96,576]{1,0:T(8,128)(2,1)S(1)}, u32[]{:S(2)}, u32[]{:S(2)}) collective-permute-start(bf16[96,576]{1,0:T(8,128)(2,1)S(1)} %collective-permute-done.11.refs_12_), channel_id=1, source_target_pairs={{8,0},{16,8},{24,16},{28,24},{20,28},{12,20},{4,12},{0,4},{9,1},{1... | collective-permute-start | bytes 331784 | tf_op jit(solution)/shard_map/ppermute | solution.py:663
  28.2 6.3 %collective-permute-start.14 = (bf16[96,576]{1,0:T(8,128)(2,1)S(1)}, bf16[96,576]{1,0:T(8,128)(2,1)S(1)}, u32[]{:S(2)}, u32[]{:S(2)}) collective-permute-start(bf16[96,576]{1,0:T(8,128)(2,1)S(1)} %collective-permute-done.12.refs_13_), channel_id=1, source_target_pairs={{0,8},{8,16},{16,24},{24,28},{28,20},{20,12},{12,4},{4,0},{1,9},{9... | collective-permute-start | bytes 331784 | tf_op jit(solution)/shard_map/ppermute | solution.py:667
  32.8 16.1 %collective-permute-start.21 = (bf16[768,192]{1,0:T(8,128)(2,1)}, bf16[768,192]{1,0:T(8,128)(2,1)S(1)}, u32[]{:S(2)}, u32[]{:S(2)}) collective-permute-start(bf16[768,192]{1,0:T(8,128)(2,1)} %get-tuple-element.155.refs_4_.refs_9_), channel_id=1, source_target_pairs={{0,2},{1,3},{2,0},{3,1},{4,6},{5,7},{6,4},{7,5},{8,10},{9,11},{10,... | collective-permute-start | bytes 884744 | tf_op jit(solution)/shard_map/ppermute | solution.py:640
  33.8 15.4 %collective-permute-start.20 = (bf16[768,192]{1,0:T(8,128)(2,1)}, bf16[768,192]{1,0:T(8,128)(2,1)S(1)}, u32[]{:S(2)}, u32[]{:S(2)}) collective-permute-start(bf16[768,192]{1,0:T(8,128)(2,1)} %get-tuple-element.155.refs_4_.refs_9_), channel_id=1, source_target_pairs={{0,1},{1,0},{2,3},{3,2},{4,5},{5,4},{6,7},{7,6},{8,9},{9,8},{10,11... | collective-permute-start | bytes 884744 | tf_op jit(solution)/shard_map/ppermute | solution.py:640
  33.8 29.3 %collective-permute-start.30 = (bf16[1536,384]{1,0:T(8,128)(2,1)S(1)}, bf16[1536,384]{1,0:T(8,128)(2,1)S(1)}, u32[]{:S(2)}, u32[]{:S(2)}) collective-permute-start(bf16[1536,384]{1,0:T(8,128)(2,1)S(1)} %pad_maximum_fusion.refs_4_.refs_6_), channel_id=1, source_target_pairs={{0,4},{4,0},{8,12},{12,8},{16,20},{20,16},{24,28},{28,24},{1,5},{5... | collective-permute-start | bytes 3538952 | tf_op jit(solution)/shard_map/ppermute | solution.py:640
  34.5 16.4 %collective-permute-start.16 = (bf16[1536,384]{1,0:T(8,128)(2,1)}, bf16[1536,384]{1,0:T(8,128)(2,1)}, u32[]{:S(2)}, u32[]{:S(2)}) collective-permute-start(bf16[1536,384]{1,0:T(8,128)(2,1)} %collective-permute-done.7.refs_6_.refs_8_), channel_id=1, source_target_pairs={{0,1},{1,0},{2,3},{3,2},{4,5},{5,4},{6,7},{7,6},{8,9},{9,8},{10,11... | collective-permute-start | bytes 3538952 | tf_op jit(solution)/shard_map/ppermute | solution.py:640
  49.2 6.3 %collective-permute-start.18 = (bf16[480,128]{1,0:T(8,128)(2,1)}, bf16[480,128]{1,0:T(8,128)(2,1)S(1)}, u32[]{:S(2)}, u32[]{:S(2)}) collective-permute-start(bf16[480,128]{1,0:T(8,128)(2,1)} %get-tuple-element.153), channel_id=1, source_target_pairs={{0,2},{1,3},{2,0},{3,1},{4,6},{5,7},{6,4},{7,5},{8,10},{9,11},{10,... | collective-permute-start | bytes 368648 | tf_op jit(solution)/shard_map/ppermute | solution.py:640
  50.7 6.4 %collective-permute-start.19 = (bf16[480,128]{1,0:T(8,128)(2,1)}, bf16[480,128]{1,0:T(8,128)(2,1)S(1)}, u32[]{:S(2)}, u32[]{:S(2)}) collective-permute-start(bf16[480,128]{1,0:T(8,128)(2,1)} %get-tuple-element.154), channel_id=1, source_target_pairs={{0,3},{1,2},{2,1},{3,0},{4,7},{5,6},{6,5},{7,4},{8,11},{9,10},{10,... | collective-permute-start | bytes 368648 | tf_op jit(solution)/shard_map/ppermute | solution.py:640
  52.7 34.7 %collective-permute-start.29 = (bf16[1536,384]{1,0:T(8,128)(2,1)}, bf16[1536,384]{1,0:T(8,128)(2,1)S(1)}, u32[]{:S(2)}, u32[]{:S(2)}) collective-permute-start(bf16[1536,384]{1,0:T(8,128)(2,1)} %collective-permute-done.7.refs_6_.refs_8_), channel_id=1, source_target_pairs={{0,4},{4,0},{8,12},{12,8},{16,20},{20,16},{24,28},{28,24},{1,5},{5... | collective-permute-start | bytes 3538952 | tf_op jit(solution)/shard_map/ppermute | solution.py:640
  58.7 8.2 %collective-permute-start.23 = (bf16[80,768]{1,0:T(8,128)(2,1)S(1)}, bf16[80,768]{1,0:T(8,128)(2,1)S(1)}, u32[]{:S(2)}, u32[]{:S(2)}) collective-permute-start(bf16[80,768]{1,0:T(8,128)(2,1)S(1)} %get-tuple-element.167.refs_24_), channel_id=1, source_target_pairs={{0,8},{4,12},{8,0},{12,4},{16,24},{20,28},{24,16},{28,20},{1,9},{5... | collective-permute-start | bytes 368648 | tf_op jit(solution)/shard_map/ppermute | solution.py:640
  60.3 12.3 %collective-permute-start.24 = (bf16[80,768]{1,0:T(8,128)(2,1)S(1)}, bf16[80,768]{1,0:T(8,128)(2,1)S(1)}, u32[]{:S(2)}, u32[]{:S(2)}) collective-permute-start(bf16[80,768]{1,0:T(8,128)(2,1)S(1)} %get-tuple-element.168.refs_25_), channel_id=1, source_target_pairs={{0,16},{4,20},{8,24},{12,28},{16,0},{20,4},{24,8},{28,12},{1,17},{... | collective-permute-start | bytes 368648 | tf_op jit(solution)/shard_map/ppermute | solution.py:640
  62.9 9.7 %collective-permute-start.25 = (bf16[80,768]{1,0:T(8,128)(2,1)S(1)}, bf16[80,768]{1,0:T(8,128)(2,1)S(1)}, u32[]{:S(2)}, u32[]{:S(2)}) collective-permute-start(bf16[80,768]{1,0:T(8,128)(2,1)S(1)} %get-tuple-element.169.refs_26_), channel_id=1, source_target_pairs={{0,24},{4,28},{8,16},{12,20},{16,8},{20,12},{24,0},{28,4},{1,25},{... | collective-permute-start | bytes 368648 | tf_op jit(solution)/shard_map/ppermute | solution.py:640
  63.1 24.4 %collective-permute-start.31 = (bf16[1536,384]{1,0:T(8,128)(2,1)S(1)}, bf16[1536,384]{1,0:T(8,128)(2,1)S(1)}, u32[]{:S(2)}, u32[]{:S(2)}) collective-permute-start(bf16[1536,384]{1,0:T(8,128)(2,1)S(1)} %collective-permute-done.30.refs_5_.refs_10_), channel_id=1, source_target_pairs={{0,1},{1,0},{2,3},{3,2},{4,5},{5,4},{6,7},{7,6},{8,9},{9,8},{10,11... | collective-permute-start | bytes 3538952 | tf_op jit(solution)/shard_map/ppermute | solution.py:640
  72.6 14.8 %collective-permute-start.26 = (bf16[80,768]{1,0:T(8,128)(2,1)S(1)}, bf16[80,768]{1,0:T(8,128)(2,1)S(1)}, u32[]{:S(2)}, u32[]{:S(2)}) collective-permute-start(bf16[80,768]{1,0:T(8,128)(2,1)S(1)} %get-tuple-element.171), channel_id=1, source_target_pairs={{0,8},{4,12},{8,0},{12,4},{16,24},{20,28},{24,16},{28,20},{1,9},{5... | collective-permute-start | bytes 368648 | tf_op jit(solution)/shard_map/ppermute | solution.py:640
  75.4 12.1 %collective-permute-start.27 = (bf16[80,768]{1,0:T(8,128)(2,1)S(1)}, bf16[80,768]{1,0:T(8,128)(2,1)S(1)}, u32[]{:S(2)}, u32[]{:S(2)}) collective-permute-start(bf16[80,768]{1,0:T(8,128)(2,1)S(1)} %get-tuple-element.172), channel_id=1, source_target_pairs={{0,16},{4,20},{8,24},{12,28},{16,0},{20,4},{24,8},{28,12},{1,17},{... | collective-permute-start | bytes 368648 | tf_op jit(solution)/shard_map/ppermute | solution.py:640
  76.4 11.1 %collective-permute-start.28 = (bf16[80,768]{1,0:T(8,128)(2,1)S(1)}, bf16[80,768]{1,0:T(8,128)(2,1)S(1)}, u32[]{:S(2)}, u32[]{:S(2)}) collective-permute-start(bf16[80,768]{1,0:T(8,128)(2,1)S(1)} %get-tuple-element.173), channel_id=1, source_target_pairs={{0,24},{4,28},{8,16},{12,20},{16,8},{20,12},{24,0},{28,4},{1,25},{... | collective-permute-start | bytes 368648 | tf_op jit(solution)/shard_map/ppermute | solution.py:640
  95.4 16.8 %collective-permute-start.36 = (bf16[4,384,768]{2,1,0:T(8,128)(2,1)S(1)}, bf16[4,384,768]{2,1,0:T(8,128)(2,1)S(1)}, u32[]{:S(2)}, u32[]{:S(2)}) collective-permute-start(bf16[4,384,768]{2,1,0:T(8,128)(2,1)S(1)} %outer_out_sent.1), channel_id=1, source_target_pairs={{0,1},{1,0},{2,3},{3,2},{4,5},{5,4},{6,7},{7,6},{8,9},{9,8},{10,11... | collective-permute-start | bytes 7077896 | tf_op jit(solution)/shard_map/ppermute | solution.py:640
  95.5 12.2 %collective-permute-start.37 = (bf16[80,768]{1,0:T(8,128)(2,1)S(1)}, bf16[80,768]{1,0:T(8,128)(2,1)S(1)}, u32[]{:S(2)}, u32[]{:S(2)}) collective-permute-start(bf16[80,768]{1,0:T(8,128)(2,1)S(1)} %get-tuple-element.193), channel_id=1, source_target_pairs={{0,8},{4,12},{8,0},{12,4},{16,24},{20,28},{24,16},{28,20},{1,9},{5... | collective-permute-start | bytes 368648 | tf_op jit(solution)/shard_map/ppermute | solution.py:640
  97.4 13.5 %collective-permute-start.38 = (bf16[80,768]{1,0:T(8,128)(2,1)S(1)}, bf16[80,768]{1,0:T(8,128)(2,1)S(1)}, u32[]{:S(2)}, u32[]{:S(2)}) collective-permute-start(bf16[80,768]{1,0:T(8,128)(2,1)S(1)} %get-tuple-element.194), channel_id=1, source_target_pairs={{0,16},{4,20},{8,24},{12,28},{16,0},{20,4},{24,8},{28,12},{1,17},{... | collective-permute-start | bytes 368648 | tf_op jit(solution)/shard_map/ppermute | solution.py:640
  99.7 12.4 %collective-permute-start.39 = (bf16[80,768]{1,0:T(8,128)(2,1)S(1)}, bf16[80,768]{1,0:T(8,128)(2,1)S(1)}, u32[]{:S(2)}, u32[]{:S(2)}) collective-permute-start(bf16[80,768]{1,0:T(8,128)(2,1)S(1)} %get-tuple-element.195), channel_id=1, source_target_pairs={{0,24},{4,28},{8,16},{12,20},{16,8},{20,12},{24,0},{28,4},{1,25},{... | collective-permute-start | bytes 368648 | tf_op jit(solution)/shard_map/ppermute | solution.py:640
  106.7 10.6 %collective-permute-start.33 = (bf16[80,768]{1,0:T(8,128)(2,1)S(1)}, bf16[80,768]{1,0:T(8,128)(2,1)S(1)}, u32[]{:S(2)}, u32[]{:S(2)}) collective-permute-start(bf16[80,768]{1,0:T(8,128)(2,1)S(1)} %get-tuple-element.188), channel_id=1, source_target_pairs={{0,8},{4,12},{8,0},{12,4},{16,24},{20,28},{24,16},{28,20},{1,9},{5... | collective-permute-start | bytes 368648 | tf_op jit(solution)/shard_map/ppermute | solution.py:640
  107.7 12.5 %collective-permute-start.34 = (bf16[80,768]{1,0:T(8,128)(2,1)S(1)}, bf16[80,768]{1,0:T(8,128)(2,1)S(1)}, u32[]{:S(2)}, u32[]{:S(2)}) collective-permute-start(bf16[80,768]{1,0:T(8,128)(2,1)S(1)} %get-tuple-element.189), channel_id=1, source_target_pairs={{0,16},{4,20},{8,24},{12,28},{16,0},{20,4},{24,8},{28,12},{1,17},{... | collective-permute-start | bytes 368648 | tf_op jit(solution)/shard_map/ppermute | solution.py:640
  110.9 9.3 %collective-permute-start.35 = (bf16[80,768]{1,0:T(8,128)(2,1)S(1)}, bf16[80,768]{1,0:T(8,128)(2,1)S(1)}, u32[]{:S(2)}, u32[]{:S(2)}) collective-permute-start(bf16[80,768]{1,0:T(8,128)(2,1)S(1)} %get-tuple-element.190), channel_id=1, source_target_pairs={{0,24},{4,28},{8,16},{12,20},{16,8},{20,12},{24,0},{28,4},{1,25},{... | collective-permute-start | bytes 368648 | tf_op jit(solution)/shard_map/ppermute | solution.py:640
  115.9 14.5 %collective-permute-start.41 = (bf16[384,768]{1,0:T(8,128)(2,1)S(1)}, bf16[384,768]{1,0:T(8,128)(2,1)S(1)}, u32[]{:S(2)}, u32[]{:S(2)}) collective-permute-start(bf16[384,768]{1,0:T(8,128)(2,1)S(1)} %get-tuple-element.206), channel_id=1, source_target_pairs={{0,4},{4,0},{8,12},{12,8},{16,20},{20,16},{24,28},{28,24},{1,5},{5... | collective-permute-start | bytes 1769480 | tf_op jit(solution)/shard_map/ppermute | solution.py:640
  117.3 7.5 %collective-permute-start.40 = (bf16[4,768,384]{2,1,0:T(8,128)(2,1)S(1)}, bf16[4,768,384]{2,1,0:T(8,128)(2,1)S(1)}, u32[]{:S(2)}, u32[]{:S(2)}) collective-permute-start(bf16[4,768,384]{2,1,0:T(8,128)(2,1)S(1)} %get-tuple-element.203), channel_id=1, source_target_pairs={{0,1},{1,0},{2,3},{3,2},{4,5},{5,4},{6,7},{7,6},{8,9},{9,8},{10,11... | collective-permute-start | bytes 7077896 | tf_op jit(solution)/shard_map/ppermute | solution.py:640
  122.8 8.7 %collective-permute-start.42 = (bf16[768,384]{1,0:T(8,128)(2,1)S(1)}, bf16[768,384]{1,0:T(8,128)(2,1)S(1)}, u32[]{:S(2)}, u32[]{:S(2)}) collective-permute-start(bf16[768,384]{1,0:T(8,128)(2,1)S(1)} %get-tuple-element.211), channel_id=1, source_target_pairs={{0,1},{1,0},{2,3},{3,2},{4,5},{5,4},{6,7},{7,6},{8,9},{9,8},{10,11... | collective-permute-start | bytes 1769480 | tf_op jit(solution)/shard_map/ppermute | solution.py:640
  127.4 35.2 %collective-permute-start.48 = (bf16[384,768]{1,0:T(8,128)(2,1)}, bf16[384,768]{1,0:T(8,128)(2,1)}, u32[]{:S(2)}, u32[]{:S(2)}) collective-permute-start(bf16[384,768]{1,0:T(8,128)(2,1)} %get-tuple-element.229), channel_id=1, source_target_pairs={{0,4},{4,0},{8,12},{12,8},{16,20},{20,16},{24,28},{28,24},{1,5},{5... | collective-permute-start | bytes 1769480 | tf_op jit(solution)/shard_map/ppermute | solution.py:640
  132.4 33.2 %all-to-all-start = ((bf16[8,96,384]{2,1,0:T(8,128)(2,1)}), bf16[8,96,384]{2,1,0:T(8,128)(2,1)}, u32[]{:S(2)}, u32[]{:S(2)}) async-start(bf16[8,96,384]{2,1,0:T(8,128)(2,1)} %bitcast.32), calls=%async_computation | async-start | bytes 1179648 | tf_op jit(solution)/shard_map/all_to_all | solution.py:996
  138.8 23.7 %collective-permute-start.49 = (bf16[320,768]{1,0:T(8,128)(2,1)S(1)}, bf16[320,768]{1,0:T(8,128)(2,1)S(1)}, u32[]{:S(2)}, u32[]{:S(2)}) collective-permute-start(bf16[320,768]{1,0:T(8,128)(2,1)S(1)} %copy-done.7), channel_id=1, source_target_pairs={{0,2},{1,3},{2,0},{3,1},{4,6},{5,7},{6,4},{7,5},{8,10},{9,11},{10,... | collective-permute-start | bytes 1474568 | tf_op jit(solution)/shard_map/ppermute | solution.py:640
  140.4 24.4 %collective-permute-start.47 = (bf16[384,768]{1,0:T(8,128)(2,1)}, bf16[384,768]{1,0:T(8,128)(2,1)S(1)}, u32[]{:S(2)}, u32[]{:S(2)}) collective-permute-start(bf16[384,768]{1,0:T(8,128)(2,1)} %add_convert_fusion.4), channel_id=1, source_target_pairs={{0,2},{1,3},{2,0},{3,1},{4,6},{5,7},{6,4},{7,5},{8,10},{9,11},{10,... | collective-permute-start | bytes 1769480 | tf_op jit(solution)/shard_map/ppermute | solution.py:640
  140.9 24.7 %collective-permute-start.46 = (bf16[768,384]{1,0:T(8,128)(2,1)}, bf16[768,384]{1,0:T(8,128)(2,1)}, u32[]{:S(2)}, u32[]{:S(2)}) collective-permute-start(bf16[768,384]{1,0:T(8,128)(2,1)} %copy-done.12), channel_id=1, source_target_pairs={{0,4},{4,0},{8,12},{12,8},{16,20},{20,16},{24,28},{28,24},{1,5},{5... | collective-permute-start | bytes 1769480 | tf_op jit(solution)/shard_map/ppermute | solution.py:640
  165.7 15.6 %collective-permute-start.54 = (bf16[4,96,640]{2,1,0:T(8,128)(2,1)}, bf16[4,96,640]{2,1,0:T(8,128)(2,1)S(1)}, u32[]{:S(2)}, u32[]{:S(2)}) collective-permute-start(bf16[4,96,640]{2,1,0:T(8,128)(2,1)} %get-tuple-element.246), channel_id=1, source_target_pairs={{0,4},{4,0},{8,12},{12,8},{16,20},{20,16},{24,28},{28,24},{1,5},{5... | collective-permute-start | bytes 1474568 | tf_op jit(solution)/shard_map/ppermute | solution.py:640
  169.5 6.6 %collective-permute-start.51 = (bf16[320,768]{1,0:T(8,128)(2,1)S(1)}, bf16[320,768]{1,0:T(8,128)(2,1)S(1)}, u32[]{:S(2)}, u32[]{:S(2)}) collective-permute-start(bf16[320,768]{1,0:T(8,128)(2,1)S(1)} %copy-done.7), channel_id=1, source_target_pairs={{0,1},{1,0},{2,3},{3,2},{4,5},{5,4},{6,7},{7,6},{8,9},{9,8},{10,11... | collective-permute-start | bytes 1474568 | tf_op jit(solution)/shard_map/ppermute | solution.py:640
  169.7 6.4 %collective-permute-start.52 = (bf16[320,768]{1,0:T(8,128)(2,1)S(1)}, bf16[320,768]{1,0:T(8,128)(2,1)S(1)}, u32[]{:S(2)}, u32[]{:S(2)}) collective-permute-start(bf16[320,768]{1,0:T(8,128)(2,1)S(1)} %copy-done.9), channel_id=1, source_target_pairs={{0,1},{1,0},{2,3},{3,2},{4,5},{5,4},{6,7},{7,6},{8,9},{9,8},{10,11... | collective-permute-start | bytes 1474568 | tf_op jit(solution)/shard_map/ppermute | solution.py:640
  172.4 23.4 %collective-permute-start.53 = (bf16[2,256,768]{2,1,0:T(8,128)(2,1)S(1)}, bf16[2,256,768]{2,1,0:T(8,128)(2,1)S(1)}, u32[]{:S(2)}, u32[]{:S(2)}) collective-permute-start(bf16[2,256,768]{2,1,0:T(8,128)(2,1)S(1)} %add_convert_fusion.1), channel_id=1, source_target_pairs={{0,2},{1,3},{2,0},{3,1},{4,6},{5,7},{6,4},{7,5},{8,10},{9,11},{10,... | collective-permute-start | bytes 2359304 | tf_op jit(solution)/shard_map/ppermute | solution.py:640
  181.5 8.1 %collective-permute-start.57 = (bf16[96,640]{1,0:T(8,128)(2,1)S(1)}, bf16[96,640]{1,0:T(8,128)(2,1)S(1)}, u32[]{:S(2)}, u32[]{:S(2)}) collective-permute-start(bf16[96,640]{1,0:T(8,128)(2,1)S(1)} %get-tuple-element.268), channel_id=1, source_target_pairs={{0,24},{4,28},{8,16},{12,20},{16,8},{20,12},{24,0},{28,4},{1,25},{... | collective-permute-start | bytes 368648 | tf_op jit(solution)/shard_map/ppermute | solution.py:640
  185.1 10.6 %collective-permute-start.56 = (bf16[96,640]{1,0:T(8,128)(2,1)S(1)}, bf16[96,640]{1,0:T(8,128)(2,1)S(1)}, u32[]{:S(2)}, u32[]{:S(2)}) collective-permute-start(bf16[96,640]{1,0:T(8,128)(2,1)S(1)} %get-tuple-element.269), channel_id=1, source_target_pairs={{0,16},{4,20},{8,24},{12,28},{16,0},{20,4},{24,8},{28,12},{1,17},{... | collective-permute-start | bytes 368648 | tf_op jit(solution)/shard_map/ppermute | solution.py:640
  185.1 10.6 %collective-permute-start.55 = (bf16[96,640]{1,0:T(8,128)(2,1)S(1)}, bf16[96,640]{1,0:T(8,128)(2,1)S(1)}, u32[]{:S(2)}, u32[]{:S(2)}) collective-permute-start(bf16[96,640]{1,0:T(8,128)(2,1)S(1)} %get-tuple-element.270), channel_id=1, source_target_pairs={{0,8},{4,12},{8,0},{12,4},{16,24},{20,28},{24,16},{28,20},{1,9},{5... | collective-permute-start | bytes 368648 | tf_op jit(solution)/shard_map/ppermute | solution.py:640
  187.9 17.2 %collective-permute-start.61 = (bf16[768,384]{1,0:T(8,128)(2,1)}, bf16[768,384]{1,0:T(8,128)(2,1)}, u32[]{:S(2)}, u32[]{:S(2)}) collective-permute-start(bf16[768,384]{1,0:T(8,128)(2,1)} %add_convert_fusion.2), channel_id=1, source_target_pairs={{0,2},{1,3},{2,0},{3,1},{4,6},{5,7},{6,4},{7,5},{8,10},{9,11},{10,... | collective-permute-start | bytes 1769480 | tf_op jit(solution)/shard_map/ppermute | solution.py:640
  189.7 15.4 %collective-permute-start.62 = (bf16[768,384]{1,0:T(8,128)(2,1)}, bf16[768,384]{1,0:T(8,128)(2,1)}, u32[]{:S(2)}, u32[]{:S(2)}) collective-permute-start(bf16[768,384]{1,0:T(8,128)(2,1)} %get-tuple-element.260), channel_id=1, source_target_pairs={{0,4},{4,0},{8,12},{12,8},{16,20},{20,16},{24,28},{28,24},{1,5},{5... | collective-permute-start | bytes 1769480 | tf_op jit(solution)/shard_map/ppermute | solution.py:640
  (67 other events, 390.8 us)

commit v4 on v3

--- a/solution.py
+++ b/solution.py
@@ -44,13 +44,13 @@
 ANY = pl.BlockSpec(memory_space=pl.ANY)
 
 
-def call(kernel, name, outs, in_specs, args, scratch=(), cost=1):
+def call(kernel, name, outs, in_specs, args, scratch=(), cost=1, out_specs=None):
     return pl.pallas_call(
         kernel,
         name=name,
         out_shape=list(outs),
         in_specs=in_specs,
-        out_specs=[VM] * len(outs),
+        out_specs=[VM] * len(outs) if out_specs is None else out_specs,
         scratch_shapes=list(scratch),
         compiler_params=pltpu.CompilerParams(
             vmem_limit_bytes=VMEM_WHOLE if name in ALONE else VMEM_BYTES
@@ -179,10 +179,10 @@
 def attend_kernel(count, *refs):
     gy_ref, gx_ref, mask_ref, x_ref, extras_ref, table_ref, brev_ref, pos_ref = refs[:8]
     pieces = refs[8 : 8 + count]
-    h1_ref, qkv_ref, prob_ref, mixed_ref, s0_ref, s1_ref, s2_ref, s3_ref = refs[
-        8 + count : 16 + count
+    h1_out, qkv_out, prob_out, mixed_ref, s0_ref, s1_ref, s2_ref, s3_ref, w_out = refs[
+        8 + count : 17 + count
     ]
-    w_ref, toep_ref, sems = refs[16 + count :]
+    toep_ref, h1_ref, qkv_ref, prob_ref, w_ref, sems, out_sems = refs[17 + count :]
     copies = assemble(pieces, gx_ref, w_ref, sems)
     seq = x_ref.shape[0]
     width = mixed_ref.shape[1]
@@ -192,6 +192,8 @@
     gain = jnp.transpose(extras_ref[...].astype(F32))[0:1]
     for copy in copies:
         copy.wait()
+    leaving = [pltpu.make_async_copy(w_ref, w_out, out_sems.at[0])]
+    leaving[0].start()
     for i in range(blocks):
         rows = pl.ds(i * BLOCK, BLOCK)
         x = x_ref[rows, :].astype(F32)
@@ -202,6 +204,9 @@
         qkv_ref[rows, :] = jnp.concatenate(
             [out[:, :width].astype(BF) * jnp.asarray(0.125, BF), out[:, width:].astype(BF)], axis=1
         )
+    for source, target in ((h1_ref, h1_out), (qkv_ref, qkv_out)):
+        leaving.append(pltpu.make_async_copy(source, target, out_sems.at[len(leaving)]))
+        leaving[-1].start()
     bucket_count = table_ref.shape[1]
     biases = []
     for k in range(blocks):
@@ -247,11 +252,20 @@
                 part = mm(prob, value)
                 acc = part if acc is None else acc + part
             mixed_ref[pl.ds(i * BLOCK, BLOCK), at : at + head] = acc.astype(BF)
+        done = pl.ds(h * (blocks * (blocks + 1) // 2), blocks * (blocks + 1) // 2)
+        leaving.append(
+            pltpu.make_async_copy(
+                prob_ref.at[done], prob_out.at[done], out_sems.at[len(leaving)]
+            )
+        )
+        leaving[-1].start()
     own = s0_ref.shape[0] * 2 // 3
     mixed = mixed_ref[...]
     for j, ref in enumerate((s0_ref, s1_ref, s2_ref, s3_ref)):
         start = jnp.bitwise_xor(gy_ref[0], j) * own
         ref[...] = fold(mm(one_hot_rows(pos_ref[...], start, own), mixed).astype(BF))
+    for copy in leaving:
+        copy.wait()
 
 
 def route_kernel(experts, pieces, *refs):
@@ -488,16 +502,28 @@
 
 def attend_back_kernel(count, *refs):
     gy_ref, gx_ref, g0_ref, g1_ref, g2_ref, g3_ref = refs[:6]
-    pos_ref, prob_ref, qkv_ref, h1_ref, x_ref, w_ref, extras_ref, brev_ref = refs[6:14]
+    pos_ref, prob_in, qkv_ref, h1_in, x_in, w_in, extras_ref, brev_ref = refs[6:14]
     d2_ref, small_ref = refs[14:16]
     dw_refs = refs[16 : 16 + count]
-    keep_ref, send_ref, table_ref, gm_ref, grads_ref, dw_buf = refs[16 + count :]
+    keep_ref, send_ref, table_ref, gm_ref, grads_ref, dw_buf = refs[16 + count : 22 + count]
+    prob_ref, h1_ref, x_ref, w_ref, sems = refs[22 + count :]
     seq, width = gm_ref.shape
     blocks = seq // BLOCK
     head = 64
     heads = width // head
     own = g0_ref.shape[0] * 2 // 3
     gy = gy_ref[0]
+    per_head = blocks * (blocks + 1) // 2
+    coming = []
+    for h in range(heads):
+        cut = pl.ds(h * per_head, per_head)
+        coming.append(
+            pltpu.make_async_copy(prob_in.at[cut], prob_ref.at[cut], sems.at[len(coming)])
+        )
+    for source, target in ((w_in, w_ref), (x_in, x_ref), (h1_in, h1_ref)):
+        coming.append(pltpu.make_async_copy(source, target, sems.at[len(coming)]))
+    for copy in coming:
+        copy.start()
     pieces = [unfold(ref[...]) for ref in (g0_ref, g1_ref, g2_ref, g3_ref)]
     for i in range(blocks):
         rows = pl.ds(i * BLOCK, BLOCK)
@@ -510,6 +536,7 @@
     sums = [[None] * heads for _ in range(blocks)]
     for h in range(heads):
         at = h * head
+        coming[h].wait()
         diagonals = [None] * blocks
         grad_keys = [None] * blocks
         grad_values = [None] * blocks
@@ -559,6 +586,8 @@
         part = mm_nt(hot, lines, HIGH)
         columns = part if columns is None else columns + part
     table_ref[...] = columns
+    for copy in coming[heads:]:
+        copy.wait()
     gain_total = None
     weights = w_ref[...]
     gain = jnp.transpose(extras_ref[...].astype(F32))[0:1]
@@ -824,8 +853,14 @@
         ),
         scratch=[
             pltpu.VMEM((blocks, BLOCK, BLOCK), F32),
+            pltpu.VMEM((seq, model), BF),
+            pltpu.VMEM((seq, 3 * width), BF),
+            pltpu.VMEM((heads * pairs, BLOCK, BLOCK), BF),
+            pltpu.VMEM((model, 3 * width), BF),
             pltpu.SemaphoreType.DMA((parts,)),
+            pltpu.SemaphoreType.DMA((3 + heads,)),
         ],
+        out_specs=[ANY] * 3 + [VM] * 5 + [ANY],
         cost=60,
     )
     mixed_pieces = [sorted_parts[0]] + [swap(sorted_parts[j], "gy", j) for j in (1, 2, 3)]
@@ -1009,7 +1044,7 @@
             struct((2, BLOCK, model), BF),
             struct((bucket_count, 8), F32),
         ],
-        [SM, SM] + [VM] * 14,
+        [SM, SM] + [VM] * 5 + [ANY, VM, ANY, ANY, ANY] + [VM] * 4,
         (
             gy,
             gx,
@@ -1029,6 +1064,11 @@
             pltpu.VMEM((seq, width), BF),
             pltpu.VMEM((seq, 3 * width), BF),
             pltpu.VMEM((model, 3 * width + spare), BF),
+            pltpu.VMEM((heads * pairs, BLOCK, BLOCK), BF),
+            pltpu.VMEM((seq, model), BF),
+            pltpu.VMEM((seq, model), BF),
+            pltpu.VMEM((model, 3 * width), BF),
+            pltpu.SemaphoreType.DMA((heads + 3,)),
         ],
         cost=60,
     )

time: 213 us -> 212 us (level)
  waiting for transfers between devices: 38.9 us -> 42.8 us
  starting transfers between devices: 71.2 us -> 68.4 us
  Pallas kernels: 73.8 us -> 71.4 us
    ppermute x49, waiting for transfers between devices: 35.4 us -> 39.4 us  [swap(): return lax.ppermute(x, axis, [(i, i ^ bit) for i in range(size)])]
    pallas_call x17, Pallas kernels: 73.8 us -> 71.4 us  [call(): pl.pallas_call(kernel, name=name, out_shape=list(outs), in_specs=in_specs...]
  transfers between devices with their start and end apart: 64 -> 64, of which waited for: 18 -> 19; matrix products, arithmetic and copies ran while one was open for 7% -> 7% of each run, Pallas kernels for 32% -> 31%
where the time goes in v4:
time: 212 us; the launch traced here: 209 us
  Pallas kernels  71.4 us (34%)
  starting transfers between devices  68.4 us (32%)
  waiting for transfers between devices  42.8 us (20%)
  other arithmetic  14.1 us (7%)
  local copies, waits for them, and re-layouts  10.6 us (5%)
    pallas_call x17, Pallas kernels, call(): pl.pallas_call(kernel, name=name, out_shape=list(outs), in_specs=in_specs...  71.4 us
    ppermute x49, starting transfers between devices, swap(): return lax.ppermute(x, axis, [(i, i ^ bit) for i in range(size)])  47.9 us
    ppermute x49, waiting for transfers between devices, swap(): return lax.ppermute(x, axis, [(i, i ^ bit) for i in range(size)])  39.4 us
    ppermute x6, starting transfers between devices, gather_rows(): up[n] = lax.ppermute(up[n], 'gx', ahead)  7.17 us
    unnamed x102, local copies, waits for them, and re-layouts  6.53 us
    ppermute x6, starting transfers between devices, gather_rows(): down[n] = lax.ppermute(down[n], 'gx', back)  5.22 us
    all_to_all x1, starting transfers between devices, on_device(): lax.all_to_all(projected, 'gx', split_axis=0, concat_axis=0, tiled=True)  4.86 us
  transfers between devices with their start and end apart: 64, of which 19 were waited for; matrix products, arithmetic and copies ran while one was open for 7% of the time, Pallas kernels for 31%

profile of v4, /device:TPU:0, one launch (start us, length us, event | category | flops | bytes accessed | tf_op | source)
XLA Modules:
  0.0 209.0 jit_solution(13615808738431540169)
XLA Ops:
  0.7 1.7 pack.1
  3.6 3.0 %collective-permute-start.7 = (bf16[1536,384]{1,0:T(8,128)(2,1)S(1)}, bf16[1536,384]{1,0:T(8,128)(2,1)}, u32[]{:S(2)}, u32[]{:S(2)}) collective-permute-start(bf16[1536,384]{1,0:T(8,128)(2,1)S(1)} %pad_maximum_fusion.refs_4_.refs_6_), channel_id=1, source_target_pairs={{0,2},{1,3},{2,0},{3,1},{4,6},{5,7},{6,4},{7,5},{8,10},{9,11},{10,... | collective-permute-start | bytes 3538952 | tf_op jit(solution)/shard_map/ppermute | solution.py:669
  6.6 1.5 collective-permute-start.1
  8.6 1.5 collective-permute-start.9
  13.6 1.6 collective-permute-start.2
  15.8 1.6 collective-permute-start.10
  18.5 1.5 collective-permute-start.4
  21.7 1.5 collective-permute-start.12
  23.7 1.5 collective-permute-start.6
  25.2 2.3 %collective-permute-done.5.refs_7_ = bf16[96,320]{1,0:T(8,128)(2,1)S(1)} collective-permute-done((bf16[96,320]{1,0:T(8,128)(2,1)S(1)}, bf16[96,320]{1,0:T(8,128)(2,1)S(1)}, u32[]{:S(2)}, u32[]{:S(2)}) %collective-permute-start.5) | collective-permute-done | bytes 61472 | tf_op jit(solution)/shard_map/ppermute | solution.py:692
  28.2 1.8 collective-permute-start.14
  30.6 2.1 %unpack.1 = (bf16[768,128]{1,0:T(8,128)(2,1)}, bf16[768,192]{1,0:T(8,128)(2,1)}) custom-call(s32[1]{0:T(128)} %bitcast.1.gx_ref.refs_0_.refs_1_, bf16[96,320]{1,0:T(8,128)(2,1)} %get-tuple-element.142.refs_1_, bf16[96,320]{1,0:T(8,128)(2,1)} %copy-done.45, bf16[96,320]{1,0:T(8,128)(2,1)} %copy-done.44, bf16[96,320]{1,0:T(8,128)(2,1)} %copy-done.46, ...), custom_call_target="tpu_custom_call" | custom-call | flops 2300000000 | bytes 1 | tf_op jit(solution)/shard_map/unpack/pallas_call | solution.py:48
  35.2 12.8 %attend.1 = (bf16[1024,768]{1,0:T(8,128)(2,1)}, bf16[1024,576]{1,0:T(8,128)(2,1)}, bf16[30,256,256]{2,1,0:T(8,128)(2,1)}, bf16[1024,192]{1,0:T(8,128)(2,1)}, bf1...) custom-call(s32[1]{0:T(128)} %bitcast.refs_0_.gy_ref, ...), custom_call_target="tpu_custom_call" | custom-call | flops 69000003584 | bytes 1 | tf_op jit(solution)/shard_map/attend/pallas_call | solution.py:48
  48.2 1.5 collective-permute-start.18
  51.8 1.5 collective-permute-start.29
  54.6 1.5 collective-permute-done.19.refs_3_.refs_16_
  56.1 1.6 route.1
  57.7 1.6 collective-permute-start.23
  59.3 2.6 %collective-permute-start.24 = (bf16[80,768]{1,0:T(8,128)(2,1)S(1)}, bf16[80,768]{1,0:T(8,128)(2,1)S(1)}, u32[]{:S(2)}, u32[]{:S(2)}) collective-permute-start(bf16[80,768]{1,0:T(8,128)(2,1)S(1)} %get-tuple-element.168.refs_25_), channel_id=1, source_target_pairs={{0,16},{4,20},{8,24},{12,28},{16,0},{20,4},{24,8},{28,12},{1,17},{... | collective-permute-start | bytes 368648 | tf_op jit(solution)/shard_map/ppermute | solution.py:669
  62.6 3.3 %collective-permute-done.23.refs_1_.refs_8_ = bf16[80,768]{1,0:T(8,128)(2,1)S(1)} collective-permute-done((bf16[80,768]{1,0:T(8,128)(2,1)S(1)}, bf16[80,768]{1,0:T(8,128)(2,1)S(1)}, u32[]{:S(2)}, u32[]{:S(2)}) %collective-permute-start.23) | collective-permute-done | bytes 122912 | tf_op jit(solution)/shard_map/ppermute | solution.py:669
  65.9 5.7 %collective-permute-done.24.refs_2_.refs_9_ = bf16[80,768]{1,0:T(8,128)(2,1)S(1)} collective-permute-done((bf16[80,768]{1,0:T(8,128)(2,1)S(1)}, bf16[80,768]{1,0:T(8,128)(2,1)S(1)}, u32[]{:S(2)}, u32[]{:S(2)}) %collective-permute-start.24) | collective-permute-done | bytes 122912 | tf_op jit(solution)/shard_map/ppermute | solution.py:669
  71.7 2.7 %collective-permute-start.26 = (bf16[80,768]{1,0:T(8,128)(2,1)S(1)}, bf16[80,768]{1,0:T(8,128)(2,1)S(1)}, u32[]{:S(2)}, u32[]{:S(2)}) collective-permute-start(bf16[80,768]{1,0:T(8,128)(2,1)S(1)} %get-tuple-element.171), channel_id=1, source_target_pairs={{0,8},{4,12},{8,0},{12,4},{16,24},{20,28},{24,16},{28,20},{1,9},{5... | collective-permute-start | bytes 368648 | tf_op jit(solution)/shard_map/ppermute | solution.py:669
  76.9 4.2 %expert_near.1 = (f32[320,768]{1,0:T(8,128)S(1)}, bf16[320,1536]{1,0:T(8,128)(2,1)S(1)}, bf16[320,1536]{1,0:T(8,128)(2,1)S(1)}) custom-call(bf16[80,768]{1,0:T(8,128)(2,1)S(1)} %get-tuple-element.166.refs_0_.refs_7_.refs_23_, bf16[80,768]{1,0:T(8,128)(2,1)S(1)} %collective-permute-done.23.refs_1_.refs_8_, ...), custom_call_target="tpu_custom_call" | custom-call | flops 8049999872 | bytes 1 | tf_op jit(solution)/shard_map/expert_near/pallas_call | solution.py:48
  81.1 6.3 %collective-permute-done.29.refs_7_.refs_12_ = bf16[1536,384]{1,0:T(8,128)(2,1)S(1)} collective-permute-done((bf16[1536,384]{1,0:T(8,128)(2,1)}, bf16[1536,384]{1,0:T(8,128)(2,1)S(1)}, u32[]{:S(2)}, u32[]{:S(2)}) %collective-permute-start.29) | collective-permute-done | bytes 1179680 | tf_op jit(solution)/shard_map/ppermute | solution.py:669
  87.6 2.8 %collective-permute-done.32.refs_8_.refs_13_ = bf16[1536,384]{1,0:T(8,128)(2,1)S(1)} collective-permute-done((bf16[1536,384]{1,0:T(8,128)(2,1)S(1)}, bf16[1536,384]{1,0:T(8,128)(2,1)S(1)}, u32[]{:S(2)}, u32[]{:S(2)}) %collective-permute-start.32) | collective-permute-done | bytes 1179680 | tf_op jit(solution)/shard_map/ppermute | solution.py:669
  90.4 3.5 %expert_far.1 = (bf16[80,768]{1,0:T(8,128)(2,1)S(1)}, bf16[80,768]{1,0:T(8,128)(2,1)S(1)}, bf16[80,768]{1,0:T(8,128)(2,1)S(1)}, bf16[80,768]{1,0:T(8,128)(2,1)S(...) custom-call(bf16[80,768]{1,0:T(8,128)(2,1)S(1)} %get-tuple-element.166.refs_0_.refs_7_.refs_23_, ...), custom_call_target="tpu_custom_call" | custom-call | flops 8625000448 | bytes 1 | tf_op jit(solution)/shard_map/expert_far/pallas_call | solution.py:48
  95.5 1.6 collective-permute-start.37
  97.1 2.5 %collective-permute-start.38 = (bf16[80,768]{1,0:T(8,128)(2,1)S(1)}, bf16[80,768]{1,0:T(8,128)(2,1)S(1)}, u32[]{:S(2)}, u32[]{:S(2)}) collective-permute-start(bf16[80,768]{1,0:T(8,128)(2,1)S(1)} %get-tuple-element.194), channel_id=1, source_target_pairs={{0,16},{4,20},{8,24},{12,28},{16,0},{20,4},{24,8},{28,12},{1,17},{... | collective-permute-start | bytes 368648 | tf_op jit(solution)/shard_map/ppermute | solution.py:669
  100.0 6.8 %expert_back.1 = (bf16[80,768]{1,0:T(8,128)(2,1)S(1)}, bf16[80,768]{1,0:T(8,128)(2,1)S(1)}, bf16[80,768]{1,0:T(8,128)(2,1)S(1)}, bf16[80,768]{1,0:T(8,128)(2,1)S(1)}, bf16[320,3072]{1,0:T(8,128)(2,1)S(1)}) custom-call(bf16[80,768]{1,0:T(8,128)(2,1)S(1)} %get-tuple-element.170.refs_0_, bf16[80,768]{1,0:T(8,128)(2,1)S(1)} %collective-permute-done.26.refs_1_, ...), custom_call_target="tpu_custom_call" | custom-call | flops 13799999488 | bytes 1 | tf_op jit(solution)/shard_map/expert_back/pallas_call | solution.py:48
  107.5 3.4 %collective-permute-start.34 = (bf16[80,768]{1,0:T(8,128)(2,1)S(1)}, bf16[80,768]{1,0:T(8,128)(2,1)S(1)}, u32[]{:S(2)}, u32[]{:S(2)}) collective-permute-start(bf16[80,768]{1,0:T(8,128)(2,1)S(1)} %get-tuple-element.189), channel_id=1, source_target_pairs={{0,16},{4,20},{8,24},{12,28},{16,0},{20,4},{24,8},{28,12},{1,17},{... | collective-permute-start | bytes 368648 | tf_op jit(solution)/shard_map/ppermute | solution.py:669
  112.0 3.8 %fill_rows.1 = (f32[384,768]{1,0:T(8,128)S(1)}, bf16[384,768]{1,0:T(8,128)(2,1)S(1)}, bf16[384,768]{1,0:T(8,128)(2,1)S(1)}, bf16[384,768]{1,0:T(8,128)(2,1)}, bf...) custom-call(bf16[80,768]{1,0:T(8,128)(2,1)S(1)} %get-tuple-element.1, ...), custom_call_target="tpu_custom_call" | custom-call | flops 14949999616 | bytes 1 | tf_op jit(solution)/shard_map/fill_rows/pallas_call | solution.py:48
  116.4 3.8 %collective-permute-done.34.refs_2_ = bf16[80,768]{1,0:T(8,128)(2,1)S(1)} collective-permute-done((bf16[80,768]{1,0:T(8,128)(2,1)S(1)}, bf16[80,768]{1,0:T(8,128)(2,1)S(1)}, u32[]{:S(2)}, u32[]{:S(2)}) %collective-permute-start.34) | collective-permute-done | bytes 122912 | tf_op jit(solution)/shard_map/ppermute | solution.py:669
  120.3 1.9 combine.1
  124.7 2.5 %outer_in_held.1 = (f32[768,384]{1,0:T(8,128)S(1)}, bf16[768,384]{1,0:T(8,128)(2,1)S(1)}, bf16[768,384]{1,0:T(8,128)(2,1)S(1)}, bf16[768,384]{1,0:T(8,128)(2,1)}) custom-call(bf16[80,768]{1,0:T(8,128)(2,1)S(1)} %get-tuple-element.166.refs_0_.refs_7_.refs_23_, bf16[80,768]{1,0:T(8,128)(2,1)S(1)} %collective-permute-done.23.refs_1_.refs_8_, ...), custom_call_target="tpu_custom_call" | custom-call | flops 1150000000 | bytes 1 | tf_op jit(solution)/shard_map/outer_in_held/pallas_call | solution.py:48
  128.0 1.5 collective-permute-done.44.refs_4_
  132.2 4.9 %all-to-all-start = ((bf16[8,96,384]{2,1,0:T(8,128)(2,1)}), bf16[8,96,384]{2,1,0:T(8,128)(2,1)}, u32[]{:S(2)}, u32[]{:S(2)}) async-start(bf16[8,96,384]{2,1,0:T(8,128)(2,1)} %bitcast.32), calls=%async_computation | async-start | bytes 1179648 | tf_op jit(solution)/shard_map/all_to_all | solution.py:1031
  139.1 2.0 collective-permute-start.46
  141.2 18.2 %attend_back.1 = (bf16[4,96,640]{2,1,0:T(8,128)(2,1)}, bf16[4,96,640]{2,1,0:T(8,128)(2,1)}, bf16[2,256,768]{2,1,0:T(8,128)(2,1)}, bf16[2,256,768]{2,1,0:T(8,128)(2,1)}, f32[32,8]{1,0:T(8,128)}) custom-call(s32[1]{0:T(128)} %bitcast.refs_0_.gy_ref, s32[1]{0:T(128)} %bitcast.1.gx_ref.refs_0_.refs_1_, bf16[480,128]{1,0:T(8,128)(2,1)} %copy-done.22, ...), custom_call_target="tpu_custom_call" | custom-call | flops 69000003584 | bytes 1 | tf_op jit(solution)/shard_map/attend_back/pallas_call | solution.py:48
  160.2 3.5 %collective-permute-done.47 = bf16[384,768]{1,0:T(8,128)(2,1)S(1)} collective-permute-done((bf16[384,768]{1,0:T(8,128)(2,1)}, bf16[384,768]{1,0:T(8,128)(2,1)S(1)}, u32[]{:S(2)}, u32[]{:S(2)}) %collective-permute-start.47) | collective-permute-done | bytes 589856 | tf_op jit(solution)/shard_map/ppermute | solution.py:669
  164.5 1.8 collective-permute-start.54
  168.9 2.3 %add_bitcast_fusion = f32[1,384,768]{2,1,0:T(8,128)} fusion(bf16[384,768]{1,0:T(8,128)(2,1)S(1)} %copy-done.26, f32[384,768]{1,0:T(8,128)S(1)} %get-tuple-element.263, bf16[384,768]{1,0:T(8,128)(2,1)} %collective-permute-done.48), kind=kLoop, calls=%fused_computation.4 | loop fusion | flops 1179648 | bytes 3538944 | tf_op jit(solution)/shard_map/broadcast_in_dim | solution.py:1147
  172.7 2.0 add_convert_fusion.2
  174.7 5.1 %unsort.1 = f32[1024,768]{1,0:T(8,128)} custom-call(s32[1]{0:T(128)} %bitcast.refs_0_.gy_ref, s32[1024,1]{1,0:T(8,128)S(1)} %copy-done.5, bf16[1024,768]{1,0:T(8,128)(2,1)S(1)} %copy-done.1, bf16[320,768]{1,0:T(8,128)(2,1)S(1)} %copy-done.7, bf16[320,768]{1,0:T(8,128)(2,1)S(1)} %collective-permute-done.51.d1_ref, bf16[320,768]{1,0:T(8,128)(2,1)S(1)} %copy-done.9, ...), custom_call_target="tpu_custom_call" | custom-call | flops 1150000000 | bytes 1 | tf_op jit(solution)/shard_map/unsort/pallas_call | solution.py:48
  180.1 3.6 %collective-permute-start.57 = (bf16[96,640]{1,0:T(8,128)(2,1)S(1)}, bf16[96,640]{1,0:T(8,128)(2,1)S(1)}, u32[]{:S(2)}, u32[]{:S(2)}) collective-permute-start(bf16[96,640]{1,0:T(8,128)(2,1)S(1)} %get-tuple-element.268), channel_id=1, source_target_pairs={{0,24},{4,28},{8,16},{12,20},{16,8},{20,12},{24,0},{28,4},{1,25},{... | collective-permute-start | bytes 368648 | tf_op jit(solution)/shard_map/ppermute | solution.py:669
  188.2 1.7 collective-permute-start.62
  189.9 4.4 %collective-permute-done.56 = bf16[96,640]{1,0:T(8,128)(2,1)S(1)} collective-permute-done((bf16[96,640]{1,0:T(8,128)(2,1)S(1)}, bf16[96,640]{1,0:T(8,128)(2,1)S(1)}, u32[]{:S(2)}, u32[]{:S(2)}) %collective-permute-start.56) | collective-permute-done | bytes 122912 | tf_op jit(solution)/shard_map/ppermute | solution.py:669
  200.7 3.1 %finish.1 = f32[1024,768]{1,0:T(8,128)} custom-call(s32[1]{0:T(128)} %bitcast.refs_0_.gy_ref, bf16[2,256,768]{2,1,0:T(8,128)(2,1)S(1)} %add_convert_fusion.own_ref, bf16[2,256,768]{2,1,0:T(8,128)(2,1)} %collective-permute-done.58.other_ref, bf16[1024,768]{1,0:T(8,128)(2,1)S(1)} %copy-done.3), custom_call_target="tpu_custom_call" | custom-call | flops 1150000000 | bytes 1 | tf_op jit(solution)/shard_map/finish/pallas_call | solution.py:48
  206.3 2.4 %add_bitcast_fusion.1 = f32[1,768,384]{2,1,0:T(8,128)} fusion(bf16[768,384]{1,0:T(8,128)(2,1)} %collective-permute-done.61, f32[768,384]{1,0:T(8,128)S(1)} %get-tuple-element.207, bf16[768,384]{1,0:T(8,128)(2,1)} %collective-permute-done.62), kind=kLoop, calls=%fused_computation.5 | loop fusion | flops 1179648 | bytes 3538944 | tf_op jit(solution)/shard_map/broadcast_in_dim | solution.py:1146
  (227 shorter events, 51.3 us)
Async XLA Ops:
  3.6 30.2 %collective-permute-start.7 = (bf16[1536,384]{1,0:T(8,128)(2,1)S(1)}, bf16[1536,384]{1,0:T(8,128)(2,1)}, u32[]{:S(2)}, u32[]{:S(2)}) collective-permute-start(bf16[1536,384]{1,0:T(8,128)(2,1)S(1)} %pad_maximum_fusion.refs_4_.refs_6_), channel_id=1, source_target_pairs={{0,2},{1,3},{2,0},{3,1},{4,6},{5,7},{6,4},{7,5},{8,10},{9,11},{10,... | collective-permute-start | bytes 3538952 | tf_op jit(solution)/shard_map/ppermute | solution.py:669
  6.6 8.7 %collective-permute-start.1 = (bf16[96,320]{1,0:T(8,128)(2,1)S(1)}, bf16[96,320]{1,0:T(8,128)(2,1)S(1)}, u32[]{:S(2)}, u32[]{:S(2)}) collective-permute-start(bf16[96,320]{1,0:T(8,128)(2,1)S(1)} %copy-done.43), channel_id=1, source_target_pairs={{8,0},{16,8},{24,16},{28,24},{20,28},{12,20},{4,12},{0,4},{9,1},{1... | collective-permute-start | bytes 184328 | tf_op jit(solution)/shard_map/ppermute | solution.py:692
  8.6 12.6 %collective-permute-start.9 = (bf16[96,576]{1,0:T(8,128)(2,1)S(1)}, bf16[96,576]{1,0:T(8,128)(2,1)S(1)}, u32[]{:S(2)}, u32[]{:S(2)}) collective-permute-start(bf16[96,576]{1,0:T(8,128)(2,1)S(1)} %copy-done.32), channel_id=1, source_target_pairs={{8,0},{16,8},{24,16},{28,24},{20,28},{12,20},{4,12},{0,4},{9,1},{1... | collective-permute-start | bytes 331784 | tf_op jit(solution)/shard_map/ppermute | solution.py:692
  15.3 7.9 %collective-permute-start.3 = (bf16[96,320]{1,0:T(8,128)(2,1)S(1)}, bf16[96,320]{1,0:T(8,128)(2,1)S(1)}, u32[]{:S(2)}, u32[]{:S(2)}) collective-permute-start(bf16[96,320]{1,0:T(8,128)(2,1)S(1)} %collective-permute-done.1.refs_3_), channel_id=1, source_target_pairs={{8,0},{16,8},{24,16},{28,24},{20,28},{12,20},{4,12},{0,4},{9,1},{1... | collective-permute-start | bytes 184328 | tf_op jit(solution)/shard_map/ppermute | solution.py:692
  21.2 6.4 %collective-permute-start.11 = (bf16[96,576]{1,0:T(8,128)(2,1)S(1)}, bf16[96,576]{1,0:T(8,128)(2,1)S(1)}, u32[]{:S(2)}, u32[]{:S(2)}) collective-permute-start(bf16[96,576]{1,0:T(8,128)(2,1)S(1)} %collective-permute-done.9.refs_10_), channel_id=1, source_target_pairs={{8,0},{16,8},{24,16},{28,24},{20,28},{12,20},{4,12},{0,4},{9,1},{1... | collective-permute-start | bytes 331784 | tf_op jit(solution)/shard_map/ppermute | solution.py:692
  21.7 6.5 %collective-permute-start.12 = (bf16[96,576]{1,0:T(8,128)(2,1)S(1)}, bf16[96,576]{1,0:T(8,128)(2,1)S(1)}, u32[]{:S(2)}, u32[]{:S(2)}) collective-permute-start(bf16[96,576]{1,0:T(8,128)(2,1)S(1)} %collective-permute-done.10.refs_11_), channel_id=1, source_target_pairs={{0,8},{8,16},{16,24},{24,28},{28,20},{20,12},{12,4},{4,0},{1,9},{9... | collective-permute-start | bytes 331784 | tf_op jit(solution)/shard_map/ppermute | solution.py:691
  27.6 22.2 %collective-permute-start.15 = (bf16[1536,384]{1,0:T(8,128)(2,1)S(1)}, bf16[1536,384]{1,0:T(8,128)(2,1)S(1)}, u32[]{:S(2)}, u32[]{:S(2)}) collective-permute-start(bf16[1536,384]{1,0:T(8,128)(2,1)S(1)} %pad_maximum_fusion.refs_4_.refs_6_), channel_id=1, source_target_pairs={{0,1},{1,0},{2,3},{3,2},{4,5},{5,4},{6,7},{7,6},{8,9},{9,8},{10,11... | collective-permute-start | bytes 3538952 | tf_op jit(solution)/shard_map/ppermute | solution.py:669
  27.6 6.2 %collective-permute-start.13 = (bf16[96,576]{1,0:T(8,128)(2,1)S(1)}, bf16[96,576]{1,0:T(8,128)(2,1)S(1)}, u32[]{:S(2)}, u32[]{:S(2)}) collective-permute-start(bf16[96,576]{1,0:T(8,128)(2,1)S(1)} %collective-permute-done.11.refs_12_), channel_id=1, source_target_pairs={{8,0},{16,8},{24,16},{28,24},{20,28},{12,20},{4,12},{0,4},{9,1},{1... | collective-permute-start | bytes 331784 | tf_op jit(solution)/shard_map/ppermute | solution.py:692
  28.2 6.3 %collective-permute-start.14 = (bf16[96,576]{1,0:T(8,128)(2,1)S(1)}, bf16[96,576]{1,0:T(8,128)(2,1)S(1)}, u32[]{:S(2)}, u32[]{:S(2)}) collective-permute-start(bf16[96,576]{1,0:T(8,128)(2,1)S(1)} %collective-permute-done.12.refs_13_), channel_id=1, source_target_pairs={{0,8},{8,16},{16,24},{24,28},{28,20},{20,12},{12,4},{4,0},{1,9},{9... | collective-permute-start | bytes 331784 | tf_op jit(solution)/shard_map/ppermute | solution.py:696
  32.8 15.2 %collective-permute-start.21 = (bf16[768,192]{1,0:T(8,128)(2,1)}, bf16[768,192]{1,0:T(8,128)(2,1)S(1)}, u32[]{:S(2)}, u32[]{:S(2)}) collective-permute-start(bf16[768,192]{1,0:T(8,128)(2,1)} %get-tuple-element.155.refs_4_.refs_9_), channel_id=1, source_target_pairs={{0,2},{1,3},{2,0},{3,1},{4,6},{5,7},{6,4},{7,5},{8,10},{9,11},{10,... | collective-permute-start | bytes 884744 | tf_op jit(solution)/shard_map/ppermute | solution.py:669
  33.8 14.4 %collective-permute-start.20 = (bf16[768,192]{1,0:T(8,128)(2,1)}, bf16[768,192]{1,0:T(8,128)(2,1)S(1)}, u32[]{:S(2)}, u32[]{:S(2)}) collective-permute-start(bf16[768,192]{1,0:T(8,128)(2,1)} %get-tuple-element.155.refs_4_.refs_9_), channel_id=1, source_target_pairs={{0,1},{1,0},{2,3},{3,2},{4,5},{5,4},{6,7},{7,6},{8,9},{9,8},{10,11... | collective-permute-start | bytes 884744 | tf_op jit(solution)/shard_map/ppermute | solution.py:669
  33.8 28.8 %collective-permute-start.30 = (bf16[1536,384]{1,0:T(8,128)(2,1)S(1)}, bf16[1536,384]{1,0:T(8,128)(2,1)S(1)}, u32[]{:S(2)}, u32[]{:S(2)}) collective-permute-start(bf16[1536,384]{1,0:T(8,128)(2,1)S(1)} %pad_maximum_fusion.refs_4_.refs_6_), channel_id=1, source_target_pairs={{0,4},{4,0},{8,12},{12,8},{16,20},{20,16},{24,28},{28,24},{1,5},{5... | collective-permute-start | bytes 3538952 | tf_op jit(solution)/shard_map/ppermute | solution.py:669
  34.5 15.4 %collective-permute-start.16 = (bf16[1536,384]{1,0:T(8,128)(2,1)}, bf16[1536,384]{1,0:T(8,128)(2,1)}, u32[]{:S(2)}, u32[]{:S(2)}) collective-permute-start(bf16[1536,384]{1,0:T(8,128)(2,1)} %collective-permute-done.7.refs_6_.refs_8_), channel_id=1, source_target_pairs={{0,1},{1,0},{2,3},{3,2},{4,5},{5,4},{6,7},{7,6},{8,9},{9,8},{10,11... | collective-permute-start | bytes 3538952 | tf_op jit(solution)/shard_map/ppermute | solution.py:669
  48.2 6.4 %collective-permute-start.18 = (bf16[480,128]{1,0:T(8,128)(2,1)}, bf16[480,128]{1,0:T(8,128)(2,1)S(1)}, u32[]{:S(2)}, u32[]{:S(2)}) collective-permute-start(bf16[480,128]{1,0:T(8,128)(2,1)} %get-tuple-element.153), channel_id=1, source_target_pairs={{0,2},{1,3},{2,0},{3,1},{4,6},{5,7},{6,4},{7,5},{8,10},{9,11},{10,... | collective-permute-start | bytes 368648 | tf_op jit(solution)/shard_map/ppermute | solution.py:669
  49.7 6.4 %collective-permute-start.19 = (bf16[480,128]{1,0:T(8,128)(2,1)}, bf16[480,128]{1,0:T(8,128)(2,1)S(1)}, u32[]{:S(2)}, u32[]{:S(2)}) collective-permute-start(bf16[480,128]{1,0:T(8,128)(2,1)} %get-tuple-element.154), channel_id=1, source_target_pairs={{0,3},{1,2},{2,1},{3,0},{4,7},{5,6},{6,5},{7,4},{8,11},{9,10},{10,... | collective-permute-start | bytes 368648 | tf_op jit(solution)/shard_map/ppermute | solution.py:669
  51.8 35.7 %collective-permute-start.29 = (bf16[1536,384]{1,0:T(8,128)(2,1)}, bf16[1536,384]{1,0:T(8,128)(2,1)S(1)}, u32[]{:S(2)}, u32[]{:S(2)}) collective-permute-start(bf16[1536,384]{1,0:T(8,128)(2,1)} %collective-permute-done.7.refs_6_.refs_8_), channel_id=1, source_target_pairs={{0,4},{4,0},{8,12},{12,8},{16,20},{20,16},{24,28},{28,24},{1,5},{5... | collective-permute-start | bytes 3538952 | tf_op jit(solution)/shard_map/ppermute | solution.py:669
  57.7 8.2 %collective-permute-start.23 = (bf16[80,768]{1,0:T(8,128)(2,1)S(1)}, bf16[80,768]{1,0:T(8,128)(2,1)S(1)}, u32[]{:S(2)}, u32[]{:S(2)}) collective-permute-start(bf16[80,768]{1,0:T(8,128)(2,1)S(1)} %get-tuple-element.167.refs_24_), channel_id=1, source_target_pairs={{0,8},{4,12},{8,0},{12,4},{16,24},{20,28},{24,16},{28,20},{1,9},{5... | collective-permute-start | bytes 368648 | tf_op jit(solution)/shard_map/ppermute | solution.py:669
  59.3 12.3 %collective-permute-start.24 = (bf16[80,768]{1,0:T(8,128)(2,1)S(1)}, bf16[80,768]{1,0:T(8,128)(2,1)S(1)}, u32[]{:S(2)}, u32[]{:S(2)}) collective-permute-start(bf16[80,768]{1,0:T(8,128)(2,1)S(1)} %get-tuple-element.168.refs_25_), channel_id=1, source_target_pairs={{0,16},{4,20},{8,24},{12,28},{16,0},{20,4},{24,8},{28,12},{1,17},{... | collective-permute-start | bytes 368648 | tf_op jit(solution)/shard_map/ppermute | solution.py:669
  61.9 9.8 %collective-permute-start.25 = (bf16[80,768]{1,0:T(8,128)(2,1)S(1)}, bf16[80,768]{1,0:T(8,128)(2,1)S(1)}, u32[]{:S(2)}, u32[]{:S(2)}) collective-permute-start(bf16[80,768]{1,0:T(8,128)(2,1)S(1)} %get-tuple-element.169.refs_26_), channel_id=1, source_target_pairs={{0,24},{4,28},{8,16},{12,20},{16,8},{20,12},{24,0},{28,4},{1,25},{... | collective-permute-start | bytes 368648 | tf_op jit(solution)/shard_map/ppermute | solution.py:669
  62.6 24.9 %collective-permute-start.31 = (bf16[1536,384]{1,0:T(8,128)(2,1)S(1)}, bf16[1536,384]{1,0:T(8,128)(2,1)S(1)}, u32[]{:S(2)}, u32[]{:S(2)}) collective-permute-start(bf16[1536,384]{1,0:T(8,128)(2,1)S(1)} %collective-permute-done.30.refs_5_.refs_10_), channel_id=1, source_target_pairs={{0,1},{1,0},{2,3},{3,2},{4,5},{5,4},{6,7},{7,6},{8,9},{9,8},{10,11... | collective-permute-start | bytes 3538952 | tf_op jit(solution)/shard_map/ppermute | solution.py:669
  71.7 15.8 %collective-permute-start.26 = (bf16[80,768]{1,0:T(8,128)(2,1)S(1)}, bf16[80,768]{1,0:T(8,128)(2,1)S(1)}, u32[]{:S(2)}, u32[]{:S(2)}) collective-permute-start(bf16[80,768]{1,0:T(8,128)(2,1)S(1)} %get-tuple-element.171), channel_id=1, source_target_pairs={{0,8},{4,12},{8,0},{12,4},{16,24},{20,28},{24,16},{28,20},{1,9},{5... | collective-permute-start | bytes 368648 | tf_op jit(solution)/shard_map/ppermute | solution.py:669
  74.4 13.1 %collective-permute-start.27 = (bf16[80,768]{1,0:T(8,128)(2,1)S(1)}, bf16[80,768]{1,0:T(8,128)(2,1)S(1)}, u32[]{:S(2)}, u32[]{:S(2)}) collective-permute-start(bf16[80,768]{1,0:T(8,128)(2,1)S(1)} %get-tuple-element.172), channel_id=1, source_target_pairs={{0,16},{4,20},{8,24},{12,28},{16,0},{20,4},{24,8},{28,12},{1,17},{... | collective-permute-start | bytes 368648 | tf_op jit(solution)/shard_map/ppermute | solution.py:669
  75.4 12.1 %collective-permute-start.28 = (bf16[80,768]{1,0:T(8,128)(2,1)S(1)}, bf16[80,768]{1,0:T(8,128)(2,1)S(1)}, u32[]{:S(2)}, u32[]{:S(2)}) collective-permute-start(bf16[80,768]{1,0:T(8,128)(2,1)S(1)} %get-tuple-element.173), channel_id=1, source_target_pairs={{0,24},{4,28},{8,16},{12,20},{16,8},{20,12},{24,0},{28,4},{1,25},{... | collective-permute-start | bytes 368648 | tf_op jit(solution)/shard_map/ppermute | solution.py:669
  95.4 16.7 %collective-permute-start.36 = (bf16[4,384,768]{2,1,0:T(8,128)(2,1)S(1)}, bf16[4,384,768]{2,1,0:T(8,128)(2,1)S(1)}, u32[]{:S(2)}, u32[]{:S(2)}) collective-permute-start(bf16[4,384,768]{2,1,0:T(8,128)(2,1)S(1)} %outer_out_sent.1), channel_id=1, source_target_pairs={{0,1},{1,0},{2,3},{3,2},{4,5},{5,4},{6,7},{7,6},{8,9},{9,8},{10,11... | collective-permute-start | bytes 7077896 | tf_op jit(solution)/shard_map/ppermute | solution.py:669
  95.5 11.9 %collective-permute-start.37 = (bf16[80,768]{1,0:T(8,128)(2,1)S(1)}, bf16[80,768]{1,0:T(8,128)(2,1)S(1)}, u32[]{:S(2)}, u32[]{:S(2)}) collective-permute-start(bf16[80,768]{1,0:T(8,128)(2,1)S(1)} %get-tuple-element.193), channel_id=1, source_target_pairs={{0,8},{4,12},{8,0},{12,4},{16,24},{20,28},{24,16},{28,20},{1,9},{5... | collective-permute-start | bytes 368648 | tf_op jit(solution)/shard_map/ppermute | solution.py:669
  97.1 13.8 %collective-permute-start.38 = (bf16[80,768]{1,0:T(8,128)(2,1)S(1)}, bf16[80,768]{1,0:T(8,128)(2,1)S(1)}, u32[]{:S(2)}, u32[]{:S(2)}) collective-permute-start(bf16[80,768]{1,0:T(8,128)(2,1)S(1)} %get-tuple-element.194), channel_id=1, source_target_pairs={{0,16},{4,20},{8,24},{12,28},{16,0},{20,4},{24,8},{28,12},{1,17},{... | collective-permute-start | bytes 368648 | tf_op jit(solution)/shard_map/ppermute | solution.py:669
  99.7 12.3 %collective-permute-start.39 = (bf16[80,768]{1,0:T(8,128)(2,1)S(1)}, bf16[80,768]{1,0:T(8,128)(2,1)S(1)}, u32[]{:S(2)}, u32[]{:S(2)}) collective-permute-start(bf16[80,768]{1,0:T(8,128)(2,1)S(1)} %get-tuple-element.195), channel_id=1, source_target_pairs={{0,24},{4,28},{8,16},{12,20},{16,8},{20,12},{24,0},{28,4},{1,25},{... | collective-permute-start | bytes 368648 | tf_op jit(solution)/shard_map/ppermute | solution.py:669
  106.7 9.7 %collective-permute-start.33 = (bf16[80,768]{1,0:T(8,128)(2,1)S(1)}, bf16[80,768]{1,0:T(8,128)(2,1)S(1)}, u32[]{:S(2)}, u32[]{:S(2)}) collective-permute-start(bf16[80,768]{1,0:T(8,128)(2,1)S(1)} %get-tuple-element.188), channel_id=1, source_target_pairs={{0,8},{4,12},{8,0},{12,4},{16,24},{20,28},{24,16},{28,20},{1,9},{5... | collective-permute-start | bytes 368648 | tf_op jit(solution)/shard_map/ppermute | solution.py:669
  107.5 12.8 %collective-permute-start.34 = (bf16[80,768]{1,0:T(8,128)(2,1)S(1)}, bf16[80,768]{1,0:T(8,128)(2,1)S(1)}, u32[]{:S(2)}, u32[]{:S(2)}) collective-permute-start(bf16[80,768]{1,0:T(8,128)(2,1)S(1)} %get-tuple-element.189), channel_id=1, source_target_pairs={{0,16},{4,20},{8,24},{12,28},{16,0},{20,4},{24,8},{28,12},{1,17},{... | collective-permute-start | bytes 368648 | tf_op jit(solution)/shard_map/ppermute | solution.py:669
  110.9 9.4 %collective-permute-start.35 = (bf16[80,768]{1,0:T(8,128)(2,1)S(1)}, bf16[80,768]{1,0:T(8,128)(2,1)S(1)}, u32[]{:S(2)}, u32[]{:S(2)}) collective-permute-start(bf16[80,768]{1,0:T(8,128)(2,1)S(1)} %get-tuple-element.190), channel_id=1, source_target_pairs={{0,24},{4,28},{8,16},{12,20},{16,8},{20,12},{24,0},{28,4},{1,25},{... | collective-permute-start | bytes 368648 | tf_op jit(solution)/shard_map/ppermute | solution.py:669
  115.8 14.4 %collective-permute-start.41 = (bf16[384,768]{1,0:T(8,128)(2,1)S(1)}, bf16[384,768]{1,0:T(8,128)(2,1)S(1)}, u32[]{:S(2)}, u32[]{:S(2)}) collective-permute-start(bf16[384,768]{1,0:T(8,128)(2,1)S(1)} %get-tuple-element.206), channel_id=1, source_target_pairs={{0,4},{4,0},{8,12},{12,8},{16,20},{20,16},{24,28},{28,24},{1,5},{5... | collective-permute-start | bytes 1769480 | tf_op jit(solution)/shard_map/ppermute | solution.py:669
  116.4 8.0 %collective-permute-start.40 = (bf16[4,768,384]{2,1,0:T(8,128)(2,1)S(1)}, bf16[4,768,384]{2,1,0:T(8,128)(2,1)S(1)}, u32[]{:S(2)}, u32[]{:S(2)}) collective-permute-start(bf16[4,768,384]{2,1,0:T(8,128)(2,1)S(1)} %get-tuple-element.203), channel_id=1, source_target_pairs={{0,1},{1,0},{2,3},{3,2},{4,5},{5,4},{6,7},{7,6},{8,9},{9,8},{10,11... | collective-permute-start | bytes 7077896 | tf_op jit(solution)/shard_map/ppermute | solution.py:669
  122.8 8.4 %collective-permute-start.42 = (bf16[768,384]{1,0:T(8,128)(2,1)S(1)}, bf16[768,384]{1,0:T(8,128)(2,1)S(1)}, u32[]{:S(2)}, u32[]{:S(2)}) collective-permute-start(bf16[768,384]{1,0:T(8,128)(2,1)S(1)} %get-tuple-element.211), channel_id=1, source_target_pairs={{0,1},{1,0},{2,3},{3,2},{4,5},{5,4},{6,7},{7,6},{8,9},{9,8},{10,11... | collective-permute-start | bytes 1769480 | tf_op jit(solution)/shard_map/ppermute | solution.py:669
  123.3 6.2 %collective-permute-start.44 = (bf16[480,128]{1,0:T(8,128)(2,1)S(1)}, bf16[480,128]{1,0:T(8,128)(2,1)S(1)}, u32[]{:S(2)}, u32[]{:S(2)}) collective-permute-start(bf16[480,128]{1,0:T(8,128)(2,1)S(1)} %get-tuple-element.214), channel_id=1, source_target_pairs={{0,2},{1,3},{2,0},{3,1},{4,6},{5,7},{6,4},{7,5},{8,10},{9,11},{10,... | collective-permute-start | bytes 368648 | tf_op jit(solution)/shard_map/ppermute | solution.py:669
  127.2 32.2 %collective-permute-start.48 = (bf16[384,768]{1,0:T(8,128)(2,1)}, bf16[384,768]{1,0:T(8,128)(2,1)}, u32[]{:S(2)}, u32[]{:S(2)}) collective-permute-start(bf16[384,768]{1,0:T(8,128)(2,1)} %get-tuple-element.229), channel_id=1, source_target_pairs={{0,4},{4,0},{8,12},{12,8},{16,20},{20,16},{24,28},{28,24},{1,5},{5... | collective-permute-start | bytes 1769480 | tf_op jit(solution)/shard_map/ppermute | solution.py:669
  132.2 32.3 %all-to-all-start = ((bf16[8,96,384]{2,1,0:T(8,128)(2,1)}), bf16[8,96,384]{2,1,0:T(8,128)(2,1)}, u32[]{:S(2)}, u32[]{:S(2)}) async-start(bf16[8,96,384]{2,1,0:T(8,128)(2,1)} %bitcast.32), calls=%async_computation | async-start | bytes 1179648 | tf_op jit(solution)/shard_map/all_to_all | solution.py:1031
  137.1 22.3 %collective-permute-start.49 = (bf16[320,768]{1,0:T(8,128)(2,1)S(1)}, bf16[320,768]{1,0:T(8,128)(2,1)S(1)}, u32[]{:S(2)}, u32[]{:S(2)}) collective-permute-start(bf16[320,768]{1,0:T(8,128)(2,1)S(1)} %copy-done.7), channel_id=1, source_target_pairs={{0,2},{1,3},{2,0},{3,1},{4,6},{5,7},{6,4},{7,5},{8,10},{9,11},{10,... | collective-permute-start | bytes 1474568 | tf_op jit(solution)/shard_map/ppermute | solution.py:669
  138.4 25.2 %collective-permute-start.47 = (bf16[384,768]{1,0:T(8,128)(2,1)}, bf16[384,768]{1,0:T(8,128)(2,1)S(1)}, u32[]{:S(2)}, u32[]{:S(2)}) collective-permute-start(bf16[384,768]{1,0:T(8,128)(2,1)} %add_convert_fusion.4), channel_id=1, source_target_pairs={{0,2},{1,3},{2,0},{3,1},{4,6},{5,7},{6,4},{7,5},{8,10},{9,11},{10,... | collective-permute-start | bytes 1769480 | tf_op jit(solution)/shard_map/ppermute | solution.py:669
  139.1 25.3 %collective-permute-start.46 = (bf16[768,384]{1,0:T(8,128)(2,1)}, bf16[768,384]{1,0:T(8,128)(2,1)}, u32[]{:S(2)}, u32[]{:S(2)}) collective-permute-start(bf16[768,384]{1,0:T(8,128)(2,1)} %copy-done.12), channel_id=1, source_target_pairs={{0,4},{4,0},{8,12},{12,8},{16,20},{20,16},{24,28},{28,24},{1,5},{5... | collective-permute-start | bytes 1769480 | tf_op jit(solution)/shard_map/ppermute | solution.py:669
  164.5 15.3 %collective-permute-start.54 = (bf16[4,96,640]{2,1,0:T(8,128)(2,1)}, bf16[4,96,640]{2,1,0:T(8,128)(2,1)S(1)}, u32[]{:S(2)}, u32[]{:S(2)}) collective-permute-start(bf16[4,96,640]{2,1,0:T(8,128)(2,1)} %get-tuple-element.246), channel_id=1, source_target_pairs={{0,4},{4,0},{8,12},{12,8},{16,20},{20,16},{24,28},{28,24},{1,5},{5... | collective-permute-start | bytes 1474568 | tf_op jit(solution)/shard_map/ppermute | solution.py:669
  168.3 6.4 %collective-permute-start.51 = (bf16[320,768]{1,0:T(8,128)(2,1)S(1)}, bf16[320,768]{1,0:T(8,128)(2,1)S(1)}, u32[]{:S(2)}, u32[]{:S(2)}) collective-permute-start(bf16[320,768]{1,0:T(8,128)(2,1)S(1)} %copy-done.7), channel_id=1, source_target_pairs={{0,1},{1,0},{2,3},{3,2},{4,5},{5,4},{6,7},{7,6},{8,9},{9,8},{10,11... | collective-permute-start | bytes 1474568 | tf_op jit(solution)/shard_map/ppermute | solution.py:669
  171.2 23.1 %collective-permute-start.53 = (bf16[2,256,768]{2,1,0:T(8,128)(2,1)S(1)}, bf16[2,256,768]{2,1,0:T(8,128)(2,1)S(1)}, u32[]{:S(2)}, u32[]{:S(2)}) collective-permute-start(bf16[2,256,768]{2,1,0:T(8,128)(2,1)S(1)} %add_convert_fusion.1), channel_id=1, source_target_pairs={{0,2},{1,3},{2,0},{3,1},{4,6},{5,7},{6,4},{7,5},{8,10},{9,11},{10,... | collective-permute-start | bytes 2359304 | tf_op jit(solution)/shard_map/ppermute | solution.py:669
  180.1 8.1 %collective-permute-start.57 = (bf16[96,640]{1,0:T(8,128)(2,1)S(1)}, bf16[96,640]{1,0:T(8,128)(2,1)S(1)}, u32[]{:S(2)}, u32[]{:S(2)}) collective-permute-start(bf16[96,640]{1,0:T(8,128)(2,1)S(1)} %get-tuple-element.268), channel_id=1, source_target_pairs={{0,24},{4,28},{8,16},{12,20},{16,8},{20,12},{24,0},{28,4},{1,25},{... | collective-permute-start | bytes 368648 | tf_op jit(solution)/shard_map/ppermute | solution.py:669
  183.7 10.6 %collective-permute-start.56 = (bf16[96,640]{1,0:T(8,128)(2,1)S(1)}, bf16[96,640]{1,0:T(8,128)(2,1)S(1)}, u32[]{:S(2)}, u32[]{:S(2)}) collective-permute-start(bf16[96,640]{1,0:T(8,128)(2,1)S(1)} %get-tuple-element.269), channel_id=1, source_target_pairs={{0,16},{4,20},{8,24},{12,28},{16,0},{20,4},{24,8},{28,12},{1,17},{... | collective-permute-start | bytes 368648 | tf_op jit(solution)/shard_map/ppermute | solution.py:669
  183.7 10.6 %collective-permute-start.55 = (bf16[96,640]{1,0:T(8,128)(2,1)S(1)}, bf16[96,640]{1,0:T(8,128)(2,1)S(1)}, u32[]{:S(2)}, u32[]{:S(2)}) collective-permute-start(bf16[96,640]{1,0:T(8,128)(2,1)S(1)} %get-tuple-element.270), channel_id=1, source_target_pairs={{0,8},{4,12},{8,0},{12,4},{16,24},{20,28},{24,16},{28,20},{1,9},{5... | collective-permute-start | bytes 368648 | tf_op jit(solution)/shard_map/ppermute | solution.py:669
  186.4 17.8 %collective-permute-start.61 = (bf16[768,384]{1,0:T(8,128)(2,1)}, bf16[768,384]{1,0:T(8,128)(2,1)}, u32[]{:S(2)}, u32[]{:S(2)}) collective-permute-start(bf16[768,384]{1,0:T(8,128)(2,1)} %add_convert_fusion.2), channel_id=1, source_target_pairs={{0,2},{1,3},{2,0},{3,1},{4,6},{5,7},{6,4},{7,5},{8,10},{9,11},{10,... | collective-permute-start | bytes 1769480 | tf_op jit(solution)/shard_map/ppermute | solution.py:669
  188.2 16.0 %collective-permute-start.62 = (bf16[768,384]{1,0:T(8,128)(2,1)}, bf16[768,384]{1,0:T(8,128)(2,1)}, u32[]{:S(2)}, u32[]{:S(2)}) collective-permute-start(bf16[768,384]{1,0:T(8,128)(2,1)} %get-tuple-element.260), channel_id=1, source_target_pairs={{0,4},{4,0},{8,12},{12,8},{16,20},{20,16},{24,28},{28,24},{1,5},{5... | collective-permute-start | bytes 1769480 | tf_op jit(solution)/shard_map/ppermute | solution.py:669
  194.5 6.2 %collective-permute-start.58 = (bf16[2,256,768]{2,1,0:T(8,128)(2,1)S(1)}, bf16[2,256,768]{2,1,0:T(8,128)(2,1)}, u32[]{:S(2)}, u32[]{:S(2)}) collective-permute-start(bf16[2,256,768]{2,1,0:T(8,128)(2,1)S(1)} %add_convert_fusion.own_ref), channel_id=1, source_target_pairs={{0,1},{1,0},{2,3},{3,2},{4,5},{5,4},{6,7},{7,6},{8,9},{9,8},{10,11... | collective-permute-start | bytes 2359304 | tf_op jit(solution)/shard_map/ppermute | solution.py:669
  (67 other events, 385.5 us)

commit v5 on v4

--- a/solution.py
+++ b/solution.py
@@ -632,13 +632,16 @@
 def unsort_kernel(gy_ref, pos_ref, x_ref, d0_ref, d1_ref, d2_ref, d3_ref, out_ref):
     own = d0_ref.shape[0]
     gy = gy_ref[0]
+    every = jnp.concatenate([ref[...] for ref in (d0_ref, d1_ref, d2_ref, d3_ref)], axis=0)
     for i in range(x_ref.shape[0] // BLOCK):
         rows = pl.ds(i * BLOCK, BLOCK)
         pos = pos_ref[rows, :]
-        acc = x_ref[rows, :].astype(F32)
-        for j, ref in enumerate((d0_ref, d1_ref, d2_ref, d3_ref)):
-            acc = acc + mm(one_hot_cols(pos, jnp.bitwise_xor(gy, j) * own, own), ref[...])
-        out_ref[rows, :] = acc
+        near = pos
+        for j in range(4):
+            start = jnp.bitwise_xor(gy, j) * own
+            near = jnp.where((pos >= start) & (pos < start + own), pos - start + j * own, near)
+        hot = one_hot_cols(near, 0, 4 * own)
+        out_ref[rows, :] = x_ref[rows, :].astype(F32) + mm(hot, every)
 
 
 def finish_kernel(gy_ref, own_ref, other_ref, g_ref, out_ref):

time: 212 us -> 212 us (level)
  transfers between devices with their start and end apart: 64 -> 64, of which waited for: 19 -> 19; matrix products, arithmetic and copies ran while one was open for 7% -> 7% of each run, Pallas kernels for 31% -> 30%
where the time goes in v5:
time: 212 us; the launch traced here: 209 us
  Pallas kernels  70.4 us (33%)
  starting transfers between devices  68.8 us (32%)
  waiting for transfers between devices  43.5 us (21%)
  other arithmetic  14.1 us (7%)
  local copies, waits for them, and re-layouts  10.6 us (5%)
    pallas_call x17, Pallas kernels, call(): pl.pallas_call(kernel, name=name, out_shape=list(outs), in_specs=in_specs...  70.4 us
    ppermute x49, starting transfers between devices, swap(): return lax.ppermute(x, axis, [(i, i ^ bit) for i in range(size)])  48.3 us
    ppermute x49, waiting for transfers between devices, swap(): return lax.ppermute(x, axis, [(i, i ^ bit) for i in range(size)])  40 us
    ppermute x6, starting transfers between devices, gather_rows(): up[n] = lax.ppermute(up[n], 'gx', ahead)  7.17 us
    unnamed x102, local copies, waits for them, and re-layouts  6.53 us
    ppermute x6, starting transfers between devices, gather_rows(): down[n] = lax.ppermute(down[n], 'gx', back)  5.22 us
    all_to_all x1, starting transfers between devices, on_device(): lax.all_to_all(projected, 'gx', split_axis=0, concat_axis=0, tiled=True)  4.86 us
  transfers between devices with their start and end apart: 64, of which 19 were waited for; matrix products, arithmetic and copies ran while one was open for 7% of the time, Pallas kernels for 30%

profile of v5, /device:TPU:0, one launch (start us, length us, event | category | flops | bytes accessed | tf_op | source)
XLA Modules:
  0.0 209.0 jit_solution(4347133883818325258)
XLA Ops:
  0.7 1.7 pack.1
  3.6 3.0 %collective-permute-start.7 = (bf16[1536,384]{1,0:T(8,128)(2,1)S(1)}, bf16[1536,384]{1,0:T(8,128)(2,1)}, u32[]{:S(2)}, u32[]{:S(2)}) collective-permute-start(bf16[1536,384]{1,0:T(8,128)(2,1)S(1)} %pad_maximum_fusion.refs_4_.refs_6_), channel_id=1, source_target_pairs={{0,2},{1,3},{2,0},{3,1},{4,6},{5,7},{6,4},{7,5},{8,10},{9,11},{10,... | collective-permute-start | bytes 3538952 | tf_op jit(solution)/shard_map/ppermute | solution.py:672
  6.6 1.5 collective-permute-start.1
  8.6 1.5 collective-permute-start.9
  13.6 1.6 collective-permute-start.2
  15.8 1.6 collective-permute-start.10
  18.5 1.5 collective-permute-start.4
  21.7 1.5 collective-permute-start.12
  23.7 1.5 collective-permute-start.6
  25.2 2.3 %collective-permute-done.5.refs_7_ = bf16[96,320]{1,0:T(8,128)(2,1)S(1)} collective-permute-done((bf16[96,320]{1,0:T(8,128)(2,1)S(1)}, bf16[96,320]{1,0:T(8,128)(2,1)S(1)}, u32[]{:S(2)}, u32[]{:S(2)}) %collective-permute-start.5) | collective-permute-done | bytes 61472 | tf_op jit(solution)/shard_map/ppermute | solution.py:695
  28.2 1.8 collective-permute-start.14
  30.6 2.1 %unpack.1 = (bf16[768,128]{1,0:T(8,128)(2,1)}, bf16[768,192]{1,0:T(8,128)(2,1)}) custom-call(s32[1]{0:T(128)} %bitcast.1.gx_ref.refs_0_.refs_1_, bf16[96,320]{1,0:T(8,128)(2,1)} %get-tuple-element.142.refs_1_, bf16[96,320]{1,0:T(8,128)(2,1)} %copy-done.45, bf16[96,320]{1,0:T(8,128)(2,1)} %copy-done.44, bf16[96,320]{1,0:T(8,128)(2,1)} %copy-done.46, ...), custom_call_target="tpu_custom_call" | custom-call | flops 2300000000 | bytes 1 | tf_op jit(solution)/shard_map/unpack/pallas_call | solution.py:48
  35.2 12.8 %attend.1 = (bf16[1024,768]{1,0:T(8,128)(2,1)}, bf16[1024,576]{1,0:T(8,128)(2,1)}, bf16[30,256,256]{2,1,0:T(8,128)(2,1)}, bf16[1024,192]{1,0:T(8,128)(2,1)}, bf1...) custom-call(s32[1]{0:T(128)} %bitcast.refs_0_.gy_ref, ...), custom_call_target="tpu_custom_call" | custom-call | flops 69000003584 | bytes 1 | tf_op jit(solution)/shard_map/attend/pallas_call | solution.py:48
  48.2 1.5 collective-permute-start.18
  51.8 1.5 collective-permute-start.29
  54.6 1.5 collective-permute-done.19.refs_3_.refs_16_
  56.1 1.6 route.1
  57.7 1.6 collective-permute-start.23
  59.3 2.6 %collective-permute-start.24 = (bf16[80,768]{1,0:T(8,128)(2,1)S(1)}, bf16[80,768]{1,0:T(8,128)(2,1)S(1)}, u32[]{:S(2)}, u32[]{:S(2)}) collective-permute-start(bf16[80,768]{1,0:T(8,128)(2,1)S(1)} %get-tuple-element.168.refs_25_), channel_id=1, source_target_pairs={{0,16},{4,20},{8,24},{12,28},{16,0},{20,4},{24,8},{28,12},{1,17},{... | collective-permute-start | bytes 368648 | tf_op jit(solution)/shard_map/ppermute | solution.py:672
  62.6 3.3 %collective-permute-done.23.refs_1_.refs_8_ = bf16[80,768]{1,0:T(8,128)(2,1)S(1)} collective-permute-done((bf16[80,768]{1,0:T(8,128)(2,1)S(1)}, bf16[80,768]{1,0:T(8,128)(2,1)S(1)}, u32[]{:S(2)}, u32[]{:S(2)}) %collective-permute-start.23) | collective-permute-done | bytes 122912 | tf_op jit(solution)/shard_map/ppermute | solution.py:672
  65.9 5.7 %collective-permute-done.24.refs_2_.refs_9_ = bf16[80,768]{1,0:T(8,128)(2,1)S(1)} collective-permute-done((bf16[80,768]{1,0:T(8,128)(2,1)S(1)}, bf16[80,768]{1,0:T(8,128)(2,1)S(1)}, u32[]{:S(2)}, u32[]{:S(2)}) %collective-permute-start.24) | collective-permute-done | bytes 122912 | tf_op jit(solution)/shard_map/ppermute | solution.py:672
  71.7 2.7 %collective-permute-start.26 = (bf16[80,768]{1,0:T(8,128)(2,1)S(1)}, bf16[80,768]{1,0:T(8,128)(2,1)S(1)}, u32[]{:S(2)}, u32[]{:S(2)}) collective-permute-start(bf16[80,768]{1,0:T(8,128)(2,1)S(1)} %get-tuple-element.171), channel_id=1, source_target_pairs={{0,8},{4,12},{8,0},{12,4},{16,24},{20,28},{24,16},{28,20},{1,9},{5... | collective-permute-start | bytes 368648 | tf_op jit(solution)/shard_map/ppermute | solution.py:672
  76.9 4.2 %expert_near.1 = (f32[320,768]{1,0:T(8,128)S(1)}, bf16[320,1536]{1,0:T(8,128)(2,1)S(1)}, bf16[320,1536]{1,0:T(8,128)(2,1)S(1)}) custom-call(bf16[80,768]{1,0:T(8,128)(2,1)S(1)} %get-tuple-element.166.refs_0_.refs_7_.refs_23_, bf16[80,768]{1,0:T(8,128)(2,1)S(1)} %collective-permute-done.23.refs_1_.refs_8_, ...), custom_call_target="tpu_custom_call" | custom-call | flops 8049999872 | bytes 1 | tf_op jit(solution)/shard_map/expert_near/pallas_call | solution.py:48
  81.1 6.3 %collective-permute-done.29.refs_7_.refs_12_ = bf16[1536,384]{1,0:T(8,128)(2,1)S(1)} collective-permute-done((bf16[1536,384]{1,0:T(8,128)(2,1)}, bf16[1536,384]{1,0:T(8,128)(2,1)S(1)}, u32[]{:S(2)}, u32[]{:S(2)}) %collective-permute-start.29) | collective-permute-done | bytes 1179680 | tf_op jit(solution)/shard_map/ppermute | solution.py:672
  87.6 2.8 %collective-permute-done.32.refs_8_.refs_13_ = bf16[1536,384]{1,0:T(8,128)(2,1)S(1)} collective-permute-done((bf16[1536,384]{1,0:T(8,128)(2,1)S(1)}, bf16[1536,384]{1,0:T(8,128)(2,1)S(1)}, u32[]{:S(2)}, u32[]{:S(2)}) %collective-permute-start.32) | collective-permute-done | bytes 1179680 | tf_op jit(solution)/shard_map/ppermute | solution.py:672
  90.4 3.5 %expert_far.1 = (bf16[80,768]{1,0:T(8,128)(2,1)S(1)}, bf16[80,768]{1,0:T(8,128)(2,1)S(1)}, bf16[80,768]{1,0:T(8,128)(2,1)S(1)}, bf16[80,768]{1,0:T(8,128)(2,1)S(...) custom-call(bf16[80,768]{1,0:T(8,128)(2,1)S(1)} %get-tuple-element.166.refs_0_.refs_7_.refs_23_, ...), custom_call_target="tpu_custom_call" | custom-call | flops 8625000448 | bytes 1 | tf_op jit(solution)/shard_map/expert_far/pallas_call | solution.py:48
  95.5 1.6 collective-permute-start.37
  97.1 2.5 %collective-permute-start.38 = (bf16[80,768]{1,0:T(8,128)(2,1)S(1)}, bf16[80,768]{1,0:T(8,128)(2,1)S(1)}, u32[]{:S(2)}, u32[]{:S(2)}) collective-permute-start(bf16[80,768]{1,0:T(8,128)(2,1)S(1)} %get-tuple-element.194), channel_id=1, source_target_pairs={{0,16},{4,20},{8,24},{12,28},{16,0},{20,4},{24,8},{28,12},{1,17},{... | collective-permute-start | bytes 368648 | tf_op jit(solution)/shard_map/ppermute | solution.py:672
  100.0 6.8 %expert_back.1 = (bf16[80,768]{1,0:T(8,128)(2,1)S(1)}, bf16[80,768]{1,0:T(8,128)(2,1)S(1)}, bf16[80,768]{1,0:T(8,128)(2,1)S(1)}, bf16[80,768]{1,0:T(8,128)(2,1)S(1)}, bf16[320,3072]{1,0:T(8,128)(2,1)S(1)}) custom-call(bf16[80,768]{1,0:T(8,128)(2,1)S(1)} %get-tuple-element.170.refs_0_, bf16[80,768]{1,0:T(8,128)(2,1)S(1)} %collective-permute-done.26.refs_1_, ...), custom_call_target="tpu_custom_call" | custom-call | flops 13799999488 | bytes 1 | tf_op jit(solution)/shard_map/expert_back/pallas_call | solution.py:48
  107.5 3.4 %collective-permute-start.34 = (bf16[80,768]{1,0:T(8,128)(2,1)S(1)}, bf16[80,768]{1,0:T(8,128)(2,1)S(1)}, u32[]{:S(2)}, u32[]{:S(2)}) collective-permute-start(bf16[80,768]{1,0:T(8,128)(2,1)S(1)} %get-tuple-element.189), channel_id=1, source_target_pairs={{0,16},{4,20},{8,24},{12,28},{16,0},{20,4},{24,8},{28,12},{1,17},{... | collective-permute-start | bytes 368648 | tf_op jit(solution)/shard_map/ppermute | solution.py:672
  112.0 3.8 %fill_rows.1 = (f32[384,768]{1,0:T(8,128)S(1)}, bf16[384,768]{1,0:T(8,128)(2,1)S(1)}, bf16[384,768]{1,0:T(8,128)(2,1)S(1)}, bf16[384,768]{1,0:T(8,128)(2,1)}, bf...) custom-call(bf16[80,768]{1,0:T(8,128)(2,1)S(1)} %get-tuple-element.1, ...), custom_call_target="tpu_custom_call" | custom-call | flops 14949999616 | bytes 1 | tf_op jit(solution)/shard_map/fill_rows/pallas_call | solution.py:48
  116.4 3.8 %collective-permute-done.34.refs_2_ = bf16[80,768]{1,0:T(8,128)(2,1)S(1)} collective-permute-done((bf16[80,768]{1,0:T(8,128)(2,1)S(1)}, bf16[80,768]{1,0:T(8,128)(2,1)S(1)}, u32[]{:S(2)}, u32[]{:S(2)}) %collective-permute-start.34) | collective-permute-done | bytes 122912 | tf_op jit(solution)/shard_map/ppermute | solution.py:672
  120.3 1.9 combine.1
  124.7 2.5 %outer_in_held.1 = (f32[768,384]{1,0:T(8,128)S(1)}, bf16[768,384]{1,0:T(8,128)(2,1)S(1)}, bf16[768,384]{1,0:T(8,128)(2,1)S(1)}, bf16[768,384]{1,0:T(8,128)(2,1)}) custom-call(bf16[80,768]{1,0:T(8,128)(2,1)S(1)} %get-tuple-element.166.refs_0_.refs_7_.refs_23_, bf16[80,768]{1,0:T(8,128)(2,1)S(1)} %collective-permute-done.23.refs_1_.refs_8_, ...), custom_call_target="tpu_custom_call" | custom-call | flops 1150000000 | bytes 1 | tf_op jit(solution)/shard_map/outer_in_held/pallas_call | solution.py:48
  128.0 1.5 collective-permute-done.44.refs_4_
  132.2 4.9 %all-to-all-start = ((bf16[8,96,384]{2,1,0:T(8,128)(2,1)}), bf16[8,96,384]{2,1,0:T(8,128)(2,1)}, u32[]{:S(2)}, u32[]{:S(2)}) async-start(bf16[8,96,384]{2,1,0:T(8,128)(2,1)} %bitcast.32), calls=%async_computation | async-start | bytes 1179648 | tf_op jit(solution)/shard_map/all_to_all | solution.py:1034
  139.1 2.0 collective-permute-start.46
  141.2 18.2 %attend_back.1 = (bf16[4,96,640]{2,1,0:T(8,128)(2,1)}, bf16[4,96,640]{2,1,0:T(8,128)(2,1)}, bf16[2,256,768]{2,1,0:T(8,128)(2,1)}, bf16[2,256,768]{2,1,0:T(8,128)(2,1)}, f32[32,8]{1,0:T(8,128)}) custom-call(s32[1]{0:T(128)} %bitcast.refs_0_.gy_ref, s32[1]{0:T(128)} %bitcast.1.gx_ref.refs_0_.refs_1_, bf16[480,128]{1,0:T(8,128)(2,1)} %copy-done.22, ...), custom_call_target="tpu_custom_call" | custom-call | flops 69000003584 | bytes 1 | tf_op jit(solution)/shard_map/attend_back/pallas_call | solution.py:48
  160.2 3.5 %collective-permute-done.47 = bf16[384,768]{1,0:T(8,128)(2,1)S(1)} collective-permute-done((bf16[384,768]{1,0:T(8,128)(2,1)}, bf16[384,768]{1,0:T(8,128)(2,1)S(1)}, u32[]{:S(2)}, u32[]{:S(2)}) %collective-permute-start.47) | collective-permute-done | bytes 589856 | tf_op jit(solution)/shard_map/ppermute | solution.py:672
  164.5 1.8 collective-permute-start.54
  168.9 2.3 %add_bitcast_fusion = f32[1,384,768]{2,1,0:T(8,128)} fusion(bf16[384,768]{1,0:T(8,128)(2,1)S(1)} %copy-done.26, f32[384,768]{1,0:T(8,128)S(1)} %get-tuple-element.263, bf16[384,768]{1,0:T(8,128)(2,1)} %collective-permute-done.48), kind=kLoop, calls=%fused_computation.4 | loop fusion | flops 1179648 | bytes 3538944 | tf_op jit(solution)/shard_map/broadcast_in_dim | solution.py:1150
  172.7 2.0 add_convert_fusion.2
  174.7 4.2 %unsort.1 = f32[1024,768]{1,0:T(8,128)} custom-call(s32[1]{0:T(128)} %bitcast.refs_0_.gy_ref, s32[1024,1]{1,0:T(8,128)S(1)} %copy-done.5, bf16[1024,768]{1,0:T(8,128)(2,1)S(1)} %copy-done.1, bf16[320,768]{1,0:T(8,128)(2,1)S(1)} %copy-done.7, bf16[320,768]{1,0:T(8,128)(2,1)S(1)} %collective-permute-done.51.d1_ref, bf16[320,768]{1,0:T(8,128)(2,1)S(1)} %copy-done.9, ...), custom_call_target="tpu_custom_call" | custom-call | flops 1150000000 | bytes 1 | tf_op jit(solution)/shard_map/unsort/pallas_call | solution.py:48
  179.1 3.6 %collective-permute-start.57 = (bf16[96,640]{1,0:T(8,128)(2,1)S(1)}, bf16[96,640]{1,0:T(8,128)(2,1)S(1)}, u32[]{:S(2)}, u32[]{:S(2)}) collective-permute-start(bf16[96,640]{1,0:T(8,128)(2,1)S(1)} %get-tuple-element.268), channel_id=1, source_target_pairs={{0,24},{4,28},{8,16},{12,20},{16,8},{20,12},{24,0},{28,4},{1,25},{... | collective-permute-start | bytes 368648 | tf_op jit(solution)/shard_map/ppermute | solution.py:672
  187.2 1.7 collective-permute-start.62
  189.0 4.4 %collective-permute-done.56 = bf16[96,640]{1,0:T(8,128)(2,1)S(1)} collective-permute-done((bf16[96,640]{1,0:T(8,128)(2,1)S(1)}, bf16[96,640]{1,0:T(8,128)(2,1)S(1)}, u32[]{:S(2)}, u32[]{:S(2)}) %collective-permute-start.56) | collective-permute-done | bytes 122912 | tf_op jit(solution)/shard_map/ppermute | solution.py:672
  199.8 3.1 %finish.1 = f32[1024,768]{1,0:T(8,128)} custom-call(s32[1]{0:T(128)} %bitcast.refs_0_.gy_ref, bf16[2,256,768]{2,1,0:T(8,128)(2,1)S(1)} %add_convert_fusion.own_ref, bf16[2,256,768]{2,1,0:T(8,128)(2,1)} %collective-permute-done.58.other_ref, bf16[1024,768]{1,0:T(8,128)(2,1)S(1)} %copy-done.3), custom_call_target="tpu_custom_call" | custom-call | flops 1150000000 | bytes 1 | tf_op jit(solution)/shard_map/finish/pallas_call | solution.py:48
  206.3 2.4 %add_bitcast_fusion.1 = f32[1,768,384]{2,1,0:T(8,128)} fusion(bf16[768,384]{1,0:T(8,128)(2,1)} %collective-permute-done.61, f32[768,384]{1,0:T(8,128)S(1)} %get-tuple-element.207, bf16[768,384]{1,0:T(8,128)(2,1)} %collective-permute-done.62), kind=kLoop, calls=%fused_computation.5 | loop fusion | flops 1179648 | bytes 3538944 | tf_op jit(solution)/shard_map/broadcast_in_dim | solution.py:1149
  (227 shorter events, 52.2 us)
Async XLA Ops:
  3.6 30.2 %collective-permute-start.7 = (bf16[1536,384]{1,0:T(8,128)(2,1)S(1)}, bf16[1536,384]{1,0:T(8,128)(2,1)}, u32[]{:S(2)}, u32[]{:S(2)}) collective-permute-start(bf16[1536,384]{1,0:T(8,128)(2,1)S(1)} %pad_maximum_fusion.refs_4_.refs_6_), channel_id=1, source_target_pairs={{0,2},{1,3},{2,0},{3,1},{4,6},{5,7},{6,4},{7,5},{8,10},{9,11},{10,... | collective-permute-start | bytes 3538952 | tf_op jit(solution)/shard_map/ppermute | solution.py:672
  6.6 8.7 %collective-permute-start.1 = (bf16[96,320]{1,0:T(8,128)(2,1)S(1)}, bf16[96,320]{1,0:T(8,128)(2,1)S(1)}, u32[]{:S(2)}, u32[]{:S(2)}) collective-permute-start(bf16[96,320]{1,0:T(8,128)(2,1)S(1)} %copy-done.43), channel_id=1, source_target_pairs={{8,0},{16,8},{24,16},{28,24},{20,28},{12,20},{4,12},{0,4},{9,1},{1... | collective-permute-start | bytes 184328 | tf_op jit(solution)/shard_map/ppermute | solution.py:695
  8.6 12.6 %collective-permute-start.9 = (bf16[96,576]{1,0:T(8,128)(2,1)S(1)}, bf16[96,576]{1,0:T(8,128)(2,1)S(1)}, u32[]{:S(2)}, u32[]{:S(2)}) collective-permute-start(bf16[96,576]{1,0:T(8,128)(2,1)S(1)} %copy-done.32), channel_id=1, source_target_pairs={{8,0},{16,8},{24,16},{28,24},{20,28},{12,20},{4,12},{0,4},{9,1},{1... | collective-permute-start | bytes 331784 | tf_op jit(solution)/shard_map/ppermute | solution.py:695
  15.3 7.9 %collective-permute-start.3 = (bf16[96,320]{1,0:T(8,128)(2,1)S(1)}, bf16[96,320]{1,0:T(8,128)(2,1)S(1)}, u32[]{:S(2)}, u32[]{:S(2)}) collective-permute-start(bf16[96,320]{1,0:T(8,128)(2,1)S(1)} %collective-permute-done.1.refs_3_), channel_id=1, source_target_pairs={{8,0},{16,8},{24,16},{28,24},{20,28},{12,20},{4,12},{0,4},{9,1},{1... | collective-permute-start | bytes 184328 | tf_op jit(solution)/shard_map/ppermute | solution.py:695
  21.2 6.4 %collective-permute-start.11 = (bf16[96,576]{1,0:T(8,128)(2,1)S(1)}, bf16[96,576]{1,0:T(8,128)(2,1)S(1)}, u32[]{:S(2)}, u32[]{:S(2)}) collective-permute-start(bf16[96,576]{1,0:T(8,128)(2,1)S(1)} %collective-permute-done.9.refs_10_), channel_id=1, source_target_pairs={{8,0},{16,8},{24,16},{28,24},{20,28},{12,20},{4,12},{0,4},{9,1},{1... | collective-permute-start | bytes 331784 | tf_op jit(solution)/shard_map/ppermute | solution.py:695
  21.7 6.5 %collective-permute-start.12 = (bf16[96,576]{1,0:T(8,128)(2,1)S(1)}, bf16[96,576]{1,0:T(8,128)(2,1)S(1)}, u32[]{:S(2)}, u32[]{:S(2)}) collective-permute-start(bf16[96,576]{1,0:T(8,128)(2,1)S(1)} %collective-permute-done.10.refs_11_), channel_id=1, source_target_pairs={{0,8},{8,16},{16,24},{24,28},{28,20},{20,12},{12,4},{4,0},{1,9},{9... | collective-permute-start | bytes 331784 | tf_op jit(solution)/shard_map/ppermute | solution.py:694
  27.6 22.2 %collective-permute-start.15 = (bf16[1536,384]{1,0:T(8,128)(2,1)S(1)}, bf16[1536,384]{1,0:T(8,128)(2,1)S(1)}, u32[]{:S(2)}, u32[]{:S(2)}) collective-permute-start(bf16[1536,384]{1,0:T(8,128)(2,1)S(1)} %pad_maximum_fusion.refs_4_.refs_6_), channel_id=1, source_target_pairs={{0,1},{1,0},{2,3},{3,2},{4,5},{5,4},{6,7},{7,6},{8,9},{9,8},{10,11... | collective-permute-start | bytes 3538952 | tf_op jit(solution)/shard_map/ppermute | solution.py:672
  27.6 6.2 %collective-permute-start.13 = (bf16[96,576]{1,0:T(8,128)(2,1)S(1)}, bf16[96,576]{1,0:T(8,128)(2,1)S(1)}, u32[]{:S(2)}, u32[]{:S(2)}) collective-permute-start(bf16[96,576]{1,0:T(8,128)(2,1)S(1)} %collective-permute-done.11.refs_12_), channel_id=1, source_target_pairs={{8,0},{16,8},{24,16},{28,24},{20,28},{12,20},{4,12},{0,4},{9,1},{1... | collective-permute-start | bytes 331784 | tf_op jit(solution)/shard_map/ppermute | solution.py:695
  28.2 6.3 %collective-permute-start.14 = (bf16[96,576]{1,0:T(8,128)(2,1)S(1)}, bf16[96,576]{1,0:T(8,128)(2,1)S(1)}, u32[]{:S(2)}, u32[]{:S(2)}) collective-permute-start(bf16[96,576]{1,0:T(8,128)(2,1)S(1)} %collective-permute-done.12.refs_13_), channel_id=1, source_target_pairs={{0,8},{8,16},{16,24},{24,28},{28,20},{20,12},{12,4},{4,0},{1,9},{9... | collective-permute-start | bytes 331784 | tf_op jit(solution)/shard_map/ppermute | solution.py:699
  32.8 15.2 %collective-permute-start.21 = (bf16[768,192]{1,0:T(8,128)(2,1)}, bf16[768,192]{1,0:T(8,128)(2,1)S(1)}, u32[]{:S(2)}, u32[]{:S(2)}) collective-permute-start(bf16[768,192]{1,0:T(8,128)(2,1)} %get-tuple-element.155.refs_4_.refs_9_), channel_id=1, source_target_pairs={{0,2},{1,3},{2,0},{3,1},{4,6},{5,7},{6,4},{7,5},{8,10},{9,11},{10,... | collective-permute-start | bytes 884744 | tf_op jit(solution)/shard_map/ppermute | solution.py:672
  33.8 14.4 %collective-permute-start.20 = (bf16[768,192]{1,0:T(8,128)(2,1)}, bf16[768,192]{1,0:T(8,128)(2,1)S(1)}, u32[]{:S(2)}, u32[]{:S(2)}) collective-permute-start(bf16[768,192]{1,0:T(8,128)(2,1)} %get-tuple-element.155.refs_4_.refs_9_), channel_id=1, source_target_pairs={{0,1},{1,0},{2,3},{3,2},{4,5},{5,4},{6,7},{7,6},{8,9},{9,8},{10,11... | collective-permute-start | bytes 884744 | tf_op jit(solution)/shard_map/ppermute | solution.py:672
  33.8 28.8 %collective-permute-start.30 = (bf16[1536,384]{1,0:T(8,128)(2,1)S(1)}, bf16[1536,384]{1,0:T(8,128)(2,1)S(1)}, u32[]{:S(2)}, u32[]{:S(2)}) collective-permute-start(bf16[1536,384]{1,0:T(8,128)(2,1)S(1)} %pad_maximum_fusion.refs_4_.refs_6_), channel_id=1, source_target_pairs={{0,4},{4,0},{8,12},{12,8},{16,20},{20,16},{24,28},{28,24},{1,5},{5... | collective-permute-start | bytes 3538952 | tf_op jit(solution)/shard_map/ppermute | solution.py:672
  34.5 15.4 %collective-permute-start.16 = (bf16[1536,384]{1,0:T(8,128)(2,1)}, bf16[1536,384]{1,0:T(8,128)(2,1)}, u32[]{:S(2)}, u32[]{:S(2)}) collective-permute-start(bf16[1536,384]{1,0:T(8,128)(2,1)} %collective-permute-done.7.refs_6_.refs_8_), channel_id=1, source_target_pairs={{0,1},{1,0},{2,3},{3,2},{4,5},{5,4},{6,7},{7,6},{8,9},{9,8},{10,11... | collective-permute-start | bytes 3538952 | tf_op jit(solution)/shard_map/ppermute | solution.py:672
  48.2 6.4 %collective-permute-start.18 = (bf16[480,128]{1,0:T(8,128)(2,1)}, bf16[480,128]{1,0:T(8,128)(2,1)S(1)}, u32[]{:S(2)}, u32[]{:S(2)}) collective-permute-start(bf16[480,128]{1,0:T(8,128)(2,1)} %get-tuple-element.153), channel_id=1, source_target_pairs={{0,2},{1,3},{2,0},{3,1},{4,6},{5,7},{6,4},{7,5},{8,10},{9,11},{10,... | collective-permute-start | bytes 368648 | tf_op jit(solution)/shard_map/ppermute | solution.py:672
  49.7 6.4 %collective-permute-start.19 = (bf16[480,128]{1,0:T(8,128)(2,1)}, bf16[480,128]{1,0:T(8,128)(2,1)S(1)}, u32[]{:S(2)}, u32[]{:S(2)}) collective-permute-start(bf16[480,128]{1,0:T(8,128)(2,1)} %get-tuple-element.154), channel_id=1, source_target_pairs={{0,3},{1,2},{2,1},{3,0},{4,7},{5,6},{6,5},{7,4},{8,11},{9,10},{10,... | collective-permute-start | bytes 368648 | tf_op jit(solution)/shard_map/ppermute | solution.py:672
  51.8 35.7 %collective-permute-start.29 = (bf16[1536,384]{1,0:T(8,128)(2,1)}, bf16[1536,384]{1,0:T(8,128)(2,1)S(1)}, u32[]{:S(2)}, u32[]{:S(2)}) collective-permute-start(bf16[1536,384]{1,0:T(8,128)(2,1)} %collective-permute-done.7.refs_6_.refs_8_), channel_id=1, source_target_pairs={{0,4},{4,0},{8,12},{12,8},{16,20},{20,16},{24,28},{28,24},{1,5},{5... | collective-permute-start | bytes 3538952 | tf_op jit(solution)/shard_map/ppermute | solution.py:672
  57.7 8.2 %collective-permute-start.23 = (bf16[80,768]{1,0:T(8,128)(2,1)S(1)}, bf16[80,768]{1,0:T(8,128)(2,1)S(1)}, u32[]{:S(2)}, u32[]{:S(2)}) collective-permute-start(bf16[80,768]{1,0:T(8,128)(2,1)S(1)} %get-tuple-element.167.refs_24_), channel_id=1, source_target_pairs={{0,8},{4,12},{8,0},{12,4},{16,24},{20,28},{24,16},{28,20},{1,9},{5... | collective-permute-start | bytes 368648 | tf_op jit(solution)/shard_map/ppermute | solution.py:672
  59.3 12.3 %collective-permute-start.24 = (bf16[80,768]{1,0:T(8,128)(2,1)S(1)}, bf16[80,768]{1,0:T(8,128)(2,1)S(1)}, u32[]{:S(2)}, u32[]{:S(2)}) collective-permute-start(bf16[80,768]{1,0:T(8,128)(2,1)S(1)} %get-tuple-element.168.refs_25_), channel_id=1, source_target_pairs={{0,16},{4,20},{8,24},{12,28},{16,0},{20,4},{24,8},{28,12},{1,17},{... | collective-permute-start | bytes 368648 | tf_op jit(solution)/shard_map/ppermute | solution.py:672
  61.9 9.8 %collective-permute-start.25 = (bf16[80,768]{1,0:T(8,128)(2,1)S(1)}, bf16[80,768]{1,0:T(8,128)(2,1)S(1)}, u32[]{:S(2)}, u32[]{:S(2)}) collective-permute-start(bf16[80,768]{1,0:T(8,128)(2,1)S(1)} %get-tuple-element.169.refs_26_), channel_id=1, source_target_pairs={{0,24},{4,28},{8,16},{12,20},{16,8},{20,12},{24,0},{28,4},{1,25},{... | collective-permute-start | bytes 368648 | tf_op jit(solution)/shard_map/ppermute | solution.py:672
  62.6 24.9 %collective-permute-start.31 = (bf16[1536,384]{1,0:T(8,128)(2,1)S(1)}, bf16[1536,384]{1,0:T(8,128)(2,1)S(1)}, u32[]{:S(2)}, u32[]{:S(2)}) collective-permute-start(bf16[1536,384]{1,0:T(8,128)(2,1)S(1)} %collective-permute-done.30.refs_5_.refs_10_), channel_id=1, source_target_pairs={{0,1},{1,0},{2,3},{3,2},{4,5},{5,4},{6,7},{7,6},{8,9},{9,8},{10,11... | collective-permute-start | bytes 3538952 | tf_op jit(solution)/shard_map/ppermute | solution.py:672
  71.7 15.8 %collective-permute-start.26 = (bf16[80,768]{1,0:T(8,128)(2,1)S(1)}, bf16[80,768]{1,0:T(8,128)(2,1)S(1)}, u32[]{:S(2)}, u32[]{:S(2)}) collective-permute-start(bf16[80,768]{1,0:T(8,128)(2,1)S(1)} %get-tuple-element.171), channel_id=1, source_target_pairs={{0,8},{4,12},{8,0},{12,4},{16,24},{20,28},{24,16},{28,20},{1,9},{5... | collective-permute-start | bytes 368648 | tf_op jit(solution)/shard_map/ppermute | solution.py:672
  74.4 13.1 %collective-permute-start.27 = (bf16[80,768]{1,0:T(8,128)(2,1)S(1)}, bf16[80,768]{1,0:T(8,128)(2,1)S(1)}, u32[]{:S(2)}, u32[]{:S(2)}) collective-permute-start(bf16[80,768]{1,0:T(8,128)(2,1)S(1)} %get-tuple-element.172), channel_id=1, source_target_pairs={{0,16},{4,20},{8,24},{12,28},{16,0},{20,4},{24,8},{28,12},{1,17},{... | collective-permute-start | bytes 368648 | tf_op jit(solution)/shard_map/ppermute | solution.py:672
  75.4 12.1 %collective-permute-start.28 = (bf16[80,768]{1,0:T(8,128)(2,1)S(1)}, bf16[80,768]{1,0:T(8,128)(2,1)S(1)}, u32[]{:S(2)}, u32[]{:S(2)}) collective-permute-start(bf16[80,768]{1,0:T(8,128)(2,1)S(1)} %get-tuple-element.173), channel_id=1, source_target_pairs={{0,24},{4,28},{8,16},{12,20},{16,8},{20,12},{24,0},{28,4},{1,25},{... | collective-permute-start | bytes 368648 | tf_op jit(solution)/shard_map/ppermute | solution.py:672
  95.4 16.7 %collective-permute-start.36 = (bf16[4,384,768]{2,1,0:T(8,128)(2,1)S(1)}, bf16[4,384,768]{2,1,0:T(8,128)(2,1)S(1)}, u32[]{:S(2)}, u32[]{:S(2)}) collective-permute-start(bf16[4,384,768]{2,1,0:T(8,128)(2,1)S(1)} %outer_out_sent.1), channel_id=1, source_target_pairs={{0,1},{1,0},{2,3},{3,2},{4,5},{5,4},{6,7},{7,6},{8,9},{9,8},{10,11... | collective-permute-start | bytes 7077896 | tf_op jit(solution)/shard_map/ppermute | solution.py:672
  95.5 11.9 %collective-permute-start.37 = (bf16[80,768]{1,0:T(8,128)(2,1)S(1)}, bf16[80,768]{1,0:T(8,128)(2,1)S(1)}, u32[]{:S(2)}, u32[]{:S(2)}) collective-permute-start(bf16[80,768]{1,0:T(8,128)(2,1)S(1)} %get-tuple-element.193), channel_id=1, source_target_pairs={{0,8},{4,12},{8,0},{12,4},{16,24},{20,28},{24,16},{28,20},{1,9},{5... | collective-permute-start | bytes 368648 | tf_op jit(solution)/shard_map/ppermute | solution.py:672
  97.1 13.8 %collective-permute-start.38 = (bf16[80,768]{1,0:T(8,128)(2,1)S(1)}, bf16[80,768]{1,0:T(8,128)(2,1)S(1)}, u32[]{:S(2)}, u32[]{:S(2)}) collective-permute-start(bf16[80,768]{1,0:T(8,128)(2,1)S(1)} %get-tuple-element.194), channel_id=1, source_target_pairs={{0,16},{4,20},{8,24},{12,28},{16,0},{20,4},{24,8},{28,12},{1,17},{... | collective-permute-start | bytes 368648 | tf_op jit(solution)/shard_map/ppermute | solution.py:672
  99.7 12.3 %collective-permute-start.39 = (bf16[80,768]{1,0:T(8,128)(2,1)S(1)}, bf16[80,768]{1,0:T(8,128)(2,1)S(1)}, u32[]{:S(2)}, u32[]{:S(2)}) collective-permute-start(bf16[80,768]{1,0:T(8,128)(2,1)S(1)} %get-tuple-element.195), channel_id=1, source_target_pairs={{0,24},{4,28},{8,16},{12,20},{16,8},{20,12},{24,0},{28,4},{1,25},{... | collective-permute-start | bytes 368648 | tf_op jit(solution)/shard_map/ppermute | solution.py:672
  106.7 9.7 %collective-permute-start.33 = (bf16[80,768]{1,0:T(8,128)(2,1)S(1)}, bf16[80,768]{1,0:T(8,128)(2,1)S(1)}, u32[]{:S(2)}, u32[]{:S(2)}) collective-permute-start(bf16[80,768]{1,0:T(8,128)(2,1)S(1)} %get-tuple-element.188), channel_id=1, source_target_pairs={{0,8},{4,12},{8,0},{12,4},{16,24},{20,28},{24,16},{28,20},{1,9},{5... | collective-permute-start | bytes 368648 | tf_op jit(solution)/shard_map/ppermute | solution.py:672
  107.5 12.8 %collective-permute-start.34 = (bf16[80,768]{1,0:T(8,128)(2,1)S(1)}, bf16[80,768]{1,0:T(8,128)(2,1)S(1)}, u32[]{:S(2)}, u32[]{:S(2)}) collective-permute-start(bf16[80,768]{1,0:T(8,128)(2,1)S(1)} %get-tuple-element.189), channel_id=1, source_target_pairs={{0,16},{4,20},{8,24},{12,28},{16,0},{20,4},{24,8},{28,12},{1,17},{... | collective-permute-start | bytes 368648 | tf_op jit(solution)/shard_map/ppermute | solution.py:672
  110.9 9.4 %collective-permute-start.35 = (bf16[80,768]{1,0:T(8,128)(2,1)S(1)}, bf16[80,768]{1,0:T(8,128)(2,1)S(1)}, u32[]{:S(2)}, u32[]{:S(2)}) collective-permute-start(bf16[80,768]{1,0:T(8,128)(2,1)S(1)} %get-tuple-element.190), channel_id=1, source_target_pairs={{0,24},{4,28},{8,16},{12,20},{16,8},{20,12},{24,0},{28,4},{1,25},{... | collective-permute-start | bytes 368648 | tf_op jit(solution)/shard_map/ppermute | solution.py:672
  115.8 14.4 %collective-permute-start.41 = (bf16[384,768]{1,0:T(8,128)(2,1)S(1)}, bf16[384,768]{1,0:T(8,128)(2,1)S(1)}, u32[]{:S(2)}, u32[]{:S(2)}) collective-permute-start(bf16[384,768]{1,0:T(8,128)(2,1)S(1)} %get-tuple-element.206), channel_id=1, source_target_pairs={{0,4},{4,0},{8,12},{12,8},{16,20},{20,16},{24,28},{28,24},{1,5},{5... | collective-permute-start | bytes 1769480 | tf_op jit(solution)/shard_map/ppermute | solution.py:672
  116.4 8.0 %collective-permute-start.40 = (bf16[4,768,384]{2,1,0:T(8,128)(2,1)S(1)}, bf16[4,768,384]{2,1,0:T(8,128)(2,1)S(1)}, u32[]{:S(2)}, u32[]{:S(2)}) collective-permute-start(bf16[4,768,384]{2,1,0:T(8,128)(2,1)S(1)} %get-tuple-element.203), channel_id=1, source_target_pairs={{0,1},{1,0},{2,3},{3,2},{4,5},{5,4},{6,7},{7,6},{8,9},{9,8},{10,11... | collective-permute-start | bytes 7077896 | tf_op jit(solution)/shard_map/ppermute | solution.py:672
  122.8 8.4 %collective-permute-start.42 = (bf16[768,384]{1,0:T(8,128)(2,1)S(1)}, bf16[768,384]{1,0:T(8,128)(2,1)S(1)}, u32[]{:S(2)}, u32[]{:S(2)}) collective-permute-start(bf16[768,384]{1,0:T(8,128)(2,1)S(1)} %get-tuple-element.211), channel_id=1, source_target_pairs={{0,1},{1,0},{2,3},{3,2},{4,5},{5,4},{6,7},{7,6},{8,9},{9,8},{10,11... | collective-permute-start | bytes 1769480 | tf_op jit(solution)/shard_map/ppermute | solution.py:672
  127.2 32.2 %collective-permute-start.48 = (bf16[384,768]{1,0:T(8,128)(2,1)}, bf16[384,768]{1,0:T(8,128)(2,1)}, u32[]{:S(2)}, u32[]{:S(2)}) collective-permute-start(bf16[384,768]{1,0:T(8,128)(2,1)} %get-tuple-element.229), channel_id=1, source_target_pairs={{0,4},{4,0},{8,12},{12,8},{16,20},{20,16},{24,28},{28,24},{1,5},{5... | collective-permute-start | bytes 1769480 | tf_op jit(solution)/shard_map/ppermute | solution.py:672
  132.2 32.3 %all-to-all-start = ((bf16[8,96,384]{2,1,0:T(8,128)(2,1)}), bf16[8,96,384]{2,1,0:T(8,128)(2,1)}, u32[]{:S(2)}, u32[]{:S(2)}) async-start(bf16[8,96,384]{2,1,0:T(8,128)(2,1)} %bitcast.32), calls=%async_computation | async-start | bytes 1179648 | tf_op jit(solution)/shard_map/all_to_all | solution.py:1034
  137.1 22.3 %collective-permute-start.49 = (bf16[320,768]{1,0:T(8,128)(2,1)S(1)}, bf16[320,768]{1,0:T(8,128)(2,1)S(1)}, u32[]{:S(2)}, u32[]{:S(2)}) collective-permute-start(bf16[320,768]{1,0:T(8,128)(2,1)S(1)} %copy-done.7), channel_id=1, source_target_pairs={{0,2},{1,3},{2,0},{3,1},{4,6},{5,7},{6,4},{7,5},{8,10},{9,11},{10,... | collective-permute-start | bytes 1474568 | tf_op jit(solution)/shard_map/ppermute | solution.py:672
  138.4 25.2 %collective-permute-start.47 = (bf16[384,768]{1,0:T(8,128)(2,1)}, bf16[384,768]{1,0:T(8,128)(2,1)S(1)}, u32[]{:S(2)}, u32[]{:S(2)}) collective-permute-start(bf16[384,768]{1,0:T(8,128)(2,1)} %add_convert_fusion.4), channel_id=1, source_target_pairs={{0,2},{1,3},{2,0},{3,1},{4,6},{5,7},{6,4},{7,5},{8,10},{9,11},{10,... | collective-permute-start | bytes 1769480 | tf_op jit(solution)/shard_map/ppermute | solution.py:672
  139.1 25.3 %collective-permute-start.46 = (bf16[768,384]{1,0:T(8,128)(2,1)}, bf16[768,384]{1,0:T(8,128)(2,1)}, u32[]{:S(2)}, u32[]{:S(2)}) collective-permute-start(bf16[768,384]{1,0:T(8,128)(2,1)} %copy-done.12), channel_id=1, source_target_pairs={{0,4},{4,0},{8,12},{12,8},{16,20},{20,16},{24,28},{28,24},{1,5},{5... | collective-permute-start | bytes 1769480 | tf_op jit(solution)/shard_map/ppermute | solution.py:672
  164.5 14.4 %collective-permute-start.54 = (bf16[4,96,640]{2,1,0:T(8,128)(2,1)}, bf16[4,96,640]{2,1,0:T(8,128)(2,1)S(1)}, u32[]{:S(2)}, u32[]{:S(2)}) collective-permute-start(bf16[4,96,640]{2,1,0:T(8,128)(2,1)} %get-tuple-element.246), channel_id=1, source_target_pairs={{0,4},{4,0},{8,12},{12,8},{16,20},{20,16},{24,28},{28,24},{1,5},{5... | collective-permute-start | bytes 1474568 | tf_op jit(solution)/shard_map/ppermute | solution.py:672
  168.3 6.4 %collective-permute-start.51 = (bf16[320,768]{1,0:T(8,128)(2,1)S(1)}, bf16[320,768]{1,0:T(8,128)(2,1)S(1)}, u32[]{:S(2)}, u32[]{:S(2)}) collective-permute-start(bf16[320,768]{1,0:T(8,128)(2,1)S(1)} %copy-done.7), channel_id=1, source_target_pairs={{0,1},{1,0},{2,3},{3,2},{4,5},{5,4},{6,7},{7,6},{8,9},{9,8},{10,11... | collective-permute-start | bytes 1474568 | tf_op jit(solution)/shard_map/ppermute | solution.py:672
  171.2 22.1 %collective-permute-start.53 = (bf16[2,256,768]{2,1,0:T(8,128)(2,1)S(1)}, bf16[2,256,768]{2,1,0:T(8,128)(2,1)S(1)}, u32[]{:S(2)}, u32[]{:S(2)}) collective-permute-start(bf16[2,256,768]{2,1,0:T(8,128)(2,1)S(1)} %add_convert_fusion.1), channel_id=1, source_target_pairs={{0,2},{1,3},{2,0},{3,1},{4,6},{5,7},{6,4},{7,5},{8,10},{9,11},{10,... | collective-permute-start | bytes 2359304 | tf_op jit(solution)/shard_map/ppermute | solution.py:672
  179.1 8.1 %collective-permute-start.57 = (bf16[96,640]{1,0:T(8,128)(2,1)S(1)}, bf16[96,640]{1,0:T(8,128)(2,1)S(1)}, u32[]{:S(2)}, u32[]{:S(2)}) collective-permute-start(bf16[96,640]{1,0:T(8,128)(2,1)S(1)} %get-tuple-element.268), channel_id=1, source_target_pairs={{0,24},{4,28},{8,16},{12,20},{16,8},{20,12},{24,0},{28,4},{1,25},{... | collective-permute-start | bytes 368648 | tf_op jit(solution)/shard_map/ppermute | solution.py:672
  182.7 10.6 %collective-permute-start.56 = (bf16[96,640]{1,0:T(8,128)(2,1)S(1)}, bf16[96,640]{1,0:T(8,128)(2,1)S(1)}, u32[]{:S(2)}, u32[]{:S(2)}) collective-permute-start(bf16[96,640]{1,0:T(8,128)(2,1)S(1)} %get-tuple-element.269), channel_id=1, source_target_pairs={{0,16},{4,20},{8,24},{12,28},{16,0},{20,4},{24,8},{28,12},{1,17},{... | collective-permute-start | bytes 368648 | tf_op jit(solution)/shard_map/ppermute | solution.py:672
  182.7 10.6 %collective-permute-start.55 = (bf16[96,640]{1,0:T(8,128)(2,1)S(1)}, bf16[96,640]{1,0:T(8,128)(2,1)S(1)}, u32[]{:S(2)}, u32[]{:S(2)}) collective-permute-start(bf16[96,640]{1,0:T(8,128)(2,1)S(1)} %get-tuple-element.270), channel_id=1, source_target_pairs={{0,8},{4,12},{8,0},{12,4},{16,24},{20,28},{24,16},{28,20},{1,9},{5... | collective-permute-start | bytes 368648 | tf_op jit(solution)/shard_map/ppermute | solution.py:672
  185.5 18.9 %collective-permute-start.61 = (bf16[768,384]{1,0:T(8,128)(2,1)}, bf16[768,384]{1,0:T(8,128)(2,1)}, u32[]{:S(2)}, u32[]{:S(2)}) collective-permute-start(bf16[768,384]{1,0:T(8,128)(2,1)} %add_convert_fusion.2), channel_id=1, source_target_pairs={{0,2},{1,3},{2,0},{3,1},{4,6},{5,7},{6,4},{7,5},{8,10},{9,11},{10,... | collective-permute-start | bytes 1769480 | tf_op jit(solution)/shard_map/ppermute | solution.py:672
  187.2 17.1 %collective-permute-start.62 = (bf16[768,384]{1,0:T(8,128)(2,1)}, bf16[768,384]{1,0:T(8,128)(2,1)}, u32[]{:S(2)}, u32[]{:S(2)}) collective-permute-start(bf16[768,384]{1,0:T(8,128)(2,1)} %get-tuple-element.260), channel_id=1, source_target_pairs={{0,4},{4,0},{8,12},{12,8},{16,20},{20,16},{24,28},{28,24},{1,5},{5... | collective-permute-start | bytes 1769480 | tf_op jit(solution)/shard_map/ppermute | solution.py:672
  193.5 6.2 %collective-permute-start.58 = (bf16[2,256,768]{2,1,0:T(8,128)(2,1)S(1)}, bf16[2,256,768]{2,1,0:T(8,128)(2,1)}, u32[]{:S(2)}, u32[]{:S(2)}) collective-permute-start(bf16[2,256,768]{2,1,0:T(8,128)(2,1)S(1)} %add_convert_fusion.own_ref), channel_id=1, source_target_pairs={{0,1},{1,0},{2,3},{3,2},{4,5},{5,4},{6,7},{7,6},{8,9},{9,8},{10,11... | collective-permute-start | bytes 2359304 | tf_op jit(solution)/shard_map/ppermute | solution.py:672
  198.8 6.8 %collective-permute-start.60 = (f32[96,256]{1,0:T(8,128)S(1)}, f32[96,256]{1,0:T(8,128)S(1)}, u32[]{:S(2)}, u32[]{:S(2)}) collective-permute-start(f32[96,256]{1,0:T(8,128)S(1)} %pad_maximum_fusion.1), channel_id=1, source_target_pairs={{0,2},{1,3},{2,0},{3,1},{4,6},{5,7},{6,4},{7,5},{8,10},{9,11},{10,... | collective-permute-start | bytes 294920 | tf_op jit(solution)/shard_map/ppermute | solution.py:672
  (67 other events, 385.9 us)
